TPU v7x, 32 devices: a whole 2x2x4 slice. The times are simulated.
32 devices in a mesh: blk: 16 (over z, y, core), fsdp: 2 (over x).
Axes of the slice: x: 2, y: 2, z: 4, core: 2. Of those that a mesh axis runs over, the one named last changes fastest.
Arguments:
- tokens: bfloat16 [2, 4096, 512], P('fsdp', 'blk'), may hold values from -6 to 6
- ln1_gain: bfloat16 [512], P(('blk', 'fsdp')), may hold values from 0.25 to 1.75
- ln1_bias: bfloat16 [512], P(('blk', 'fsdp')), may hold values from -3 to 3
- qkv_weight: bfloat16 [512, 1536], P(('blk', 'fsdp')), may hold values from -0.25 to 0.25
- query_bias: bfloat16 [512], P(('blk', 'fsdp')), may hold values from -3 to 3
- value_bias: bfloat16 [512], P(('blk', 'fsdp')), may hold values from -0.29882812 to 0.29882812
- out_weight: bfloat16 [512, 512], P(('blk', 'fsdp')), may hold values from -6 to 6
- out_bias: bfloat16 [512], P(('blk', 'fsdp')), may hold values from -3 to 3
- ln2_gain: bfloat16 [512], P(('blk', 'fsdp')), may hold values from 0.25 to 1.75
- ln2_bias: bfloat16 [512], P(('blk', 'fsdp')), may hold values from -3 to 3
- up_weight: bfloat16 [512, 2048], P(('blk', 'fsdp')), may hold values from -0.25 to 0.25
- up_bias: bfloat16 [2048], P(('blk', 'fsdp')), may hold values from -3 to 3
- down_weight: bfloat16 [2048, 512], P(('blk', 'fsdp')), may hold values from -0.125 to 0.125
- down_bias: bfloat16 [512], P(('blk', 'fsdp')), may hold values from -3 to 3
- table_lengths: int32 [2, 8], P('fsdp'), may hold values from 1 to 3879, as said below
- support_lengths: int32 [2, 8], P('fsdp'), may hold values from 1 to 2910, as said below
- cotangent: bfloat16 [2, 4096, 512], P('fsdp', 'blk'), may hold values from -6 to 6
Outputs:
- block_out: bfloat16 [2, 4096, 512], P('fsdp', 'blk')
- grad_tokens: bfloat16 [2, 4096, 512], P('fsdp', 'blk')
- grad_ln1_gain: float32 [512], P(('blk', 'fsdp'))
- grad_ln1_bias: float32 [512], P(('blk', 'fsdp'))
- grad_qkv_weight: float32 [512, 1536], P(('blk', 'fsdp'))
- grad_query_bias: float32 [512], P(('blk', 'fsdp'))
- grad_value_bias: float32 [512], P(('blk', 'fsdp'))
- grad_out_weight: float32 [512, 512], P(('blk', 'fsdp'))
- grad_out_bias: float32 [512], P(('blk', 'fsdp'))
- grad_ln2_gain: float32 [512], P(('blk', 'fsdp'))
- grad_ln2_bias: float32 [512], P(('blk', 'fsdp'))
- grad_up_weight: float32 [512, 2048], P(('blk', 'fsdp'))
- grad_up_bias: float32 [2048], P(('blk', 'fsdp'))
- grad_down_weight: float32 [2048, 512], P(('blk', 'fsdp'))
- grad_down_bias: float32 [512], P(('blk', 'fsdp'))
Inputs may be any that keep to these rules, and one draw needn't show every extreme that they name: `table_lengths`: in each bucket the 8 lengths sum to 4096; one table of each bucket has exactly the largest length. Entry by entry, support_lengths is at most table_lengths; the longest table of each bucket has the largest support.
All inputs are finite; a program needn't handle non-finite values.
Results may differ from a plain program's by a relative error of at most 0.012.
Values may be sent and summed in bfloat16 or wider, within the bound.
A program may use at most 128 MiB of HBM per device.

v0:
```python
import jax
import jax.numpy as jnp
from jax import lax
from jax.sharding import PartitionSpec as P

H = 4


EPSILON = 1e-05
MASKED = -1e30


def normalize(values, norm_gain, norm_bias):
    row_mean = jnp.mean(values, axis=-1, keepdims=True)
    centered = values - row_mean
    variance = jnp.mean(centered * centered, axis=-1, keepdims=True)
    return centered * lax.rsqrt(variance + EPSILON) * norm_gain + norm_bias


def gelu_exact(values):
    return jax.nn.gelu(values, approximate=False)


def row_codes(lengths, support, positions):
    table_ends = jnp.cumsum(lengths)
    table_ids = jnp.sum((positions[:, None] >= table_ends[None, :]).astype(jnp.int32), axis=1)
    starts = table_ends - lengths
    chosen = (table_ids[:, None] == jnp.arange(lengths.shape[0], dtype=jnp.int32)[None, :]).astype(
        jnp.int32
    )
    support_end = jnp.sum(chosen * (starts + support)[None, :], axis=1)
    key_codes = jnp.where(positions < support_end, table_ids, -1)
    return (table_ids, key_codes)


def inner_rows(left, right):
    return lax.dot_general(
        left, right, (((0,), (0,)), ((), ())), preferred_element_type=jnp.float32
    )


def times_transposed(left, right):
    return lax.dot_general(
        left, right, (((1,), (1,)), ((), ())), preferred_element_type=jnp.float32
    )


def blockwise(step_fn, running, portions):
    total_rows = portions[0].shape[0]
    block_size = total_rows
    while block_size > 1536 and block_size % 2 == 0:
        block_size = block_size // 2
    block_count = total_rows // block_size
    shaped = tuple(
        (member.reshape((block_count, block_size) + member.shape[1:]) for member in portions)
    )

    def scan_turn(inner_state, scan_item):
        block_index, members = scan_item
        return (step_fn(inner_state, members, block_index * block_size), None)

    running, _ = lax.scan(scan_turn, running, (jnp.arange(block_count, dtype=jnp.int32), shaped))
    return running


def guarded(compute_block, running):
    result = compute_block(running)
    return result


def shards(
    tokens,
    ln1_gain,
    ln1_bias,
    qkv_weight,
    query_bias,
    value_bias,
    out_weight,
    out_bias,
    ln2_gain,
    ln2_bias,
    up_weight,
    up_bias,
    down_weight,
    down_bias,
    table_lengths,
    support_lengths,
    cotangent,
):
    row_count = tokens.shape[1]
    model_width = tokens.shape[2]
    head_size = model_width // H
    score_scale = head_size ** (-0.5)
    lengths = table_lengths[0]
    support = support_lengths[0]
    my_rows = lax.axis_index("blk") * row_count + jnp.arange(row_count, dtype=jnp.int32)
    my_tables, my_codes = row_codes(lengths, support, my_rows)

    def block_info(first_row, block_rows):
        return row_codes(lengths, support, first_row + jnp.arange(block_rows, dtype=jnp.int32))

    def heads_of(values):
        return values.reshape(values.shape[0], H, head_size)

    def head_scores(left_heads, right_heads):
        return (
            jnp.einsum("qhd,khd->hqk", left_heads, right_heads, preferred_element_type=jnp.float32)
            * score_scale
        )

    attn_full = (
        lax.all_gather(ln1_gain, ("blk", "fsdp"), axis=0, tiled=True),
        lax.all_gather(ln1_bias, ("blk", "fsdp"), axis=0, tiled=True),
        lax.all_gather(qkv_weight, ("blk", "fsdp"), axis=0, tiled=True),
        lax.all_gather(query_bias, ("blk", "fsdp"), axis=0, tiled=True),
        lax.all_gather(value_bias, ("blk", "fsdp"), axis=0, tiled=True),
        lax.all_gather(out_weight, ("blk", "fsdp"), axis=0, tiled=True),
        lax.all_gather(out_bias, ("blk", "fsdp"), axis=0, tiled=True),
    )
    mlp_full = (
        lax.all_gather(ln2_gain, ("blk", "fsdp"), axis=0, tiled=True),
        lax.all_gather(ln2_bias, ("blk", "fsdp"), axis=0, tiled=True),
        lax.all_gather(up_weight, ("blk", "fsdp"), axis=0, tiled=True),
        lax.all_gather(up_bias, ("blk", "fsdp"), axis=0, tiled=True),
        lax.all_gather(down_weight, ("blk", "fsdp"), axis=0, tiled=True),
        lax.all_gather(down_bias, ("blk", "fsdp"), axis=0, tiled=True),
    )
    gain_first, bias_first, w_qkv, q_shift, v_shift, w_out, b_out = attn_full
    gain_second, bias_second, w_up, b_up, w_down, b_down = mlp_full
    inputs = tokens[0].astype(jnp.float32)
    gain_first_f = gain_first.astype(jnp.float32)
    bias_first_f = bias_first.astype(jnp.float32)
    normed_first = normalize(inputs, gain_first_f, bias_first_f).astype(jnp.bfloat16)
    projected = jnp.dot(normed_first, w_qkv, preferred_element_type=jnp.float32)
    queries = (projected[:, :model_width] + q_shift.astype(jnp.float32)).astype(jnp.bfloat16)
    key_rows = projected[:, model_width : 2 * model_width].astype(jnp.bfloat16)
    value_rows = (projected[:, 2 * model_width :] + v_shift.astype(jnp.float32)).astype(
        jnp.bfloat16
    )
    query_heads = heads_of(queries)
    key_heads = heads_of(key_rows)
    value_heads = heads_of(value_rows)

    def stats_step(running, members, first_row):
        block_keys = members[0]
        allowed = my_tables[:, None] == block_info(first_row, block_keys.shape[0])[1][None, :]

        def compute_block(running_pair):
            highest, summed = running_pair
            scores = jnp.where(
                allowed[None], head_scores(query_heads, heads_of(block_keys)), MASKED
            )
            new_high = jnp.maximum(highest, jnp.max(scores, axis=-1))
            grown = jnp.sum(
                jnp.where(allowed[None], jnp.exp(scores - new_high[:, :, None]), 0.0), axis=-1
            )
            return (new_high, summed * jnp.exp(highest - new_high) + grown)

        return guarded(compute_block, running)

    start_high = jnp.full((H, row_count), MASKED, jnp.float32)
    start_sum = jnp.zeros((H, row_count), jnp.float32)
    highest, summed = blockwise(
        stats_step, (start_high, start_sum), (lax.all_gather(key_rows, "blk", axis=0, tiled=True),)
    )
    log_total = highest + jnp.log(summed)

    def values_step(running, members, first_row):
        block_keys, block_values = members
        allowed = my_tables[:, None] == block_info(first_row, block_keys.shape[0])[1][None, :]

        def compute_block(accum_pair):
            accum, leftover_sum = accum_pair
            scores = head_scores(query_heads, heads_of(block_keys))
            exact = jnp.where(allowed[None], jnp.exp(scores - log_total[:, :, None]), 0.0)
            probs = exact.astype(jnp.bfloat16)
            leftover = (exact - probs.astype(jnp.float32)).astype(jnp.bfloat16)
            value_part = heads_of(block_values)
            accum = accum + jnp.einsum(
                "hqk,khd->qhd", probs, value_part, preferred_element_type=jnp.float32
            )
            leftover_sum = leftover_sum + jnp.einsum(
                "hqk,khd->qhd", leftover, value_part, preferred_element_type=jnp.float32
            )
            return (accum, leftover_sum)

        return guarded(compute_block, running)

    head_zeros = jnp.zeros((row_count, H, head_size), jnp.float32)
    attended, leftover_sum = blockwise(
        values_step,
        (head_zeros, head_zeros),
        (
            lax.all_gather(key_rows, "blk", axis=0, tiled=True),
            lax.all_gather(value_rows, "blk", axis=0, tiled=True),
        ),
    )
    attended_exact = attended + leftover_sum
    attn_float = attended.reshape(row_count, model_width)
    attn_low = attn_float.astype(jnp.bfloat16)
    branch = jnp.dot(attn_low, w_out, preferred_element_type=jnp.float32) + b_out.astype(
        jnp.float32
    )
    hidden_res = inputs + branch
    gain_second_f = gain_second.astype(jnp.float32)
    bias_second_f = bias_second.astype(jnp.float32)
    normed_second = normalize(hidden_res, gain_second_f, bias_second_f).astype(jnp.bfloat16)
    pre_act = jnp.dot(normed_second, w_up, preferred_element_type=jnp.float32) + b_up.astype(
        jnp.float32
    )
    activated, gelu_back = jax.vjp(gelu_exact, pre_act)
    act_low = activated.astype(jnp.bfloat16)
    output = (
        hidden_res
        + jnp.dot(act_low, w_down, preferred_element_type=jnp.float32)
        + b_down.astype(jnp.float32)
    )
    block_out = output.astype(jnp.bfloat16)[None]
    w_up_back = mlp_full[2]
    w_down_back = mlp_full[4]
    grad_out = cotangent[0]
    grad_down_w = inner_rows(act_low, grad_out)
    grad_down_b = jnp.sum(grad_out.astype(jnp.float32), axis=0)
    grad_act = times_transposed(grad_out, w_down_back)
    grad_pre = gelu_back(grad_act)[0].astype(jnp.bfloat16)
    grad_up_w = inner_rows(normed_second, grad_pre)
    grad_up_b = jnp.sum(grad_pre.astype(jnp.float32), axis=0)
    grad_second = times_transposed(grad_pre, w_up_back)
    _, second_back = jax.vjp(normalize, hidden_res, gain_second_f, bias_second_f)
    grad_hidden_part, grad_gain_second, grad_bias_second = second_back(grad_second)
    grad_hidden = grad_out.astype(jnp.float32) + grad_hidden_part
    mlp_grads = (
        lax.psum_scatter(grad_gain_second, ("blk", "fsdp"), scatter_dimension=0, tiled=True),
        lax.psum_scatter(grad_bias_second, ("blk", "fsdp"), scatter_dimension=0, tiled=True),
        lax.psum_scatter(grad_up_w, ("blk", "fsdp"), scatter_dimension=0, tiled=True),
        lax.psum_scatter(grad_up_b, ("blk", "fsdp"), scatter_dimension=0, tiled=True),
        lax.psum_scatter(grad_down_w, ("blk", "fsdp"), scatter_dimension=0, tiled=True),
        lax.psum_scatter(grad_down_b, ("blk", "fsdp"), scatter_dimension=0, tiled=True),
    )
    w_qkv_back = attn_full[2]
    w_out_back = attn_full[5]
    grad_branch = grad_hidden.astype(jnp.bfloat16)
    grad_out_w = inner_rows(attn_low, grad_branch)
    grad_out_b = jnp.sum(grad_branch.astype(jnp.float32), axis=0)
    grad_attended = times_transposed(grad_branch, w_out_back).astype(jnp.bfloat16)
    grad_heads = heads_of(grad_attended)
    row_delta = jnp.einsum("qhd,qhd->hq", grad_heads.astype(jnp.float32), attended_exact)
    all_log, all_delta = (
        lax.all_gather(log_total, "blk", axis=1, tiled=True),
        lax.all_gather(row_delta, "blk", axis=1, tiled=True),
    )

    def key_grad_step(running, members, first_row):
        block_queries, block_grads = members
        query_count = block_queries.shape[0]
        allowed = block_info(first_row, query_count)[0][:, None] == my_codes[None, :]

        def compute_block(grad_pair):
            grad_k, grad_v = grad_pair
            query_part = heads_of(block_queries)
            grad_part = heads_of(block_grads)
            block_log = lax.dynamic_slice_in_dim(all_log, first_row, query_count, 1)
            block_delta = lax.dynamic_slice_in_dim(all_delta, first_row, query_count, 1)
            scores = head_scores(query_part, key_heads)
            weights = jnp.where(allowed[None], jnp.exp(scores - block_log[:, :, None]), 0.0)
            grad_v = grad_v + jnp.einsum(
                "hqk,qhd->khd",
                weights.astype(jnp.bfloat16),
                grad_part,
                preferred_element_type=jnp.float32,
            )
            grad_probs = jnp.einsum(
                "qhd,khd->hqk", grad_part, value_heads, preferred_element_type=jnp.float32
            )
            grad_scores = (weights * (grad_probs - block_delta[:, :, None])).astype(jnp.bfloat16)
            grad_k = (
                grad_k
                + jnp.einsum(
                    "hqk,qhd->khd", grad_scores, query_part, preferred_element_type=jnp.float32
                )
                * score_scale
            )
            return (grad_k, grad_v)

        return guarded(compute_block, running)

    grad_keys, grad_values = blockwise(
        key_grad_step,
        (head_zeros, head_zeros),
        (
            lax.all_gather(queries, "blk", axis=0, tiled=True),
            lax.all_gather(grad_attended, "blk", axis=0, tiled=True),
        ),
    )

    def query_grad_step(running, members, first_row):
        block_keys, block_values = members
        allowed = my_tables[:, None] == block_info(first_row, block_keys.shape[0])[1][None, :]

        def compute_block(grad_q):
            key_part = heads_of(block_keys)
            scores = head_scores(query_heads, key_part)
            weights = jnp.where(allowed[None], jnp.exp(scores - log_total[:, :, None]), 0.0)
            grad_probs = jnp.einsum(
                "qhd,khd->hqk",
                grad_heads,
                heads_of(block_values),
                preferred_element_type=jnp.float32,
            )
            grad_scores = (weights * (grad_probs - row_delta[:, :, None])).astype(jnp.bfloat16)
            return (
                grad_q
                + jnp.einsum(
                    "hqk,khd->qhd", grad_scores, key_part, preferred_element_type=jnp.float32
                )
                * score_scale
            )

        return guarded(compute_block, running)

    grad_queries = blockwise(
        query_grad_step,
        head_zeros,
        (
            lax.all_gather(key_rows, "blk", axis=0, tiled=True),
            lax.all_gather(value_rows, "blk", axis=0, tiled=True),
        ),
    )
    grad_q_low = grad_queries.reshape(row_count, model_width).astype(jnp.bfloat16)
    grad_k_low = grad_keys.reshape(row_count, model_width).astype(jnp.bfloat16)
    grad_v_low = grad_values.reshape(row_count, model_width).astype(jnp.bfloat16)
    grad_projected = jnp.concatenate([grad_q_low, grad_k_low, grad_v_low], axis=1)
    grad_qkv_w = inner_rows(normed_first, grad_projected)
    grad_q_b = jnp.sum(grad_q_low.astype(jnp.float32), axis=0)
    grad_v_b = jnp.sum(grad_v_low.astype(jnp.float32), axis=0)
    grad_first = times_transposed(grad_projected, w_qkv_back)
    _, first_back = jax.vjp(normalize, inputs, gain_first_f, bias_first_f)
    grad_input_part, grad_gain_first, grad_bias_first = first_back(grad_first)
    grad_input = (grad_hidden + grad_input_part).astype(jnp.bfloat16)[None]
    attn_grads = (
        lax.psum_scatter(grad_gain_first, ("blk", "fsdp"), scatter_dimension=0, tiled=True),
        lax.psum_scatter(grad_bias_first, ("blk", "fsdp"), scatter_dimension=0, tiled=True),
        lax.psum_scatter(grad_qkv_w, ("blk", "fsdp"), scatter_dimension=0, tiled=True),
        lax.psum_scatter(grad_q_b, ("blk", "fsdp"), scatter_dimension=0, tiled=True),
        lax.psum_scatter(grad_v_b, ("blk", "fsdp"), scatter_dimension=0, tiled=True),
        lax.psum_scatter(grad_out_w, ("blk", "fsdp"), scatter_dimension=0, tiled=True),
        lax.psum_scatter(grad_out_b, ("blk", "fsdp"), scatter_dimension=0, tiled=True),
    )
    return (
        block_out,
        grad_input,
        attn_grads[0],
        attn_grads[1],
        attn_grads[2],
        attn_grads[3],
        attn_grads[4],
        attn_grads[5],
        attn_grads[6],
        mlp_grads[0],
        mlp_grads[1],
        mlp_grads[2],
        mlp_grads[3],
        mlp_grads[4],
        mlp_grads[5],
    )


def solution(mesh):
    return jax.shard_map(
        shards,
        mesh=mesh,
        in_specs=(
            P("fsdp", "blk", None),
            P(("blk", "fsdp")),
            P(("blk", "fsdp")),
            P(("blk", "fsdp"), None),
            P(("blk", "fsdp")),
            P(("blk", "fsdp")),
            P(("blk", "fsdp"), None),
            P(("blk", "fsdp")),
            P(("blk", "fsdp")),
            P(("blk", "fsdp")),
            P(("blk", "fsdp"), None),
            P(("blk", "fsdp")),
            P(("blk", "fsdp"), None),
            P(("blk", "fsdp")),
            P("fsdp", None),
            P("fsdp", None),
            P("fsdp", "blk", None),
        ),
        out_specs=(
            P("fsdp", "blk", None),
            P("fsdp", "blk", None),
            P(("blk", "fsdp")),
            P(("blk", "fsdp")),
            P(("blk", "fsdp"), None),
            P(("blk", "fsdp")),
            P(("blk", "fsdp")),
            P(("blk", "fsdp"), None),
            P(("blk", "fsdp")),
            P(("blk", "fsdp")),
            P(("blk", "fsdp")),
            P(("blk", "fsdp"), None),
            P(("blk", "fsdp")),
            P(("blk", "fsdp"), None),
            P(("blk", "fsdp")),
        ),
        check_vma=False,
    )
```

profile of v0, /device:TPU:0, one launch (start us, length us, event | category | flops | bytes accessed | tf_op | source)
XLA Modules:
  0.0 926.7 jit_solution(1057519487957317292)
XLA Ops:
  15.6 42.3 %all-reduce.19 = (bf16[512]{0:T(512)(128)(2,1)S(1)}, bf16[512]{0:T(512)(128)(2,1)S(1)}, bf16[512]{0:T(512)(128)(2,1)S(1)}, bf16[512]{0:T(512)(128)(2,1)S(1)}, bf...) all-reduce(bf16[512]{0:T(512)(128)(2,1)S(1)} %dynamic-update-slice., ...), channel_id=1, replica_groups=mesh['blk'=16,'fsdp'=2] {'blk','fsdp'}, use_global_device_ids=true, to_apply=%add.1 | all-reduce | flops 6144 | bytes 24576
  60.8 8.0 all-gather.8.cloned.1.call-done
  74.2 76.5 %all_gather.67 = bf16[512,512]{1,0:T(8,128)(2,1)} all-gather(bf16[16,512]{1,0:T(8,128)(2,1)S(1)} %copy-done.36), channel_id=1, replica_groups=mesh['blk'=16,'fsdp'=2] {'blk','fsdp'}, dimensions={0}, use_global_device_ids=true | all-gather | bytes 540672 | tf_op jit(solution)/shard_map/all_gather | solution.py:117
  151.0 6.3 copy.107
  157.4 36.6 %while.58 = (s32[]{:T(128)}, f32[4,256]{1,0:T(4,128)S(1)}, f32[4,256]{1,0:T(4,128)S(1)}, s32[256]{0:T(256)S(1)}, s32[4]{0:T(128)S(1)}, /*index=5*/s32[8,1]{0,1:T...) while((s32[]{:T(128)}, f32[4,256]{1,0:T(4,128)S(1)}, ...), condition=%wide.region_9.10_spmd.clone, body=%wide.region_4.9_spmd.clone.sunk | while | flops 277142528 | bytes 12674276 | solution.py:62
  194.1 6.3 copy.106
  200.4 53.1 %while.59 = (s32[]{:T(128)}, f32[256,4,128]{0,2,1:T(8,128)}, f32[256,4,128]{0,2,1:T(8,128)}, bf16[4,1024,512]{1,2,0:T(8,128)(2,1)}, s32[256]{0:T(256)S(1)}, /*in...) while((s32[]{:T(128)}, f32[256,4,128]{0,2,1:T(8,128)}, ...), condition=%wide.region_13.14_spmd.clone, body=%wide.region_10.13_spmd.clone.sunk | while | flops 817678336 | bytes 39892236 | solution.py:62
  218.9 4.6 fusion.180
  232.5 4.6 fusion.180
  246.0 4.6 fusion.180
  256.4 8.4 multiply_convert_fusion.1
  264.8 26.5 %all-gather.16.cloned.1.call-done = bf16[2048,512]{1,0:T(8,128)(2,1)} async-done(((bf16[64,512]{1,0:T(8,128)(2,1)}), bf16[2048,512]{1,0:T(8,128)(2,1)}) %all-gather.16.cloned.1.call-update) | async-done | bytes 2097168 | tf_op jit(solution)/shard_map/all_gather | solution.py:125
  304.9 20.5 %all_gather.76 = f32[4,4096]{1,0:T(4,128)S(1)} all-gather(f32[4,256]{1,0:T(4,128)S(1)} %get-tuple-element.1558), channel_id=1, replica_groups=mesh['blk'=16,'fsdp'=2] {'blk'}, dimensions={1}, use_global_device_ids=true | all-gather | bytes 69632 | tf_op jit(solution)/shard_map/all_gather | solution.py:249
  326.7 19.2 %all_gather.78 = f32[4,4096]{1,0:T(4,128)} all-gather(f32[4,256]{1,0:T(4,128)S(1)} %multiply_reduce_fusion), channel_id=1, replica_groups=mesh['blk'=16,'fsdp'=2] {'blk'}, dimensions={1}, use_global_device_ids=true | all-gather | bytes 69632 | tf_op jit(solution)/shard_map/all_gather | solution.py:250
  349.6 44.2 %while.60 = (s32[]{:T(128)}, f32[256,4,128]{0,2,1:T(8,128)}, bf16[4,1024,512]{1,2,0:T(8,128)(2,1)}, s32[256]{0:T(256)S(1)}, s32[4]{0:T(128)S(1)}, /*index=5*/s32...) while((s32[]{:T(128)}, f32[256,4,128]{0,2,1:T(8,128)}, ...), condition=%wide.region_21.22_spmd.clone, body=%wide.region_18.21_spmd.clone.sunk | while | flops 812304384 | bytes 18920728 | solution.py:62
  355.8 4.8 fusion.187
  366.7 4.9 fusion.187
  377.8 5.0 fusion.187
  388.9 4.9 fusion.187
  400.1 77.4 %while.61 = (s32[]{:T(128)}, f32[256,4,128]{0,2,1:T(8,128)}, f32[256,4,128]{0,2,1:T(8,128)}, bf16[4,1024,512]{2,1,0:T(8,128)(2,1)}, s32[4]{0:T(128)}, /*index=5*...) while((s32[]{:T(128)}, f32[256,4,128]{0,2,1:T(8,128)}, ...), condition=%wide.region_26.27_spmd.clone, body=%wide.region_24.26_spmd.clone.sunk | while | flops 1085169664 | bytes 34997620 | solution.py:62
  490.8 37.4 %all-reduce.18 = (f32[512]{0:T(512)S(1)}, f32[512]{0:T(512)S(1)}, f32[512]{0:T(512)S(1)}, f32[512]{0:T(512)S(1)}, f32[512]{0:T(512)S(1)}, /*index=5*/f32[512]{0:...) all-reduce(f32[512]{0:T(512)S(1)} %get-tuple-element.908, ...), channel_id=2, replica_groups=mesh['blk'=16,'fsdp'=2] {'blk','fsdp'}, use_global_device_ids=true, to_apply=%region_30.31.clone | all-reduce | flops 6144 | bytes 49152
  533.4 139.7 %reduce-scatter.9.cloned.1.call-done = f32[16,2048]{1,0:T(8,128)} async-done(((f32[512,2048]{1,0:T(8,128)}), f32[16,2048]{1,0:T(8,128)}) %reduce-scatter.9.cloned.1.call-update) | async-done | bytes 131088 | tf_op jit(solution)/shard_map/reduce_scatter | solution.py:235
  673.1 141.9 %reduce-scatter.11.cloned.1.call-done = f32[64,512]{1,0:T(8,128)} async-done(((f32[2048,512]{1,0:T(8,128)}), f32[64,512]{1,0:T(8,128)}) %reduce-scatter.11.cloned.1.call-update) | async-done | bytes 131088 | tf_op jit(solution)/shard_map/reduce_scatter | solution.py:237
  815.0 105.2 %reduce-scatter.5.cloned.1.call-done = f32[16,1536]{1,0:T(8,128)} async-done(((f32[512,1536]{1,0:T(8,128)}), f32[16,1536]{1,0:T(8,128)}) %reduce-scatter.5.cloned.1.call-update) | async-done | bytes 98320 | tf_op jit(solution)/shard_map/reduce_scatter | solution.py:343
  (408 shorter events, 229.1 us)
Async XLA Ops:
  7.2 61.6 %all-gather.8.cloned.1.call-start = ((), (), s32[]{:S(2)}) async-start(), calls=%async_computation.4 | async-start | bytes 1622016 | tf_op jit(solution)/shard_map/all_gather | solution.py:114
  7.9 143.1 %all-gather.12.cloned.1.call-start = ((), (), s32[]{:S(2)}) async-start(), calls=%async_computation.6 | async-start | bytes 4456448 | tf_op jit(solution)/shard_map/all_gather | solution.py:194
  58.0 13.7 %copy-start.28 = (f32[512]{0:T(512)}, f32[512]{0:T(512)S(1)}, u32[]{:S(2)}) copy-start(f32[512]{0:T(512)S(1)} %convert_element_type.168) | copy-start | bytes 6148
  58.0 13.7 %copy-start.30 = (f32[512]{0:T(512)}, f32[512]{0:T(512)S(1)}, u32[]{:S(2)}) copy-start(f32[512]{0:T(512)S(1)} %convert_element_type.169) | copy-start | bytes 6148
  59.1 12.6 %copy-start.32 = (f32[256]{0:T(256)}, f32[256]{0:T(256)S(1)}, u32[]{:S(2)}) copy-start(f32[256]{0:T(256)S(1)} %broadcast_multiply_fusion.1) | copy-start | bytes 3076
  71.7 122.4 %all-gather.10.cloned.1.call-start = ((), (), s32[]{:S(2)}) async-start(), calls=%async_computation.5 | async-start | bytes 4456448 | tf_op jit(solution)/shard_map/all_gather | solution.py:195
  72.6 78.1 %copy-start.13 = (bf16[256,512]{1,0:T(8,128)(2,1)}, bf16[256,512]{1,0:T(8,128)(2,1)S(1)}, u32[]{:S(2)}) copy-start(bf16[256,512]{1,0:T(8,128)(2,1)S(1)} %get-tuple-element.1039) | copy-start | bytes 786436
  72.6 183.8 %all-gather.14.cloned.1.call-start = ((), (), s32[]{:S(2)}) async-start(), calls=%async_computation.7 | async-start | bytes 2162688 | tf_op jit(solution)/shard_map/all_gather | solution.py:123
  73.2 218.1 %all-gather.16.cloned.1.call-start = ((), (), s32[]{:S(2)}) async-start(), calls=%async_computation.8 | async-start | bytes 2162688 | tf_op jit(solution)/shard_map/all_gather | solution.py:125
  73.8 325.8 %all-gather.18.cloned.1.call-start = ((), (), s32[]{:S(2)}) async-start(), calls=%async_computation.9 | async-start | bytes 4456448 | tf_op jit(solution)/shard_map/all_gather | solution.py:291
  150.8 248.8 %all-gather.20.cloned.1.call-start = ((), (), s32[]{:S(2)}) async-start(), calls=%async_computation.10 | async-start | bytes 4456448 | tf_op jit(solution)/shard_map/all_gather | solution.py:292
  200.4 54.2 %copy-start.1 = (bf16[1,256,512]{2,1,0:T(8,128)(2,1)S(1)}, bf16[1,256,512]{2,1,0:T(8,128)(2,1)}, u32[]{:S(2)}) copy-start(bf16[1,256,512]{2,1,0:T(8,128)(2,1)} %param.25) | copy-start | bytes 786436
  256.1 89.8 %copy-start.2 = (f32[256,512]{1,0:T(8,128)}, f32[256,512]{1,0:T(8,128)S(1)}, u32[]{:S(2)}) copy-start(f32[256,512]{1,0:T(8,128)S(1)} %get-tuple-element.1044) | copy-start | bytes 1572868
  256.4 35.0 %copy-start.10 = (bf16[1,256,512]{2,1,0:T(8,128)(2,1)S(1)}, bf16[1,256,512]{2,1,0:T(8,128)(2,1)}, u32[]{:S(2)}) copy-start(bf16[1,256,512]{2,1,0:T(8,128)(2,1)} %param.41) | copy-start | bytes 786436
  299.3 234.1 %reduce-scatter.7.cloned.1.call-start = ((), (), s32[]{:S(2)}) async-start(), calls=%async_computation.12 | async-start | bytes 1081344 | tf_op jit(solution)/shard_map/reduce_scatter | solution.py:346
  301.7 371.3 %reduce-scatter.9.cloned.1.call-start = ((), (), s32[]{:S(2)}) async-start(), calls=%async_computation.13 | async-start | bytes 4325376 | tf_op jit(solution)/shard_map/reduce_scatter | solution.py:235
  304.5 41.4 %copy-start.18 = (bf16[256,2048]{1,0:T(8,128)(2,1)S(1)}, bf16[256,2048]{1,0:T(8,128)(2,1)}, u32[]{:S(2)}) copy-start(bf16[256,2048]{1,0:T(8,128)(2,1)} %copy-done.17) | copy-start | bytes 3145732
  348.8 466.2 %reduce-scatter.11.cloned.1.call-start = ((), (), s32[]{:S(2)}) async-start(), calls=%async_computation.14 | async-start | bytes 4325376 | tf_op jit(solution)/shard_map/reduce_scatter | solution.py:237
  349.6 46.0 %copy-start.11 = (bf16[1,256,512]{2,1,0:T(8,128)(2,1)S(1)}, bf16[1,256,512]{2,1,0:T(8,128)(2,1)}, u32[]{:S(2)}) copy-start(bf16[1,256,512]{2,1,0:T(8,128)(2,1)} %param.41) | copy-start | bytes 786436
  399.5 520.6 %reduce-scatter.5.cloned.1.call-start = ((), (), s32[]{:S(2)}) async-start(), calls=%async_computation.11 | async-start | bytes 3244032 | tf_op jit(solution)/shard_map/reduce_scatter | solution.py:343
  400.1 80.5 %copy-start.29 = (f32[512]{0:T(512)S(1)}, f32[512]{0:T(512)}, u32[]{:S(2)}) copy-start(f32[512]{0:T(512)} %copy-done.28) | copy-start | bytes 6148
  400.1 80.5 %copy-start.31 = (f32[512]{0:T(512)S(1)}, f32[512]{0:T(512)}, u32[]{:S(2)}) copy-start(f32[512]{0:T(512)} %copy-done.30) | copy-start | bytes 6148
  400.1 80.5 %copy-start.33 = (f32[256]{0:T(256)S(1)}, f32[256]{0:T(256)}, u32[]{:S(2)}) copy-start(f32[256]{0:T(256)} %copy-done.32) | copy-start | bytes 3076
  400.1 80.5 %copy-start.35 = (f32[256]{0:T(256)S(1)}, f32[256]{0:T(256)}, u32[]{:S(2)}) copy-start(f32[256]{0:T(256)} %copy-done.34) | copy-start | bytes 3076
  (49 other events, 144.3 us)
Sparse Core Ops, SparseCore 0:
  10.9 57.8 all-gather.7
  71.8 51.1 all-gather.11
  125.8 49.2 all-gather.9
  178.0 54.9 all-gather.13
  235.8 55.4 all-gather.15
  293.3 50.0 all-gather.17
  346.1 49.3 all-gather.19
  398.3 133.8 reduce-scatter.6
  535.2 137.8 reduce-scatter.8
  675.9 139.0 reduce-scatter.10
  821.9 98.2 reduce-scatter.4
where the time goes:
time: 929 us; the launch traced here: 927 us
  waiting for transfers between devices  423 us (46%)
  blocking collectives  196 us (21%)
  matrix products  165 us (18%)
  local copies, waits for them, and re-layouts  81.9 us (9%)
  other arithmetic  33.9 us (4%)
  between operations  14.4 us (2%)
  loops' own time  11.6 us (1%)
    reduce_scatter x1, waiting for transfers between devices, shards(): lax.psum_scatter(grad_down_w, ('blk', 'fsdp'), scatter_dimension=0, tiled...  142 us
    reduce_scatter x1, waiting for transfers between devices, shards(): lax.psum_scatter(grad_up_w, ('blk', 'fsdp'), scatter_dimension=0, tiled=T...  140 us
    reduce_scatter x1, waiting for transfers between devices, shards(): lax.psum_scatter(grad_qkv_w, ('blk', 'fsdp'), scatter_dimension=0, tiled=...  105 us
    unnamed x2, blocking collectives  79.7 us
    all_gather x1, blocking collectives, shards(): lax.all_gather(out_weight, ('blk', 'fsdp'), axis=0, tiled=True)  76.5 us
    dot_general x16, matrix products, head_scores(): jnp.einsum('qhd,khd->hqk', left_heads, right_heads, preferred_element_typ...  48.2 us
    dynamic_slice x40, local copies, waits for them, and re-layouts, blockwise(): lax.scan(scan_turn, running, (jnp.arange(block_count, dtype=jnp.int32), s...  42 us
    unnamed x110, local copies, waits for them, and re-layouts  32.4 us
  transfers between devices with their start and end apart: 11, of which 5 were waited for; matrix products, arithmetic and copies ran while one was open for 29% of the time, Pallas kernels for 0%

commit v1 on v0

v1 whole, which is shorter than its diff:
```python
import functools
import math

import jax
import jax.numpy as jnp
from jax import lax
from jax.experimental import pallas as pl
from jax.experimental.pallas import tpu as pltpu
from jax.sharding import PartitionSpec as P

H = 4
HD = 128
SLAB = 16
EPSILON = 1e-05
MASKED = -1e30
LN2 = math.log(2.0)
MESH = pl.DeviceIdType.MESH
F32 = jnp.float32
BF16 = jnp.bfloat16


def dot_nn(a, b):
    return lax.dot_general(a, b, (((1,), (0,)), ((), ())), preferred_element_type=F32)


def dot_nt(a, b):
    return lax.dot_general(a, b, (((1,), (1,)), ((), ())), preferred_element_type=F32)


def dot_tn(a, b):
    return lax.dot_general(a, b, (((0,), (0,)), ((), ())), preferred_element_type=F32)


def moments(v):
    mean = jnp.mean(v, axis=-1, keepdims=True)
    centered = v - mean
    rstd = lax.rsqrt(jnp.mean(centered * centered, axis=-1, keepdims=True) + EPSILON)
    return mean, centered, rstd


def norm_back(g, n, r):
    return r * (g - jnp.mean(g, axis=-1, keepdims=True) - n * jnp.mean(g * n, axis=-1, keepdims=True))


def three_terms(v):
    first = v.astype(BF16)
    rest = v - first.astype(F32)
    second = rest.astype(BF16)
    third = (rest - second.astype(F32)).astype(BF16)
    return first.astype(F32), second.astype(F32), third.astype(F32)


def col_sum(v):
    return jnp.sum(v, axis=0, keepdims=True)


def fold_rows(v):
    return jnp.sum(v.reshape(v.shape[0] // 8, 8, v.shape[1]), axis=0)


def body(
    Z, FK, R, D, NT,
    tok_ref, cot_ref, wq_ref, wo_ref, wu_ref, wd_ref, sm_ref, len_ref, sup_ref,
    out_ref, gtok_ref, gqkv_ref, gout_ref, gup_ref, gdown_ref, gsm_ref,
    tokb, kb, vb, eb, stat, w0, w1, w2, g0, g1, g2,
    c0, c1, c2, x0, x1, x2, y0, y1, y2, z0, z1, z2,
    crf, yrf, zrf, par, upb, qt, dot_, qs, dos, ot, mrun, dqt,
    nrm2, hid, acc, gsec, xg, dwkv, lacc, upg, xown,
    sg, src, srx, sry, srz,
    s_tz, s_ty, s_tc, r_t,
    s_wz, r_wz, s_wy, r_wy, s_wx, r_wx, s_wc, r_wc,
    s_gc, r_gc, s_gx, r_gx, s_gy, r_gy, s_gz, r_gz,
    s_pc, r_pc, s_py, r_py, s_pz, r_pz,
    s_sc, r_sc, s_sx, r_sx, s_sy, r_sy, s_sz, r_sz,
):
    i = lax.axis_index("blk")
    f = lax.axis_index("fsdp")
    c = lax.rem(i, 2)
    y = lax.rem(i // 2, 2)
    z = i // 4
    oc = 1 - c
    oy = 1 - y
    CH = 4 * FK * SLAB * 4
    FF = Z * CH
    NSH = Z * 4 * FK
    KEEP = Z <= 4

    def dev(zz, yy, cc, ff):
        return ((zz * 2 + yy) * 2 + cc, ff)

    d_core = dev(z, y, oc, f)
    d_y = dev(z, oy, c, f)

    def zplus(k):
        return lax.rem(z + k, Z)

    def fplus(k):
        return lax.rem(f + k, FK)

    def d_z(zz):
        return dev(zz, y, c, f)

    def d_f(ff):
        return (i, ff)

    def cp(s, d, ss, rs, to):
        return pltpu.make_async_remote_copy(
            src_ref=s, dst_ref=d, send_sem=ss, recv_sem=rs, device_id=to, device_id_type=MESH
        )

    def push(s, d, ss, rs, to):
        cp(s, d, ss, rs, to).start()

    def got(d, rs):
        cp(d, d, rs, rs, d_core).wait_recv()

    def sent(s, ss):
        cp(s, s, ss, ss, d_core).wait_send()

    bar = pltpu.get_barrier_semaphore()
    partners = [d_core, d_y] + [d_z(zplus(k)) for k in range(1, Z)] + [d_f(fplus(k)) for k in range(1, FK)]
    for to in partners:
        pl.semaphore_signal(bar, inc=1, device_id=to, device_id_type=MESH)
    pl.semaphore_wait(bar, len(partners))

    def tok_push(zz, ss_z, to):
        t = tokb.at[zz, y, c]
        push(t, t, ss_z, r_t.at[zz, y, c], to)

    def tok_side(zz):
        t = tokb.at[zz, y, c]
        push(t, t, s_ty.at[zz], r_t.at[zz, y, c], d_y)
        push(t, t, s_tc.at[zz, 0], r_t.at[zz, y, c], d_core)

    def tok_right(zz):
        @pl.when(z < Z - 1)
        def _():
            tok_push(zz, s_tz.at[0, zz], d_z(z + 1))

    def tok_left(zz):
        @pl.when(z > 0)
        def _():
            tok_push(zz, s_tz.at[1, zz], d_z(z - 1))

    def tok_z(k):
        @pl.when(z - k >= 0)
        def _():
            zz = z - k
            got(tokb.at[zz, y, c], r_t.at[zz, y, c])
            tok_right(zz)
            tok_side(zz)

        @pl.when(z + k < Z)
        def _():
            zz = z + k
            got(tokb.at[zz, y, c], r_t.at[zz, y, c])
            tok_left(zz)
            tok_side(zz)

    def tok_y_one(zz):
        t = tokb.at[zz, oy, c]
        got(t, r_t.at[zz, oy, c])
        push(t, t, s_tc.at[zz, 1], r_t.at[zz, oy, c], d_core)

    def tok_y(k):
        if k == 0:
            tok_y_one(z)
        else:
            @pl.when(z - k >= 0)
            def _():
                tok_y_one(z - k)

            @pl.when(z + k < Z)
            def _():
                tok_y_one(z + k)

    wb = (w0, w1, w2)

    def w_side(g, zz, yy):
        for k in range(1, FK):
            ff = fplus(k)
            t = wb[g].at[zz, yy, c, f]
            push(t, t, s_wx.at[g, ff, zz, yy], r_wx.at[g, f, zz, yy], d_f(ff))

    def w_own(g):
        t = wb[g].at[z, y, c, f]
        for k in range(1, Z):
            zz = zplus(k)
            push(t, t, s_wz.at[g, zz], r_wz.at[g, z], d_z(zz))
        push(t, t, s_wy.at[g, z], r_wy.at[g, z], d_y)
        w_side(g, z, y)

    def w_z(g):
        for k in range(1, Z):
            zz = zplus(k)
            t = wb[g].at[zz, y, c, f]
            got(t, r_wz.at[g, zz])
            push(t, t, s_wy.at[g, zz], r_wy.at[g, zz], d_y)
            w_side(g, zz, y)

    def w_core(g, ff, n):
        t = wb[g].at[:, :, c, ff]
        push(t, t, s_wc.at[g, n], r_wc.at[g, n], d_core)

    def w_y(g):
        for k in range(Z):
            zz = zplus(k)
            got(wb[g].at[zz, oy, c, f], r_wy.at[g, zz])
            w_side(g, zz, oy)
        w_core(g, f, 0)

    def w_x(g):
        for k in range(1, FK):
            ff = fplus(k)
            for zz in range(Z):
                for yy in range(2):
                    got(wb[g].at[zz, yy, c, ff], r_wx.at[g, ff, zz, yy])
            w_core(g, ff, k)

    def w_c(g):
        for k in range(FK):
            got(wb[g].at[:, :, oc, fplus(k)], r_wc.at[g, k])

    tokb[z, y, c] = tok_ref[...]
    w0[z, y, c, f, :, 0 : 3 * D] = wq_ref[...]
    w0[z, y, c, f, :, 3 * D : 3 * D + 128] = sm_ref[...]
    w1[z, y, c, f, :, 0:D] = wo_ref[...]
    w1[z, y, c, f, :, D : D + FF] = wu_ref[...]
    w2[z, y, c, f] = wd_ref[...]

    w_own(0)
    tok_right(z)
    tok_left(z)
    tok_side(z)
    w_own(1)
    w_own(2)

    starts, ends, stops = [], [], []
    total = jnp.int32(0)
    for t in range(NT):
        starts.append(total)
        stops.append(total + sup_ref[0, t])
        total = total + len_ref[0, t]
        ends.append(total)

    lane = lax.broadcasted_iota(jnp.int32, (1, 128), 1)
    lane_start = jnp.zeros((1, 128), jnp.int32)
    lane_stop = jnp.zeros((1, 128), jnp.int32)
    for t in range(NT):
        lane_start = jnp.where(lane == t, starts[t], lane_start)
        lane_stop = jnp.where(lane == t, stops[t], lane_stop)
    lane_ones = jnp.where((lane >= NT) & (lane < NT + 3), 1.0, 0.0)

    def mask_of(n):
        pos = n * R + lax.broadcasted_iota(jnp.int32, (R, 128), 0)
        seen = (pos >= lane_start) & (pos < lane_stop)
        extra = jnp.where(lane < NT, jnp.where(seen, 0.0, MASKED), lane_ones)
        return extra.astype(BF16)

    def mask_block(n, carry):
        eb[n] = mask_of(n)
        return carry

    if KEEP:
        lax.fori_loop(0, 4 * Z, mask_block, 0)

    row = lax.broadcasted_iota(jnp.int32, (128, R), 0)
    qpos = i * R + lax.broadcasted_iota(jnp.int32, (128, R), 1)
    onehot = jnp.zeros((128, R), F32)
    for t in range(NT):
        onehot = jnp.where((row == t) & (qpos >= starts[t]) & (qpos < ends[t]), 1.0, onehot)

    tok_z(1)
    w_z(0)
    tok_y(0)
    for k in range(2, Z):
        tok_z(k)
        if k == 2:
            w_y(0)
            w_z(1)
        tok_y(k - 1)
    w_x(0)
    tok_y(Z - 1)
    w_z(2)
    w_c(0)

    piece = D // NSH
    small = w0[:, :, :, :, :, 3 * D : 3 * D + 128].reshape(NSH * SLAB, 128)
    spread = (
        lax.rem(lax.broadcasted_iota(jnp.int32, (128, D), 1), piece)
        == lax.broadcasted_iota(jnp.int32, (128, D), 0)
    )
    wide = dot_nn(small, spread.astype(BF16))
    mine = (
        lax.broadcasted_iota(jnp.int32, (NSH * SLAB, D), 1) // piece
        == lax.broadcasted_iota(jnp.int32, (NSH * SLAB, D), 0) // SLAB
    )
    wide = jnp.where(mine, wide, 0.0)
    par[...] = jnp.sum(wide.reshape(NSH, SLAB, D), axis=0)
    pick = (
        lax.broadcasted_iota(jnp.int32, (NSH, NSH * SLAB), 1)
        == lax.broadcasted_iota(jnp.int32, (NSH, NSH * SLAB), 0) * SLAB + 8
    )
    ups = dot_nn(pick.astype(BF16), small).astype(BF16)
    spread = (
        lax.rem(lax.broadcasted_iota(jnp.int32, (128, FF), 1), 4 * piece)
        == lax.broadcasted_iota(jnp.int32, (128, FF), 0)
    )
    wide = dot_nn(ups, spread.astype(BF16))
    mine = (
        lax.broadcasted_iota(jnp.int32, (NSH, FF), 1) // (4 * piece)
        == lax.broadcasted_iota(jnp.int32, (NSH, FF), 0)
    )
    upb[...] = col_sum(jnp.where(mine, wide, 0.0))
    ln1g, ln1b = par[0:1, :], par[1:2, :]

    tokens = tok_ref[...].astype(F32)
    mean, centered, rstd = moments(tokens)
    own = (centered * rstd * ln1g + ln1b).astype(BF16)
    xown[...] = own
    wq = w0[:, :, :, :, :, 0:D].reshape(D, D)
    qscale = HD ** (-0.5) / LN2
    qs[...] = ((dot_nn(own, wq) + par[2:3, :]) * qscale).astype(BF16)
    for h in range(H):
        qt[h, 0:HD, :] = qs[:, h * HD : (h + 1) * HD].T
        qt[h, HD : 2 * HD, :] = onehot.astype(BF16)
        ot[h] = jnp.zeros((2 * HD, R), F32)
        mrun[h] = jnp.full((1, R), MASKED, F32)

    def place(n):
        zz = zplus(n // 4)
        part = lax.rem(n, 4)
        yy = lax.rem(y + part // 2, 2)
        cc = lax.rem(c + part, 2)
        return zz, yy, cc

    def ahead(n, carry):
        zz, yy, cc = place(n)

        @pl.when(lax.rem(n, 2) == 1)
        def _():
            got(tokb.at[zz, yy, cc], r_t.at[zz, yy, cc])

        b = (zz * 2 + yy) * 2 + cc
        mean, centered, rstd = moments(tokb[zz, yy, cc].astype(F32))
        if KEEP:
            stat[b] = jnp.where(lax.broadcasted_iota(jnp.int32, (R, 128), 1) == 0, mean, rstd)
        x = (centered * rstd * par[0:1, :] + par[1:2, :]).astype(BF16)
        kv = dot_nn(x, w0[:, :, :, :, :, D : 3 * D].reshape(D, 2 * D))
        keys = kv[:, 0:D].astype(BF16)
        values = (kv[:, D : 2 * D] + par[3:4, :]).astype(BF16)
        kb[b] = keys
        vb[b] = values
        extra = eb[b] if KEEP else mask_of(b)
        for h in range(H):
            cols = slice(h * HD, (h + 1) * HD)
            s = dot_nn(jnp.concatenate([keys[:, cols], extra], axis=1), qt[h])
            before = mrun[h]
            top = jnp.maximum(before, jnp.ceil(jnp.max(s, axis=0, keepdims=True)))
            e = jnp.exp2(s - top).astype(BF16)
            grown = dot_tn(jnp.concatenate([values[:, cols], extra], axis=1), e)
            ot[h] = ot[h] * jnp.exp2(before - top) + grown
            mrun[h] = top
        return carry

    lax.fori_loop(0, 4 * Z, ahead, 0)

    w_y(1)
    w_y(2)
    w_x(1)
    w_x(2)
    w_c(1)
    w_c(2)

    parts = []
    for h in range(H):
        inverse = 1.0 / ot[h, HD + NT : HD + NT + 1, :]
        attended = ot[h, 0:HD, :] * inverse
        ot[h, 0:HD, :] = attended
        dot_[h, HD : HD + 1, :] = inverse.astype(BF16)
        ot[h, HD : HD + 1, :] = inverse
        parts.append(attended.T.astype(BF16))
        m1, m2, m3 = three_terms(mrun[h])
        tail = jnp.where(row == NT, -m1, jnp.where(row == NT + 1, -m2, jnp.where(row == NT + 2, -m3, onehot)))
        qt[h, HD : 2 * HD, :] = tail.astype(BF16)
    attn_low = jnp.concatenate(parts, axis=1)
    w_out = w1[:, :, :, :, :, 0:D].reshape(D, D)
    hidden = tokens + (dot_nn(attn_low, w_out) + par[4:5, :])
    hid[...] = hidden
    mean2, centered, rstd2 = moments(hidden)
    n2 = centered * rstd2
    nrm2[...] = (n2 * par[5:6, :] + par[6:7, :]).astype(BF16)
    acc[...] = hidden + par[7:8, :]
    gsec[...] = jnp.zeros((R, D), F32)

    def chunk(j, carry):
        cols = pl.ds(pl.multiple_of(D + j * CH, 128), CH)
        bcols = pl.ds(pl.multiple_of(j * CH, 128), CH)
        up = w1[:, :, :, :, :, cols].reshape(D, CH)
        down = w2[j].reshape(CH, D)
        normed = nrm2[...]
        cot = cot_ref[...]
        pre = dot_nn(normed, up) + upb[:, bcols]
        phi = 0.5 * (1.0 + lax.erf(pre * (0.5**0.5)))
        act = (pre * phi).astype(BF16)
        slope = phi + pre * (jnp.exp2(pre * pre * (-0.5 / LN2)) * ((2.0 * math.pi) ** -0.5))
        acc[...] += dot_nn(act, down)
        gpre32 = dot_nt(cot, down) * slope
        gpre = gpre32.astype(BF16)
        gsec[...] += dot_nt(gpre, up)
        upg[:, bcols] = col_sum(gpre.astype(F32))
        g1[:, :, :, :, :, cols] = dot_tn(normed, gpre).astype(BF16).reshape(Z, 2, 2, FK, SLAB, CH)
        g2[j] = dot_tn(act, cot).astype(BF16).reshape(2, 2, FK, 4 * SLAB, D)
        return carry

    lax.fori_loop(0, Z, chunk, 0)
    out_ref[...] = acc[...].astype(BF16)

    gb = (g0, g1, g2)
    cb = (c0, c1, c2)
    xb = (x0, x1, x2)
    yb = (y0, y1, y2)
    zb = (z0, z1, z2)

    def r_c(g):
        push(gb[g].at[:, :, oc], cb[g], s_gc.at[g], r_gc.at[g], d_core)

    def r_x(g):
        got(cb[g], r_gc.at[g])

        def one(zz, carry):
            t = gb[g][zz, :, c].astype(F32) + cb[g][zz].astype(F32)
            gb[g][zz, :, c] = t.astype(BF16)
            return carry

        lax.fori_loop(0, Z, one, 0)
        for k in range(1, FK):
            ff = fplus(k)
            push(gb[g].at[:, :, c, ff], xb[g].at[f], s_gx.at[g, ff], r_gx.at[g, f], d_f(ff))

    def r_y(g):
        for k in range(1, FK):
            got(xb[g].at[fplus(k)], r_gx.at[g, fplus(k)])

        if FK > 1:
            def one(zz, carry):
                t = gb[g][zz, :, c, f].astype(F32)
                for k in range(1, FK):
                    t = t + xb[g][fplus(k), zz].astype(F32)
                gb[g][zz, :, c, f] = t.astype(BF16)
                return carry

            lax.fori_loop(0, Z, one, 0)
        push(gb[g].at[:, oy, c, f], yb[g], s_gy.at[g], r_gy.at[g], d_y)

    def r_z(g):
        got(yb[g], r_gy.at[g])

        def one(zz, carry):
            t = gb[g][zz, y, c, f].astype(F32) + yb[g][zz].astype(F32)
            gb[g][zz, y, c, f] = t.astype(BF16)
            return carry

        lax.fori_loop(0, Z, one, 0)
        for k in range(1, Z):
            zz = zplus(k)
            push(gb[g].at[zz, y, c, f], zb[g].at[z], s_gz.at[g, zz], r_gz.at[g, z], d_z(zz))

    def r_end(g):
        t = gb[g][z, y, c, f].astype(F32)
        for k in range(1, Z):
            zz = zplus(k)
            got(zb[g].at[zz], r_gz.at[g, zz])
            t = t + zb[g][zz].astype(F32)
        return t

    def r_sent(g):
        sent(gb[g].at[:, :, oc], s_gc.at[g])
        for k in range(1, FK):
            sent(gb[g].at[:, :, c, fplus(k)], s_gx.at[g, fplus(k)])
        sent(gb[g].at[:, oy, c, f], s_gy.at[g])
        for k in range(1, Z):
            sent(gb[g].at[zplus(k), y, c, f], s_gz.at[g, zplus(k)])

    r_c(2)

    g_second = gsec[...]
    n2 = (hid[...] - mean2) * rstd2
    ln2g = par[5:6, :]
    cot32 = cot_ref[...].astype(F32)
    grad_hidden = cot32 + norm_back(g_second * ln2g, n2, rstd2)
    hid[...] = grad_hidden
    g_branch = grad_hidden.astype(BF16)
    g1[:, :, :, :, :, 0:D] = dot_tn(attn_low, g_branch).astype(BF16).reshape(Z, 2, 2, FK, SLAB, D)
    r_c(1)
    zero = jnp.zeros((1, D), F32)
    for r in range(SLAB):
        sg[0, r : r + 1, :] = zero
    sg[0, 4:5, :] = col_sum(g_branch.astype(F32))
    sg[0, 5:6, :] = col_sum(g_second * n2)
    sg[0, 6:7, :] = col_sum(g_second)
    sg[0, 7:8, :] = col_sum(cot32)
    for r in range(FF // D):
        sg[0, 8 + r : 9 + r, :] = upg[:, r * D : (r + 1) * D]

    for h in range(H):
        rows = slice(h * HD, (h + 1) * HD)
        w_head = w1[:, :, :, :, :, 0:D].reshape(D, D)[rows, :]
        ga = dot_nt(w_head, g_branch).astype(BF16).astype(F32)
        low = (ga * ot[h, HD : HD + 1, :]).astype(BF16)
        delta = col_sum(low.astype(F32) * ot[h, 0:HD, :])
        d1, d2, d3 = three_terms(delta)
        tail = jnp.where(row == NT, -d1, jnp.where(row == NT + 1, -d2, jnp.where(row == NT + 2, -d3, 0.0)))
        dot_[h, 0:HD, :] = low
        dot_[h, HD : 2 * HD, :] = tail.astype(BF16)
        dos[:, rows] = low.T
        dqt[h] = jnp.zeros((HD, R), F32)

    def tok_sent():
        @pl.when(z < Z - 1)
        def _():
            for k in range(Z):
                @pl.when(z - k >= 0)
                def _():
                    sent(tokb.at[z - k, y, c], s_tz.at[0, z - k])

        @pl.when(z > 0)
        def _():
            for k in range(Z):
                @pl.when(z + k < Z)
                def _():
                    sent(tokb.at[z + k, y, c], s_tz.at[1, z + k])

        for zz in range(Z):
            sent(tokb.at[zz, y, c], s_ty.at[zz])
            sent(tokb.at[zz, y, c], s_tc.at[zz, 0])
            sent(tokb.at[zz, oy, c], s_tc.at[zz, 1])

    tok_sent()

    dwkv[...] = jnp.zeros((D, 2 * D), F32)
    lacc[...] = jnp.zeros((3, 8, D), F32)

    def p_c(zz, yy):
        push(tokb.at[zz, yy, oc], crf.at[zz, yy], s_pc.at[zz, yy], r_pc.at[zz, yy], d_core)

    def p_y(zz):
        got(crf.at[zz, oy], r_pc.at[zz, oy])
        t = tokb[zz, oy, c].astype(F32) + crf[zz, oy].astype(F32)
        tokb[zz, oy, c] = t.astype(BF16)
        push(tokb.at[zz, oy, c], yrf.at[zz], s_py.at[zz], r_py.at[zz], d_y)

    def p_sum(zz):
        got(crf.at[zz, y], r_pc.at[zz, y])
        got(yrf.at[zz], r_py.at[zz])
        return tokb[zz, y, c].astype(F32) + crf[zz, y].astype(F32) + yrf[zz].astype(F32)

    def p_z(zz):
        tokb[zz, y, c] = p_sum(zz).astype(BF16)
        push(tokb.at[zz, y, c], zrf.at[z], s_pz.at[zz], r_pz.at[z], d_z(zz))

    def back_place(n):
        zz = zplus(1 + n // 4)
        part = lax.rem(n, 4)
        yy = lax.rem(y + 1 + part // 2, 2)
        cc = lax.rem(c + 1 + part, 2)
        return zz, yy, cc

    timed = {3: (r_x, 2), 7: (r_x, 1), 13: (r_y, 2)}

    def behind(n, carry):
        zz, yy, cc = back_place(n)
        part = lax.rem(n, 4)

        for at, (step, g) in timed.items():
            @pl.when(n == at)
            def _():
                step(g)

        @pl.when((part == 0) & (n >= 8))
        def _():
            p_z(zplus(n // 4 - 1))

        @pl.when(part == 3)
        def _():
            p_y(zz)

        b = (zz * 2 + yy) * 2 + cc
        keys, values, extra = kb[b], vb[b], eb[b] if KEEP else mask_of(b)
        dks, dvs = [], []
        for h in range(H):
            cols = slice(h * HD, (h + 1) * HD)
            s = dot_nn(jnp.concatenate([keys[:, cols], extra], axis=1), qt[h])
            dp = dot_nn(jnp.concatenate([values[:, cols], extra], axis=1), dot_[h])
            e = jnp.exp2(s).astype(BF16)
            ds = (e.astype(F32) * dp).astype(BF16)
            dvs.append(dot_nn(e, dos[:, cols]))
            dks.append(dot_nn(ds, qs[:, cols]) * LN2)
            dqt[h] += dot_tn(keys[:, cols], ds)
        dv = jnp.concatenate(dvs, axis=1)
        dkv = jnp.concatenate(dks + [dv], axis=1).astype(BF16)
        kb[b] = dkv[:, 0:D]
        vb[b] = dkv[:, D : 2 * D]
        gp = dot_nt(dkv, w0[:, :, :, :, :, D : 3 * D].reshape(D, 2 * D))
        if KEEP:
            norm = (tokb[zz, yy, cc].astype(F32) - stat[b, :, 0:1]) * stat[b, :, 1:2]
        else:
            mean, centered, rstd = moments(tokb[zz, yy, cc].astype(F32))
            norm = centered * rstd
        span = pl.ds(pl.multiple_of((yy * 2 + cc) * R, R), R)
        xg[span, :] = (norm * par[0:1, :] + par[1:2, :]).astype(BF16)
        lacc[0] += fold_rows(gp * norm)
        lacc[1] += fold_rows(gp)
        lacc[2] += fold_rows(dv)
        tokb[zz, yy, cc] = gp.astype(BF16)

        @pl.when(lax.rem(part, 2) == 0)
        def _():
            p_c(zz, yy)

        @pl.when(part == 3)
        def _():
            xs = xg[...]
            four = pl.ds(pl.multiple_of(zz * 4, 4), 4)
            dwkv[:, 0:D] += dot_tn(xs, kb[four].reshape(4 * R, D))
            dwkv[:, D : 2 * D] += dot_tn(xs, vb[four].reshape(4 * R, D))

        return carry

    lax.fori_loop(0, 4 * Z, behind, 0)

    dq = jnp.concatenate([(dqt[h] * (HD**-0.5)).T for h in range(H)], axis=1).astype(BF16)
    own = xown[...]
    g0[:, :, :, :, :, 0:D] = dot_tn(own, dq).astype(BF16).reshape(Z, 2, 2, FK, SLAB, D)
    g0[:, :, :, :, :, D : 3 * D] = dwkv[...].astype(BF16).reshape(Z, 2, 2, FK, SLAB, 2 * D)
    r_c(0)
    gq = dot_nt(dq, w0[:, :, :, :, :, 0:D].reshape(D, D))
    mean, centered, rstd1 = moments(tok_ref[...].astype(F32))
    n1 = centered * rstd1
    sg[0, 0:1, :] = col_sum(lacc[0]) + col_sum(gq * n1)
    sg[0, 1:2, :] = col_sum(lacc[1]) + col_sum(gq)
    sg[0, 2:3, :] = col_sum(dq.astype(F32))
    sg[0, 3:4, :] = col_sum(lacc[2])
    push(sg.at[0], src, s_sc, r_sc, d_core)

    if Z >= 2:
        p_z(zplus(Z - 1))
    r_x(0)
    got(src, r_sc)
    sg[1] = sg[0] + src[...]
    for k in range(1, FK):
        ff = fplus(k)
        push(sg.at[1], srx.at[f], s_sx.at[ff], r_sx.at[f], d_f(ff))
    r_y(1)
    r_z(2)
    acc[...] = p_sum(z) + gq
    r_y(0)
    t = sg[1]
    for k in range(1, FK):
        got(srx.at[fplus(k)], r_sx.at[fplus(k)])
        t = t + srx[fplus(k)]
    sg[2] = t
    push(sg.at[2], sry, s_sy, r_sy, d_y)
    r_z(1)
    r_z(0)
    got(sry, r_sy)
    sg[3] = sg[2] + sry[...]
    for k in range(1, Z):
        zz = zplus(k)
        push(sg.at[3], srz.at[z], s_sz.at[zz], r_sz.at[z], d_z(zz))

    t = acc[...]
    for k in range(1, Z):
        zz = zplus(k)
        got(zrf.at[zz], r_pz.at[zz])
        t = t + zrf[zz].astype(F32)
    gtok_ref[...] = (hid[...] + norm_back(t * par[0:1, :], n1, rstd1)).astype(BF16)

    gdown_ref[...] = r_end(2)
    t = r_end(1)
    gout_ref[...] = t[:, 0:D]
    gup_ref[...] = t[:, D : D + FF]
    gqkv_ref[...] = r_end(0)
    t = sg[3]
    for k in range(1, Z):
        zz = zplus(k)
        got(srz.at[zz], r_sz.at[zz])
        t = t + srz[zz]
    gsm_ref[...] = t

    for g in range(3):
        t = wb[g].at[z, y, c, f]
        for k in range(1, Z):
            sent(t, s_wz.at[g, zplus(k)])
        for zz in range(Z):
            sent(wb[g].at[zz, y, c, f], s_wy.at[g, zz])
            for k in range(1, FK):
                for yy in range(2):
                    sent(wb[g].at[zz, yy, c, f], s_wx.at[g, fplus(k), zz, yy])
        for k in range(FK):
            sent(wb[g].at[:, :, c, fplus(k)], s_wc.at[g, k])
        r_sent(g)
    for zz in range(Z):
        for yy in range(2):
            sent(tokb.at[zz, yy, oc], s_pc.at[zz, yy])
        sent(tokb.at[zz, oy, c], s_py.at[zz])
    for k in range(1, Z):
        sent(tokb.at[zplus(k), y, c], s_pz.at[zplus(k)])
        sent(sg.at[3], s_sz.at[zplus(k)])
    sent(sg.at[0], s_sc)
    for k in range(1, FK):
        sent(sg.at[1], s_sx.at[fplus(k)])
    sent(sg.at[2], s_sy)


def layer(Z, FK, R, D, FF, NT, operands):
    vm = lambda shape, dtype: pltpu.VMEM(shape, dtype)
    dma = lambda *shape: pltpu.SemaphoreType.DMA(shape)
    lead = (Z, 2, 2, FK)
    half = (Z, 2, FK)
    slabs = ((SLAB, 3 * D + 128), (SLAB, D + FF), (4 * SLAB, D))
    gslabs = ((SLAB, 3 * D), (SLAB, D + FF), (4 * SLAB, D))
    scratch = [
        vm((Z, 2, 2, R, D), BF16),
        vm((4 * Z, R, D), BF16),
        vm((4 * Z, R, D), BF16),
        vm((4 * Z if Z <= 4 else 1, R, 128), BF16),
        vm((4 * Z if Z <= 4 else 1, R, 128), F32),
        *[vm(lead + s, BF16) for s in slabs],
        *[vm(lead + s, BF16) for s in gslabs],
        *[vm(half + s, BF16) for s in gslabs],
        *[vm((FK, Z, 2) + s if FK > 1 else (SLAB, 128), BF16) for s in gslabs],
        *[vm((Z,) + s, BF16) for s in gslabs],
        *[vm((Z,) + s, BF16) for s in gslabs],
        vm((Z, 2, R, D), BF16),
        vm((Z, R, D), BF16),
        vm((Z, R, D), BF16),
        vm((SLAB, D), F32),
        vm((1, FF), F32),
        vm((H, 2 * HD, R), BF16),
        vm((H, 2 * HD, R), BF16),
        vm((R, D), BF16),
        vm((R, D), BF16),
        vm((H, 2 * HD, R), F32),
        vm((H, 1, R), F32),
        vm((H, HD, R), F32),
        vm((R, D), BF16),
        vm((R, D), F32),
        vm((R, D), F32),
        vm((R, D), F32),
        vm((4 * R, D), BF16),
        vm((D, 2 * D), F32),
        vm((3, 8, D), F32),
        vm((1, FF), F32),
        vm((R, D), BF16),
        vm((4, SLAB, D), F32),
        vm((SLAB, D), F32),
        vm((FK, SLAB, D), F32),
        vm((SLAB, D), F32),
        vm((Z, SLAB, D), F32),
        dma(2, Z), dma(Z), dma(Z, 2), dma(Z, 2, 2),
        dma(3, Z), dma(3, Z), dma(3, Z), dma(3, Z),
        dma(3, FK, Z, 2), dma(3, FK, Z, 2), dma(3, FK), dma(3, FK),
        dma(3), dma(3), dma(3, FK), dma(3, FK), dma(3), dma(3), dma(3, Z), dma(3, Z),
        dma(Z, 2), dma(Z, 2), dma(Z), dma(Z), dma(Z), dma(Z),
        pltpu.SemaphoreType.DMA, pltpu.SemaphoreType.DMA,
        dma(FK), dma(FK),
        pltpu.SemaphoreType.DMA, pltpu.SemaphoreType.DMA,
        dma(Z), dma(Z),
    ]
    vmem = pl.BlockSpec(memory_space=pltpu.VMEM)
    smem = pl.BlockSpec(memory_space=pltpu.SMEM)
    shape = jax.ShapeDtypeStruct
    return pl.pallas_call(
        functools.partial(body, Z, FK, R, D, NT),
        out_shape=(
            shape((R, D), BF16),
            shape((R, D), BF16),
            shape((SLAB, 3 * D), F32),
            shape((SLAB, D), F32),
            shape((SLAB, FF), F32),
            shape((4 * SLAB, D), F32),
            shape((SLAB, D), F32),
        ),
        in_specs=[vmem] * 7 + [smem] * 2,
        out_specs=[vmem] * 7,
        scratch_shapes=scratch,
        compiler_params=pltpu.CompilerParams(
            collective_id=0, has_side_effects=True, vmem_limit_bytes=63 * 2**20
        ),
        name="layer",
    )(*operands)


def shards(
    blocks, fsdp,
    tokens, ln1_gain, ln1_bias, qkv_weight, query_bias, value_bias, out_weight, out_bias,
    ln2_gain, ln2_bias, up_weight, up_bias, down_weight, down_bias,
    table_lengths, support_lengths, cotangent,
):
    R, D = tokens.shape[1:]
    FF = up_weight.shape[1]
    NT = table_lengths.shape[1]
    smalls = (ln1_gain, ln1_bias, query_bias, value_bias, out_bias, ln2_gain, ln2_bias, down_bias, up_bias)
    weights = (qkv_weight, out_weight, up_weight, down_weight)
    inside = qkv_weight.shape[0] == SLAB
    FK = fsdp if inside else 1
    if not inside:
        whole = lambda v: lax.all_gather(v, "fsdp", axis=0, tiled=True)
        smalls = tuple(whole(v) for v in smalls)
        weights = tuple(whole(v) for v in weights)
    rows = [jnp.pad(v[None], ((0, 0), (0, 128 - v.shape[0]))) for v in smalls]
    rows.append(jnp.zeros((SLAB - len(rows), 128), BF16))
    small_tile = jnp.concatenate(rows, axis=0)
    block_out, grad_tokens, g_qkv, g_out, g_up, g_down, g_small = layer(
        blocks // 4, FK, R, D, FF, NT,
        (tokens[0], cotangent[0], *weights, small_tile, table_lengths, support_lengths),
    )
    at = lax.axis_index("blk") * FK + (lax.axis_index("fsdp") if inside else 0)
    piece = D // (blocks * FK)
    cut = lax.dynamic_slice(g_small, (0, at * piece), (8, piece))
    up_cut = lax.dynamic_slice(g_small[8 : 8 + FF // D].reshape(FF), (at * 4 * piece,), (4 * piece,))
    small_grads = [cut[r] for r in range(8)] + [up_cut]
    weight_grads = [g_qkv, g_out, g_up, g_down]
    if not inside:
        spread = lambda v: lax.psum_scatter(v, "fsdp", scatter_dimension=0, tiled=True)
        small_grads = [spread(v) for v in small_grads]
        weight_grads = [spread(v) for v in weight_grads]
    g_ln1g, g_ln1b, g_qb, g_vb, g_ob, g_ln2g, g_ln2b, g_db, g_ub = small_grads
    g_qkv, g_out, g_up, g_down = weight_grads
    return (
        block_out[None], grad_tokens[None], g_ln1g, g_ln1b, g_qkv, g_qb, g_vb, g_out, g_ob,
        g_ln2g, g_ln2b, g_up, g_ub, g_down, g_db,
    )


def solution(mesh):
    both = ("blk", "fsdp")
    vec, mat, rows = P(both), P(both, None), P("fsdp", "blk", None)
    return jax.shard_map(
        functools.partial(shards, mesh.shape["blk"], mesh.shape["fsdp"]),
        mesh=mesh,
        in_specs=(
            rows, vec, vec, mat, vec, vec, mat, vec, vec, vec, mat, vec, mat, vec,
            P("fsdp", None), P("fsdp", None), rows,
        ),
        out_specs=(rows, rows, vec, vec, mat, vec, vec, mat, vec, vec, vec, mat, vec, mat, vec),
        check_vma=False,
    )
```

time: 929 us -> 169 us (0.18)
  waiting for transfers between devices: 423 us -> 0 us
  blocking collectives: 196 us -> 0 us
  matrix products: 165 us -> 0 us
  Pallas kernels: 0 us -> 153 us
  local copies, waits for them, and re-layouts: 81.9 us -> 15.4 us
  other arithmetic: 33.9 us -> 0 us
  between operations: 14.4 us -> 0.69 us
  loops' own time: 11.6 us -> 0 us
    reduce_scatter x4 -> x0, waiting for transfers between devices: 387 us -> none  [the longest x1 142 us: shards(): lax.psum_scatter(grad_down_w, ('blk', 'fsdp'), scatter_dimension=0, tiled...]
    dot_general x48 -> x0, matrix products: 165 us -> none  [the longest x16 48.2 us: head_scores(): jnp.einsum('qhd,khd->hqk', left_heads, right_heads, preferred_element_typ...]
    pallas_call x0 -> x1, Pallas kernels: none -> 153 us  [layer(): pl.pallas_call(functools.partial(body, Z, FK, R, D, NT), out_shape=(shape...]
    all_gather x3 -> x0, blocking collectives: 116 us -> none  [the longest x1 76.5 us: shards(): lax.all_gather(out_weight, ('blk', 'fsdp'), axis=0, tiled=True)]
    unnamed x2 -> x0, blocking collectives: 79.7 us -> none
    dynamic_slice x44 -> x2, local copies, waits for them, and re-layouts: 44.9 us -> 1.34 us  [the longest x1 0.75 us: shards(): cut = lax.dynamic_slice(g_small, (0, at * piece), (8, piece))]
    all_gather x7 -> x0, waiting for transfers between devices: 34.6 us -> none  [the longest x1 26.5 us: shards(): lax.all_gather(down_weight, ('blk', 'fsdp'), axis=0, tiled=True)]
    reduce_sum x43 -> x0, other arithmetic: 22.6 us -> none  [the longest x4 12.9 us: compute_block(): jnp.sum(jnp.where(allowed[None], jnp.exp(scores - new_high[:, :, None]),...]
  transfers between devices with their start and end apart: 11 -> 0, of which waited for: 5 -> 0; matrix products, arithmetic and copies ran while one was open for 29% -> 0% of each run, Pallas kernels for 0% -> 0%
where the time goes in v1:
time: 169 us
  Pallas kernels  153 us (91%)
  local copies, waits for them, and re-layouts  15.4 us (9%)
    pallas_call x1, Pallas kernels, layer(): pl.pallas_call(functools.partial(body, Z, FK, R, D, NT), out_shape=(shape...  153 us
    unnamed x36, local copies, waits for them, and re-layouts  12.3 us

profile of v1, /device:TPU:0, one launch (start us, length us, event | category | flops | bytes accessed | tf_op | source)
XLA Modules:
  0.0 168.7 jit_solution(10540906661891776549)
XLA Ops:
  0.7 0.6 copy-done.5
  1.3 0.7 copy-done.6
  2.0 0.7 copy-done.7
  2.6 0.7 copy-done.8
  3.3 0.7 copy-done.9
  4.0 0.7 copy-done.10
  4.6 0.7 copy-done.11
  5.3 0.7 copy-done.12
  6.0 0.7 copy-done.13
  6.6 1.2 concatenate.3.sm_ref
  7.8 152.6 %layer.1 = (bf16[256,512]{1,0:T(8,128)(2,1)}, bf16[256,512]{1,0:T(8,128)(2,1)}, f32[16,1536]{1,0:T(8,128)}, f32[16,512]{1,0:T(8,128)}, f32[16,2048]{1,0:T(8,128)}, /*index=5*/f32[64,512]{1,0:T(8,128)}, f32[16,512]{1,0:T(8,128)}) custom-call(bf16[256,512]{1,0:T(8,128)(2,1)} %bitcast.32, bf16[256,512]{1,0:T(8,128)(2,1)} %bitcast.33, bf16[16,1536]{1,0:T(8,128)(2,1)} %wq_ref.1, ...), custom_call_target="tpu_custom_call" | custom-call | tf_op jit(solution)/shard_map/layer/pallas_call | solution.py:774
  160.5 0.8 constant_dynamic-slice_fusion
  161.2 0.5 slice_bitcast_fusion.1
  161.8 0.7 slice_bitcast_fusion
  162.5 0.6 dynamic_slice.7
  163.1 1.7 %copy.39 = bf16[1,256,512]{2,1,0:T(8,128)(2,1)} copy(bf16[1,256,512]{2,1,0:T(8,128)(2,1)} %bitcast.35) | data formatting | bytes 524288
  164.8 0.7 copy.40
  165.5 0.3 copy-done.3
  165.8 0.6 copy.41
  166.4 0.1 copy-done.4
  166.5 0.6 copy.42
  167.1 0.7 copy.43
  167.8 0.3 copy-done.1
  168.1 0.7 copy.44
  (27 shorter events, 0.1 us)
Async XLA Ops:
  0.7 0.7 copy-start.5
  1.3 0.7 copy-start.6
  2.0 0.7 copy-start.7
  2.6 0.7 copy-start.8
  3.3 0.7 copy-start.9
  4.0 0.7 copy-start.10
  4.6 0.7 copy-start.11
  5.3 0.7 copy-start.12
  5.9 0.7 copy-start.13
  163.1 1.7 %copy-start = (bf16[256,512]{1,0:T(8,128)(2,1)S(1)}, bf16[256,512]{1,0:T(8,128)(2,1)}, u32[]{:S(2)}) copy-start(bf16[256,512]{1,0:T(8,128)(2,1)} %get-tuple-element.23) | copy-start | bytes 786436
  164.8 1.0 copy-start.3
  165.8 0.8 copy-start.4
  165.8 1.4 copy-start.2
  167.1 1.0 copy-start.1

commit v2 on v1

--- a/solution.py
+++ b/solution.py
@@ -60,13 +60,14 @@
 
 def body(
     Z, FK, R, D, NT,
-    tok_ref, cot_ref, wq_ref, wo_ref, wu_ref, wd_ref, sm_ref, len_ref, sup_ref,
+    tok_ref, cot_ref, wq_ref, wo_ref, wu_ref, wd_ref,
+    v0, v1, v2, v3, v4, v5, v6, v7, v8, len_ref, sup_ref,
     out_ref, gtok_ref, gqkv_ref, gout_ref, gup_ref, gdown_ref, gsm_ref,
     tokb, kb, vb, eb, stat, w0, w1, w2, g0, g1, g2,
     c0, c1, c2, x0, x1, x2, y0, y1, y2, z0, z1, z2,
     crf, yrf, zrf, par, upb, qt, dot_, qs, dos, ot, mrun, dqt,
     nrm2, hid, acc, gsec, xg, dwkv, lacc, upg, xown,
-    sg, src, srx, sry, srz,
+    sg, src, srx, sry, srz, tile,
     s_tz, s_ty, s_tc, r_t,
     s_wz, r_wz, s_wy, r_wy, s_wx, r_wx, s_wc, r_wc,
     s_gc, r_gc, s_gx, r_gx, s_gy, r_gy, s_gz, r_gz,
@@ -182,11 +183,14 @@
             t = wb[g].at[zz, yy, c, f]
             push(t, t, s_wx.at[g, ff, zz, yy], r_wx.at[g, f, zz, yy], d_f(ff))
 
-    def w_own(g):
+    def w_out_z(g):
         t = wb[g].at[z, y, c, f]
         for k in range(1, Z):
             zz = zplus(k)
             push(t, t, s_wz.at[g, zz], r_wz.at[g, z], d_z(zz))
+
+    def w_own(g):
+        t = wb[g].at[z, y, c, f]
         push(t, t, s_wy.at[g, z], r_wy.at[g, z], d_y)
         w_side(g, z, y)
 
@@ -223,15 +227,20 @@
 
     tokb[z, y, c] = tok_ref[...]
     w0[z, y, c, f, :, 0 : 3 * D] = wq_ref[...]
-    w0[z, y, c, f, :, 3 * D : 3 * D + 128] = sm_ref[...]
+    tile[...] = jnp.zeros((SLAB, 128), F32)
+    for r, v in enumerate((v0, v1, v2, v3, v4, v5, v6, v7, v8)):
+        tile[r : r + 1, 0 : v.shape[1]] = v[...].astype(F32)
+    w0[z, y, c, f, :, 3 * D : 3 * D + 128] = tile[...].astype(BF16)
     w1[z, y, c, f, :, 0:D] = wo_ref[...]
     w1[z, y, c, f, :, D : D + FF] = wu_ref[...]
     w2[z, y, c, f] = wd_ref[...]
 
-    w_own(0)
+    w_out_z(0)
     tok_right(z)
     tok_left(z)
     tok_side(z)
+    w_own(0)
+    w_out_z(1)
     w_own(1)
     w_own(2)
 
@@ -270,18 +279,14 @@
     for t in range(NT):
         onehot = jnp.where((row == t) & (qpos >= starts[t]) & (qpos < ends[t]), 1.0, onehot)
 
-    tok_z(1)
     w_z(0)
     tok_y(0)
-    for k in range(2, Z):
-        tok_z(k)
-        if k == 2:
-            w_y(0)
-            w_z(1)
-        tok_y(k - 1)
+    tok_z(1)
+    w_out_z(2)
+    w_y(0)
+    w_z(1)
     w_x(0)
-    tok_y(Z - 1)
-    w_z(2)
+    tok_y(1)
     w_c(0)
 
     piece = D // NSH
@@ -327,15 +332,34 @@
         ot[h] = jnp.zeros((2 * HD, R), F32)
         mrun[h] = jnp.full((1, R), MASKED, F32)
 
+    def near(s):
+        inner = jnp.minimum(z, Z - 1 - z)
+        odd = lax.rem(s, 2)
+        paired = z + (1 - 2 * odd) * ((s + 1) // 2)
+        rest = jnp.where(z < Z - 1 - z, s, Z - 1 - s)
+        return jnp.where(s <= 2 * inner, paired, rest)
+
     def place(n):
-        zz = zplus(n // 4)
+        zz = near(n // 4)
         part = lax.rem(n, 4)
         yy = lax.rem(y + part // 2, 2)
         cc = lax.rem(c + part, 2)
         return zz, yy, cc
 
+    arrivals = {2: [lambda: tok_z(2)], 4: [lambda: w_y(1)], 5: [lambda: w_z(2)], 8: [lambda: tok_y(2), lambda: w_x(1)]}
+    for k in range(3, Z):
+        arrivals.setdefault(4 * k - 3, []).append(lambda k=k: tok_z(k))
+        arrivals.setdefault(4 * k + 2, []).append(lambda k=k: tok_y(k))
+    arrivals.setdefault(12, []).append(lambda: w_y(2))
+
     def ahead(n, carry):
         zz, yy, cc = place(n)
+
+        for at in sorted(arrivals):
+            @pl.when(n == at)
+            def _():
+                for step in arrivals[at]:
+                    step()
 
         @pl.when(lax.rem(n, 2) == 1)
         def _():
@@ -365,9 +389,6 @@
 
     lax.fori_loop(0, 4 * Z, ahead, 0)
 
-    w_y(1)
-    w_y(2)
-    w_x(1)
     w_x(2)
     w_c(1)
     w_c(2)
@@ -758,6 +779,7 @@
         vm((FK, SLAB, D), F32),
         vm((SLAB, D), F32),
         vm((Z, SLAB, D), F32),
+        vm((SLAB, 128), F32),
         dma(2, Z), dma(Z), dma(Z, 2), dma(Z, 2, 2),
         dma(3, Z), dma(3, Z), dma(3, Z), dma(3, Z),
         dma(3, FK, Z, 2), dma(3, FK, Z, 2), dma(3, FK), dma(3, FK),
@@ -782,7 +804,7 @@
             shape((4 * SLAB, D), F32),
             shape((SLAB, D), F32),
         ),
-        in_specs=[vmem] * 7 + [smem] * 2,
+        in_specs=[vmem] * 15 + [smem] * 2,
         out_specs=[vmem] * 7,
         scratch_shapes=scratch,
         compiler_params=pltpu.CompilerParams(
@@ -790,6 +812,47 @@
         ),
         name="layer",
     )(*operands)
+
+
+def finish(NSH, FK, *refs):
+    big_in, small_in, big_out, small_out = refs[0:6], refs[6], refs[7:13], refs[13:22]
+    for a, b in zip(big_in, big_out):
+        b[...] = a[...]
+    at = lax.axis_index("blk") * FK
+    if FK > 1:
+        at = at + lax.axis_index("fsdp")
+    D = small_in.shape[1]
+    piece = D // NSH
+    lane = lax.broadcasted_iota(jnp.int32, (128, D), 1)
+    take = lax.broadcasted_iota(jnp.int32, (128, D), 0)
+    full = small_in[...]
+    for r in range(8):
+        chosen = jnp.where(lane == at * piece + take, full[r : r + 1, :], 0.0)
+        small_out[r][...] = jnp.sum(chosen, axis=1).reshape(1, 128)[:, 0:piece]
+    FF = D * 4
+    total = jnp.zeros((128,), F32)
+    for r in range(4):
+        chosen = jnp.where(lane + r * D == at * 4 * piece + take, full[8 + r : 9 + r, :], 0.0)
+        total = total + jnp.sum(chosen, axis=1)
+    small_out[8][...] = total.reshape(1, 128)[:, 0 : 4 * piece]
+
+
+def hand_over(NSH, FK, FF, results):
+    *big, small = results
+    D = small.shape[1]
+    vmem = pl.BlockSpec(memory_space=pltpu.VMEM)
+    shape = jax.ShapeDtypeStruct
+    return pl.pallas_call(
+        functools.partial(finish, NSH, FK),
+        out_shape=(
+            *[shape(v.shape, v.dtype) for v in big],
+            *[shape((1, D // NSH), F32) for _ in range(8)],
+            shape((1, FF // NSH), F32),
+        ),
+        in_specs=[vmem] * 7,
+        out_specs=[vmem] * 15,
+        name="finish",
+    )(*results)
 
 
 def shards(
@@ -809,18 +872,14 @@
         whole = lambda v: lax.all_gather(v, "fsdp", axis=0, tiled=True)
         smalls = tuple(whole(v) for v in smalls)
         weights = tuple(whole(v) for v in weights)
-    rows = [jnp.pad(v[None], ((0, 0), (0, 128 - v.shape[0]))) for v in smalls]
-    rows.append(jnp.zeros((SLAB - len(rows), 128), BF16))
-    small_tile = jnp.concatenate(rows, axis=0)
-    block_out, grad_tokens, g_qkv, g_out, g_up, g_down, g_small = layer(
+    results = layer(
         blocks // 4, FK, R, D, FF, NT,
-        (tokens[0], cotangent[0], *weights, small_tile, table_lengths, support_lengths),
+        (tokens[0], cotangent[0], *weights, *[v[None] for v in smalls], table_lengths, support_lengths),
     )
-    at = lax.axis_index("blk") * FK + (lax.axis_index("fsdp") if inside else 0)
-    piece = D // (blocks * FK)
-    cut = lax.dynamic_slice(g_small, (0, at * piece), (8, piece))
-    up_cut = lax.dynamic_slice(g_small[8 : 8 + FF // D].reshape(FF), (at * 4 * piece,), (4 * piece,))
-    small_grads = [cut[r] for r in range(8)] + [up_cut]
+    block_out, grad_tokens, g_qkv, g_out, g_up, g_down, *small_grads = hand_over(
+        blocks * FK, FK, FF, results
+    )
+    small_grads = [v[0] for v in small_grads]
     weight_grads = [g_qkv, g_out, g_up, g_down]
     if not inside:
         spread = lambda v: lax.psum_scatter(v, "fsdp", scatter_dimension=0, tiled=True)

time: 169 us -> 135 us (0.80)
  Pallas kernels: 153 us -> 134 us
  local copies, waits for them, and re-layouts: 15.4 us -> 0 us
    pallas_call x1, Pallas kernels: 153 us -> 132 us  [layer(): pl.pallas_call(functools.partial(body, Z, FK, R, D, NT), out_shape=(shape...]
    unnamed x36 -> x0, local copies, waits for them, and re-layouts: 12.3 us -> none
    pallas_call x0 -> x1, Pallas kernels: none -> 2.22 us  [hand_over(): pl.pallas_call(functools.partial(finish, NSH, FK), out_shape=(*[shape(v.s...]
where the time goes in v2:
time: 135 us
  Pallas kernels  134 us (99%)
    pallas_call x1, Pallas kernels, layer(): pl.pallas_call(functools.partial(body, Z, FK, R, D, NT), out_shape=(shape...  132 us

profile of v2, /device:TPU:0, one launch (start us, length us, event | category | flops | bytes accessed | tf_op | source)
XLA Modules:
  0.0 134.7 jit_solution(6646502500998978621)
XLA Ops:
  0.7 131.9 %layer.1 = (bf16[256,512]{1,0:T(8,128)(2,1)}, bf16[256,512]{1,0:T(8,128)(2,1)}, f32[16,1536]{1,0:T(8,128)}, f32[16,512]{1,0:T(8,128)}, f32[16,2048]{1,0:T(8,128)}, /*index=5*/f32[64,512]{1,0:T(8,128)}, f32[16,512]{1,0:T(8,128)}) custom-call(bf16[256,512]{1,0:T(8,128)(2,1)} %bitcast.22, bf16[256,512]{1,0:T(8,128)(2,1)} %bitcast.23, bf16[16,1536]{1,0:T(8,128)(2,1)} %wq_ref.1, ...), custom_call_target="tpu_custom_call" | custom-call | tf_op jit(solution)/shard_map/layer/pallas_call | solution.py:796
  132.5 2.2 %finish.1 = (bf16[256,512]{1,0:T(8,128)(2,1)}, bf16[256,512]{1,0:T(8,128)(2,1)}, f32[16,1536]{1,0:T(8,128)}, f32[16,512]{1,0:T(8,128)}, f32[16,2048]{1,0:T(8,128...) custom-call(bf16[256,512]{1,0:T(8,128)(2,1)} %get-tuple-element.37.r, ...), custom_call_target="tpu_custom_call" | custom-call | tf_op jit(solution)/shard_map/finish/pallas_call | solution.py:845

commit v3 on v2

v3 whole, which is shorter than its diff:
```python
import functools
import math

import jax
import jax.numpy as jnp
from jax import lax
from jax.experimental import pallas as pl
from jax.experimental.pallas import tpu as pltpu
from jax.sharding import PartitionSpec as P

H = 4
HD = 128
SLAB = 16
EPSILON = 1e-05
MASKED = -1e30
LN2 = math.log(2.0)
MESH = pl.DeviceIdType.MESH
F32 = jnp.float32
BF16 = jnp.bfloat16


def dot_nn(a, b):
    return lax.dot_general(a, b, (((1,), (0,)), ((), ())), preferred_element_type=F32)


def dot_nt(a, b):
    return lax.dot_general(a, b, (((1,), (1,)), ((), ())), preferred_element_type=F32)


def dot_tn(a, b):
    return lax.dot_general(a, b, (((0,), (0,)), ((), ())), preferred_element_type=F32)


def moments(v):
    mean = jnp.mean(v, axis=-1, keepdims=True)
    centered = v - mean
    rstd = lax.rsqrt(jnp.mean(centered * centered, axis=-1, keepdims=True) + EPSILON)
    return mean, centered, rstd


def norm_back(g, n, r):
    return r * (g - jnp.mean(g, axis=-1, keepdims=True) - n * jnp.mean(g * n, axis=-1, keepdims=True))


def three_terms(v):
    first = v.astype(BF16)
    rest = v - first.astype(F32)
    second = rest.astype(BF16)
    third = (rest - second.astype(F32)).astype(BF16)
    return first.astype(F32), second.astype(F32), third.astype(F32)


def col_sum(v):
    return jnp.sum(v, axis=0, keepdims=True)


def fold_rows(v):
    return jnp.sum(v.reshape(v.shape[0] // 8, 8, v.shape[1]), axis=0)


def body(
    Z, FK, R, D, NT,
    tok_ref, cot_ref, wq_ref, wo_ref, wu_ref, wd_ref,
    v0, v1, v2, v3, v4, v5, v6, v7, v8, len_ref, sup_ref,
    out_ref, gtok_ref, gqkv_ref, gout_ref, gup_ref, gdown_ref, gsm_ref,
    tokb, tokp, kb, vb, eb, stat, w0, w1, w2, gs, gu, gd,
    cs, cu, cd, xs, xu, xd, ys, yu, yd, zs, zu, zd,
    crf, zrf, par, upb, qt, dot_, qs, dos, ot, mrun, dqt,
    oh, ol, ml, ohr, olr, mlr, gqs, gqr,
    nrm2, hid, acc, gsec, dwkv, lacc, upg, xq,
    sg, src, srx, sry, srz, tile,
    s_tz, s_tc, r_t, s_tp, r_tp,
    s_wz, r_wz, s_wy, r_wy, s_wx, r_wx, s_wc, r_wc,
    s_gc, r_gc, s_gx, r_gx, s_gy, r_gy, s_gz, r_gz,
    s_pc, r_pc, s_pz, r_pz, s_y, r_y,
    s_sc, r_sc, s_sx, r_sx, s_sy, r_sy, s_sz, r_sz,
):
    i = lax.axis_index("blk")
    f = lax.axis_index("fsdp")
    c = lax.rem(i, 2)
    y = lax.rem(i // 2, 2)
    z = i // 4
    oc = 1 - c
    oy = 1 - y
    CH = 4 * FK * SLAB * 4
    FF = Z * CH
    NSH = Z * 4 * FK

    def dev(zz, yy, cc, ff):
        return ((zz * 2 + yy) * 2 + cc, ff)

    d_core = dev(z, y, oc, f)
    d_y = dev(z, oy, c, f)

    def zplus(k):
        return lax.rem(z + k, Z)

    def zxor(m):
        out, bit = z, 1
        while bit < Z:
            out = out + bit * ((m // bit) % 2) * (1 - 2 * lax.rem(z // bit, 2))
            bit *= 2
        return out

    def fplus(k):
        return lax.rem(f + k, FK)

    def d_z(zz):
        return dev(zz, y, c, f)

    def d_f(ff):
        return (i, ff)

    def cp(s, d, ss, rs, to):
        return pltpu.make_async_remote_copy(
            src_ref=s, dst_ref=d, send_sem=ss, recv_sem=rs, device_id=to, device_id_type=MESH
        )

    def push(s, d, ss, rs, to):
        cp(s, d, ss, rs, to).start()

    def got(d, rs):
        cp(d, d, rs, rs, d_core).wait_recv()

    def sent(s, ss):
        cp(s, s, ss, ss, d_core).wait_send()

    bar = pltpu.get_barrier_semaphore()
    partners = [d_core, d_y] + [d_z(zplus(k)) for k in range(1, Z)] + [d_f(fplus(k)) for k in range(1, FK)]
    for to in partners:
        pl.semaphore_signal(bar, inc=1, device_id=to, device_id_type=MESH)
    pl.semaphore_wait(bar, len(partners))

    def tok_push(zz, ss_z, to):
        t = tokb.at[zz, c]
        push(t, t, ss_z, r_t.at[zz, c], to)

    def tok_core(zz):
        t = tokb.at[zz, c]
        push(t, t, s_tc.at[zz], r_t.at[zz, c], d_core)

    def tok_right(zz):
        @pl.when(z < Z - 1)
        def _():
            tok_push(zz, s_tz.at[0, zz], d_z(z + 1))

    def tok_left(zz):
        @pl.when(z > 0)
        def _():
            tok_push(zz, s_tz.at[1, zz], d_z(z - 1))

    def tok_z(k):
        @pl.when(z - k >= 0)
        def _():
            zz = z - k
            got(tokb.at[zz, c], r_t.at[zz, c])
            tok_right(zz)
            tok_core(zz)

        @pl.when(z + k < Z)
        def _():
            zz = z + k
            got(tokb.at[zz, c], r_t.at[zz, c])
            tok_left(zz)
            tok_core(zz)

    wb = (w0, w1, w2)

    x_first = {2}

    def w_push_x(g, zz, yy):
        for k in range(1, FK):
            ff = fplus(k)
            t = wb[g].at[zz, yy, c, f]
            push(t, t, s_wx.at[g, ff, zz, yy], r_wx.at[g, f, zz, yy], d_f(ff))

    def w_push_y(g, zz, ff):
        t = wb[g].at[zz, y, c, ff]
        push(t, t, s_wy.at[g, zz, ff], r_wy.at[g, zz, ff], d_y)

    def w_out_z(g):
        t = wb[g].at[z, y, c, f]
        for k in range(1, Z):
            zz = zplus(k)
            push(t, t, s_wz.at[g, zz], r_wz.at[g, z], d_z(zz))

    def w_own_y(g):
        w_push_y(g, z, f)

    def w_own_x(g):
        w_push_x(g, z, y)

    def w_z(g):
        for k in range(1, Z):
            zz = zplus(k)
            got(wb[g].at[zz, y, c, f], r_wz.at[g, zz])
            w_push_x(g, zz, y)
            w_push_y(g, zz, f)

    def w_to_core(g, n):
        if g in x_first:
            t = wb[g].at[:, y if n == 0 else oy, c]
        else:
            t = wb[g].at[:, :, c, fplus(n)]
        push(t, t, s_wc.at[g, n], r_wc.at[g, n], d_core)

    def w_m(g):
        if g in x_first:
            for zz in range(Z):
                for k in range(1, FK):
                    ff = fplus(k)
                    got(wb[g].at[zz, y, c, ff], r_wx.at[g, ff, zz, y])
                    w_push_y(g, zz, ff)
        else:
            for zz in range(Z):
                got(wb[g].at[zz, oy, c, f], r_wy.at[g, zz, f])
                w_push_x(g, zz, oy)
        w_to_core(g, 0)

    def w_l(g):
        if g in x_first:
            for zz in range(Z):
                for ff in range(FK):
                    got(wb[g].at[zz, oy, c, ff], r_wy.at[g, zz, ff])
            w_to_core(g, 1)
        else:
            for k in range(1, FK):
                ff = fplus(k)
                for zz in range(Z):
                    for yy in range(2):
                        got(wb[g].at[zz, yy, c, ff], r_wx.at[g, ff, zz, yy])
                w_to_core(g, k)

    def w_parts(g):
        return 2 if g in x_first else FK

    def w_c(g):
        for n in range(w_parts(g)):
            if g in x_first:
                got(wb[g].at[:, y if n == 0 else oy, oc], r_wc.at[g, n])
            else:
                got(wb[g].at[:, :, oc, fplus(n)], r_wc.at[g, n])

    tokb[z, c] = tok_ref[...]
    w0[z, y, c, f, :, 0 : 3 * D] = wq_ref[...]
    tile[...] = jnp.zeros((SLAB, 128), F32)
    for r, v in enumerate((v0, v1, v2, v3, v4, v5, v6, v7, v8)):
        tile[r : r + 1, 0 : v.shape[1]] = v[...].astype(F32)
    w0[z, y, c, f, :, 3 * D : 3 * D + 128] = tile[...].astype(BF16)
    w1[z, y, c, f, :, 0:D] = wo_ref[...]
    w1[z, y, c, f, :, D : D + FF] = wu_ref[...]
    w2[z, y, c, f] = wd_ref[...]

    w_out_z(0)
    w_own_y(0)
    w_own_x(0)
    tok_right(z)
    tok_left(z)
    w_out_z(1)
    w_own_y(1)
    w_own_x(1)
    w_own_x(2)
    push(tokb.at[z, c], tokp, s_tp, r_tp, d_y)
    tok_core(z)
    w_own_y(2)

    starts, ends, stops = [], [], []
    total = jnp.int32(0)
    for t in range(NT):
        starts.append(total)
        stops.append(total + sup_ref[0, t])
        total = total + len_ref[0, t]
        ends.append(total)

    lane = lax.broadcasted_iota(jnp.int32, (1, 128), 1)
    lane_start = jnp.zeros((1, 128), jnp.int32)
    lane_stop = jnp.zeros((1, 128), jnp.int32)
    for t in range(NT):
        lane_start = jnp.where(lane == t, starts[t], lane_start)
        lane_stop = jnp.where(lane == t, stops[t], lane_stop)
    lane_ones = jnp.where((lane >= NT) & (lane < NT + 3), 1.0, 0.0)

    def mask_of(n):
        pos = (n * 2 + y) * 2 * R + lax.broadcasted_iota(jnp.int32, (2 * R, 128), 0)
        seen = (pos >= lane_start) & (pos < lane_stop)
        extra = jnp.where(lane < NT, jnp.where(seen, 0.0, MASKED), lane_ones)
        return extra.astype(BF16)

    def mask_block(n, carry):
        eb[n] = mask_of(n)
        return carry

    lax.fori_loop(0, Z, mask_block, 0)

    row = lax.broadcasted_iota(jnp.int32, (HD, 2 * R), 0)
    col = lax.broadcasted_iota(jnp.int32, (HD, 2 * R), 1)
    qpos = jnp.where(col < R, i * R + col, ((z * 2 + oy) * 2 + c - 1) * R + col)
    onehot = jnp.zeros((HD, 2 * R), F32)
    for t in range(NT):
        onehot = jnp.where((row == t) & (qpos >= starts[t]) & (qpos < ends[t]), 1.0, onehot)
    for h in range(H):
        qt[h, HD : 2 * HD, :] = onehot.astype(BF16)
        dot_[h, HD + SLAB : 2 * HD, :] = jnp.zeros((HD - SLAB, 2 * R), BF16)
        ot[h] = jnp.zeros((2 * HD, 2 * R), F32)
        mrun[h] = jnp.full((1, 2 * R), MASKED, F32)

    w_z(0)
    w_m(0)
    tok_z(1)
    w_out_z(2)
    w_l(0)
    w_z(1)
    w_c(0)

    piece = D // NSH
    small = w0[:, :, :, :, :, 3 * D : 3 * D + 128].reshape(NSH * SLAB, 128)
    spread = (
        lax.rem(lax.broadcasted_iota(jnp.int32, (128, D), 1), piece)
        == lax.broadcasted_iota(jnp.int32, (128, D), 0)
    )
    wide = dot_nn(small, spread.astype(BF16))
    mine = (
        lax.broadcasted_iota(jnp.int32, (NSH * SLAB, D), 1) // piece
        == lax.broadcasted_iota(jnp.int32, (NSH * SLAB, D), 0) // SLAB
    )
    wide = jnp.where(mine, wide, 0.0)
    par[...] = jnp.sum(wide.reshape(NSH, SLAB, D), axis=0)
    pick = (
        lax.broadcasted_iota(jnp.int32, (NSH, NSH * SLAB), 1)
        == lax.broadcasted_iota(jnp.int32, (NSH, NSH * SLAB), 0) * SLAB + 8
    )
    ups = dot_nn(pick.astype(BF16), small).astype(BF16)
    spread = (
        lax.rem(lax.broadcasted_iota(jnp.int32, (128, FF), 1), 4 * piece)
        == lax.broadcasted_iota(jnp.int32, (128, FF), 0)
    )
    wide = dot_nn(ups, spread.astype(BF16))
    mine = (
        lax.broadcasted_iota(jnp.int32, (NSH, FF), 1) // (4 * piece)
        == lax.broadcasted_iota(jnp.int32, (NSH, FF), 0)
    )
    upb[...] = col_sum(jnp.where(mine, wide, 0.0))
    ln1g, ln1b = par[0:1, :], par[1:2, :]

    got(tokp, r_tp)
    tokens = tok_ref[...].astype(F32)
    mean, centered, rstd = moments(tokens)
    xq[0:R, :] = (centered * rstd * ln1g + ln1b).astype(BF16)
    mean, centered, rstd = moments(tokp[...].astype(F32))
    xq[R : 2 * R, :] = (centered * rstd * ln1g + ln1b).astype(BF16)
    wq = w0[:, :, :, :, :, 0:D].reshape(D, D)
    qscale = HD ** (-0.5) / LN2
    qs[...] = ((dot_nn(xq[...], wq) + par[2:3, :]) * qscale).astype(BF16)
    for h in range(H):
        qt[h, 0:HD, :] = qs[:, h * HD : (h + 1) * HD].T

    def near(s):
        inner = jnp.minimum(z, Z - 1 - z)
        odd = lax.rem(s, 2)
        paired = z + (1 - 2 * odd) * ((s + 1) // 2)
        rest = jnp.where(z < Z - 1 - z, s, Z - 1 - s)
        return jnp.where(s <= 2 * inner, paired, rest)

    if Z == 4:
        arrivals = {
            1: [(tok_z, 2)],
            2: [(w_m, 1), (w_z, 2)],
            3: [(tok_z, 3)],
            4: [(w_m, 2)],
            6: [(w_l, 1)],
        }
    else:
        arrivals = {n: [(tok_z, n + 1)] for n in range(1, Z - 1)}
        arrivals[Z] = [(w_m, 1), (w_z, 2), (w_l, 1), (w_m, 2)]

    def run(table, n):
        for at in sorted(table):
            @pl.when(n == at)
            def _():
                for step, which in table[at]:
                    step(which)

    def attend(h, keys, values, extra, span):
        cols = slice(h * HD, (h + 1) * HD)
        s = dot_nn(jnp.concatenate([keys[:, cols], extra], axis=1), qt[h, :, span])
        top0 = mrun[h, :, span]
        top = jnp.maximum(top0, jnp.ceil(jnp.max(s, axis=0, keepdims=True)))
        e = jnp.exp2(s - top).astype(BF16)
        grown = dot_tn(jnp.concatenate([values[:, cols], extra], axis=1), e)
        ot[h, :, span] = ot[h, :, span] * jnp.exp2(top0 - top) + grown
        mrun[h, :, span] = top

    def ahead(n, carry):
        zz = near(n)
        run(arrivals, n)
        got(tokb.at[zz, oc], r_t.at[zz, oc])
        mean, centered, rstd = moments(tokb[zz].reshape(2 * R, D).astype(F32))
        stat[zz] = jnp.where(lax.broadcasted_iota(jnp.int32, (2 * R, 128), 1) == 0, mean, rstd)
        x = (centered * rstd * par[0:1, :] + par[1:2, :]).astype(BF16)
        kv = dot_nn(x, w0[:, :, :, :, :, D : 3 * D].reshape(D, 2 * D))
        keys = kv[:, 0:D].astype(BF16)
        values = (kv[:, D : 2 * D] + par[3:4, :]).astype(BF16)
        kb[zz] = keys
        vb[zz] = values
        extra = eb[zz]
        for h in range(H):
            attend(h, keys, values, extra, slice(R, 2 * R))
        return carry

    lax.fori_loop(0, Z, ahead, 0)

    for h in range(H):
        t = ot[h, 0:HD, R : 2 * R]
        first_part = t.astype(BF16)
        oh[h] = first_part
        ol[h] = (t - first_part.astype(F32)).astype(BF16)
        ml[h : h + 1, :] = mrun[h, :, R : 2 * R]
        ml[H + h : H + h + 1, :] = ot[h, HD + NT : HD + NT + 1, R : 2 * R]
    push(oh, ohr, s_y.at[0], r_y.at[0], d_y)
    push(ml, mlr, s_y.at[1], r_y.at[1], d_y)

    def ahead_own(n, carry):
        zz = near(n)
        run(arrivals, Z + n)
        for h in range(H):
            attend(h, kb[zz], vb[zz], eb[zz], slice(0, R))
        return carry

    lax.fori_loop(0, Z, ahead_own, 0)
    w_l(2)
    w_c(1)
    push(ol, olr, s_y.at[2], r_y.at[2], d_y)

    got(ohr, r_y.at[0])
    got(mlr, r_y.at[1])
    parts = []
    row_tail = lax.broadcasted_iota(jnp.int32, (SLAB, R), 0)
    for h in range(H):
        m_own, m_far = mrun[h, :, 0:R], mlr[h : h + 1, :]
        top = jnp.maximum(m_own, m_far)
        a_own, a_far = jnp.exp2(m_own - top), jnp.exp2(m_far - top)
        total = a_own * ot[h, HD + NT : HD + NT + 1, 0:R] + a_far * mlr[H + h : H + h + 1, :]
        inverse = 1.0 / total
        attended = ot[h, 0:HD, 0:R] * (a_own * inverse) + ohr[h].astype(F32) * (a_far * inverse)
        ot[h, 0:HD, 0:R] = attended
        ot[h, HD : HD + 1, 0:R] = inverse
        ot[h, HD + 1 : HD + 2, 0:R] = a_far * inverse
        parts.append(attended.T.astype(BF16))
        m1, m2, m3 = three_terms(top)
        tail = jnp.where(
            row_tail == NT, -m1,
            jnp.where(row_tail == NT + 1, -m2, jnp.where(row_tail == NT + 2, -m3, onehot[0:SLAB, 0:R])),
        )
        qt[h, HD : HD + SLAB, 0:R] = tail.astype(BF16)
    push(qt.at[:, HD : HD + SLAB, 0:R], qt.at[:, HD : HD + SLAB, R : 2 * R], s_y.at[3], r_y.at[3], d_y)
    attn_low = jnp.concatenate(parts, axis=1)
    w_out = w1[:, :, :, :, :, 0:D].reshape(D, D)
    hidden = tokens + (dot_nn(attn_low, w_out) + par[4:5, :])
    hid[...] = hidden
    mean2, centered, rstd2 = moments(hidden)
    n2 = centered * rstd2
    nrm2[...] = (n2 * par[5:6, :] + par[6:7, :]).astype(BF16)
    acc[...] = hidden + par[7:8, :]
    gsec[...] = jnp.zeros((R, D), F32)
    w_c(2)

    HF = FF // 2
    store = (gs, gs, gs, gs, gu, gu, gd, gd)
    from_core = (cs, cs, cs, cs, cu, cu, cd, cd)
    from_x = (xs, xs, xs, xs, xu, xu, xd, xd)
    from_y = (ys, ys, ys, ys, yu, yu, yd, yd)
    from_z = (zs, zs, zs, zs, zu, zu, zd, zd)
    lead = (0, 1, 2, 3, 0, 1, 0, 1)
    Q, K, V, O, UA, UB, DA, DB = range(8)
    y_first = {V, DB}
    straight = {Q, K, V}

    def r_c(g):
        n = lead[g]
        push(store[g].at[n, :, :, oc], from_core[g].at[n], s_gc.at[g], r_gc.at[g], d_core)

    def r_push_x(g, whole):
        n = lead[g]
        for k in range(1, FK):
            ff = fplus(k)
            if whole:
                push(store[g].at[n, :, :, c, ff], from_x[g].at[n, f], s_gx.at[g, ff], r_gx.at[g, f], d_f(ff))
            else:
                push(store[g].at[n, :, y, c, ff], from_x[g].at[n, f, :, 0], s_gx.at[g, ff], r_gx.at[g, f], d_f(ff))

    def r_push_y(g, whole):
        n = lead[g]
        if whole:
            push(store[g].at[n, :, oy, c], from_y[g].at[n], s_gy.at[g], r_gy.at[g], d_y)
        else:
            push(store[g].at[n, :, oy, c, f], from_y[g].at[n, :, 0], s_gy.at[g], r_gy.at[g], d_y)

    def over_z(one):
        def step(zz, carry):
            one(zz)
            return carry

        lax.fori_loop(0, Z, step, 0)

    def r_1(g):
        n = lead[g]
        got(from_core[g].at[n], r_gc.at[g])

        def one(zz):
            t = store[g][n, zz, :, c].astype(F32) + from_core[g][n, zz].astype(F32)
            store[g][n, zz, :, c] = t.astype(BF16)

        over_z(one)
        if g in y_first:
            r_push_y(g, True)
        else:
            r_push_x(g, True)

    def r_2(g):
        n = lead[g]
        if g in y_first:
            got(from_y[g].at[n], r_gy.at[g])

            def one(zz):
                t = store[g][n, zz, y, c].astype(F32) + from_y[g][n, zz].astype(F32)
                store[g][n, zz, y, c] = t.astype(BF16)

            over_z(one)
            r_push_x(g, False)
        else:
            for k in range(1, FK):
                got(from_x[g].at[n, fplus(k)], r_gx.at[g, fplus(k)])

            def one(zz):
                t = store[g][n, zz, :, c, f].astype(F32)
                for k in range(1, FK):
                    t = t + from_x[g][n, fplus(k), zz].astype(F32)
                store[g][n, zz, :, c, f] = t.astype(BF16)

            if FK > 1:
                over_z(one)
            r_push_y(g, False)

    def r_z(g):
        n = lead[g]
        if g in y_first:
            for k in range(1, FK):
                got(from_x[g].at[n, fplus(k), :, 0], r_gx.at[g, fplus(k)])

            def one(zz):
                t = store[g][n, zz, y, c, f].astype(F32)
                for k in range(1, FK):
                    t = t + from_x[g][n, fplus(k), zz, 0].astype(F32)
                store[g][n, zz, y, c, f] = t.astype(BF16)

            if FK > 1:
                over_z(one)
        else:
            got(from_y[g].at[n, :, 0], r_gy.at[g])

            def one(zz):
                t = store[g][n, zz, y, c, f].astype(F32) + from_y[g][n, zz, 0].astype(F32)
                store[g][n, zz, y, c, f] = t.astype(BF16)

            over_z(one)
        if g in straight:
            for k in range(1, Z):
                zz = zplus(k)
                push(store[g].at[n, zz, y, c, f], from_z[g].at[n, z], s_gz.at[g, zz], r_gz.at[g, z], d_z(zz))
        else:
            r_fold(g, 1)

    def r_fold(g, bit):
        n = lead[g]
        for m in range(bit, Z, 2 * bit):
            push(
                store[g].at[n, zxor(m), y, c, f], from_z[g].at[n, zxor(bit ^ (m - 1))],
                s_gz.at[g, zxor(m)], r_gz.at[g, zxor(bit ^ (m - 1))], d_z(zxor(bit)),
            )

    def r_zz(g):
        n = lead[g]
        bit = 1
        while 2 * bit < Z:
            for m in range(0, Z, 2 * bit):
                zz, at = zxor(m), zxor(m + bit - 1)
                got(from_z[g].at[n, at], r_gz.at[g, at])
                t = store[g][n, zz, y, c, f].astype(F32) + from_z[g][n, at].astype(F32)
                store[g][n, zz, y, c, f] = t.astype(BF16)
            bit *= 2
            r_fold(g, bit)

    def r_end(g):
        n = lead[g]
        t = store[g][n, z, y, c, f].astype(F32)
        if g in straight:
            for k in range(1, Z):
                zz = zplus(k)
                got(from_z[g].at[n, zz], r_gz.at[g, zz])
                t = t + from_z[g][n, zz].astype(F32)
        else:
            at = zxor(Z // 2 - 1)
            got(from_z[g].at[n, at], r_gz.at[g, at])
            t = t + from_z[g][n, at].astype(F32)
        if g <= V:
            gqkv_ref[:, g * D : (g + 1) * D] = t
        elif g == O:
            gout_ref[...] = t
        elif g <= UB:
            gup_ref[:, (g - UA) * HF : (g - UA + 1) * HF] = t
        else:
            gdown_ref[(g - DA) * 2 * SLAB : (g - DA + 1) * 2 * SLAB, :] = t

    def r_sent(g):
        n = lead[g]
        sent(store[g].at[n, :, :, oc], s_gc.at[g])
        for k in range(1, FK):
            ff = fplus(k)
            if g in y_first:
                sent(store[g].at[n, :, y, c, ff], s_gx.at[g, ff])
            else:
                sent(store[g].at[n, :, :, c, ff], s_gx.at[g, ff])
        if g in y_first:
            sent(store[g].at[n, :, oy, c], s_gy.at[g])
        else:
            sent(store[g].at[n, :, oy, c, f], s_gy.at[g])
        for k in range(1, Z):
            sent(store[g].at[n, zplus(k), y, c, f], s_gz.at[g, zplus(k)])

    def half(hh):
        def chunk(j, carry):
            cols = pl.ds(pl.multiple_of(D + j * CH, 128), CH)
            bcols = pl.ds(pl.multiple_of(j * CH, 128), CH)
            hcols = pl.ds(pl.multiple_of((j - hh * (Z // 2)) * CH, 128), CH)
            up = w1[:, :, :, :, :, cols].reshape(D, CH)
            down = w2[j].reshape(CH, D)
            normed = nrm2[...]
            cot = cot_ref[...]
            pre = dot_nn(normed, up) + upb[:, bcols]
            phi = 0.5 * (1.0 + lax.erf(pre * (0.5**0.5)))
            act = (pre * phi).astype(BF16)
            slope = phi + pre * (jnp.exp2(pre * pre * (-0.5 / LN2)) * ((2.0 * math.pi) ** -0.5))
            acc[...] += dot_nn(act, down)
            gpre32 = dot_nt(cot, down) * slope
            gpre = gpre32.astype(BF16)
            gsec[...] += dot_nt(gpre, up)
            upg[:, bcols] = col_sum(gpre.astype(F32))
            gu[hh, :, :, :, :, :, hcols] = dot_tn(normed, gpre).astype(BF16).reshape(Z, 2, 2, FK, SLAB, CH)
            g_down = dot_tn(act, cot).astype(BF16).reshape(2, 2, FK, 4 * SLAB, D)
            gd[0, j] = g_down[:, :, :, 0 : 2 * SLAB]
            gd[1, j] = g_down[:, :, :, 2 * SLAB : 4 * SLAB]
            return carry

        lax.fori_loop(hh * (Z // 2), (hh + 1) * (Z // 2), chunk, 0)

    half(0)
    r_c(UA)
    half(1)
    r_1(UA)
    out_ref[...] = acc[...].astype(BF16)

    g_second = gsec[...]
    n2 = (hid[...] - mean2) * rstd2
    ln2g = par[5:6, :]
    cot32 = cot_ref[...].astype(F32)
    grad_hidden = cot32 + norm_back(g_second * ln2g, n2, rstd2)
    hid[...] = grad_hidden
    g_branch = grad_hidden.astype(BF16)
    gs[O] = dot_tn(attn_low, g_branch).astype(BF16).reshape(Z, 2, 2, FK, SLAB, D)
    r_c(UB)
    r_c(DA)
    r_c(DB)
    r_c(O)
    zero = jnp.zeros((1, D), F32)
    for r in range(SLAB):
        sg[0, r : r + 1, :] = zero
    sg[0, 4:5, :] = col_sum(g_branch.astype(F32))
    sg[0, 5:6, :] = col_sum(g_second * n2)
    sg[0, 6:7, :] = col_sum(g_second)
    sg[0, 7:8, :] = col_sum(cot32)
    for r in range(FF // D):
        sg[0, 8 + r : 9 + r, :] = upg[:, r * D : (r + 1) * D]

    got(olr, r_y.at[2])
    for h in range(H):
        rows = slice(h * HD, (h + 1) * HD)
        w_head = w1[:, :, :, :, :, 0:D].reshape(D, D)[rows, :]
        ga = dot_nt(w_head, g_branch).astype(BF16).astype(F32)
        low = (ga * ot[h, HD : HD + 1, 0:R]).astype(BF16)
        exact = ot[h, 0:HD, 0:R] + olr[h].astype(F32) * ot[h, HD + 1 : HD + 2, 0:R]
        delta = col_sum(low.astype(F32) * exact)
        d1, d2, d3 = three_terms(delta)
        tail = jnp.where(
            row_tail == NT, -d1, jnp.where(row_tail == NT + 1, -d2, jnp.where(row_tail == NT + 2, -d3, 0.0))
        )
        dot_[h, 0:HD, 0:R] = low
        dot_[h, HD : HD + SLAB, 0:R] = tail.astype(BF16)
        dos[0:R, rows] = low.T
    push(dot_.at[:, 0 : HD + SLAB, 0:R], dot_.at[:, 0 : HD + SLAB, R : 2 * R], s_y.at[4], r_y.at[4], d_y)
    dqt[...] = jnp.zeros((H, HD, 2 * R), F32)
    dwkv[...] = jnp.zeros((D, 2 * D), F32)
    lacc[...] = jnp.zeros((3, 8, D), F32)

    def tok_sent():
        @pl.when(z < Z - 1)
        def _():
            for k in range(Z):
                @pl.when(z - k >= 0)
                def _():
                    sent(tokb.at[z - k, c], s_tz.at[0, z - k])

        @pl.when(z > 0)
        def _():
            for k in range(Z):
                @pl.when(z + k < Z)
                def _():
                    sent(tokb.at[z + k, c], s_tz.at[1, z + k])

        for zz in range(Z):
            sent(tokb.at[zz, c], s_tc.at[zz])
        sent(tokb.at[z, c], s_tp)

    tok_sent()
    r_1(UB)
    r_1(DA)
    r_1(DB)

    got(qt.at[:, HD : HD + SLAB, R : 2 * R], r_y.at[3])
    got(dot_.at[:, 0 : HD + SLAB, R : 2 * R], r_y.at[4])
    for h in range(H):
        dos[R : 2 * R, h * HD : (h + 1) * HD] = dot_[h, 0:HD, R : 2 * R].T

    turns = sorted(range(1, Z), key=lambda m: (m & -m, m)) + [0]

    def plane(n):
        m = jnp.int32(0)
        for k in range(Z - 1):
            m = jnp.where(n == k, turns[k], m)
        return zxor(m)

    def p_sum(m):
        zz = zxor(m)
        got(crf.at[zz], r_pc.at[zz])
        t = tokb[zz, c].astype(F32) + crf[zz].astype(F32)
        bit = 1
        while bit < Z and m % (2 * bit) == 0:
            at = zxor(m + bit - 1)
            got(zrf.at[at], r_pz.at[at])
            t = t + zrf[at].astype(F32)
            bit *= 2
        return t

    def p_z(s):
        m = turns[s]
        bit = m & -m
        zz, at = zxor(m), zxor(bit ^ (m - 1))
        tokb[zz, c] = p_sum(m).astype(BF16)
        push(tokb.at[zz, c], zrf.at[at], s_pz.at[zz], r_pz.at[at], d_z(zxor(bit)))

    if Z == 4:
        before = {
            1: [(r_1, O), (r_2, UA)],
            2: [(r_2, DB), (r_2, UB)],
            3: [(r_2, DA), (r_z, UA)],
        }
        between = {
            1: [(p_z, 0)],
            2: [(p_z, 1)],
            3: [(p_z, 2), (r_z, UB)],
        }
        late = [
            (r_c, K), (r_c, V), "queries", (r_c, Q), (r_z, DB), "sums", (r_1, V), (r_1, K), "gq", (r_z, DA), (r_2, O),
            "core", (r_1, Q), (r_zz, UA), "x", (r_2, K), (r_2, V), (r_z, O), (r_zz, UB), (r_2, Q), "y", (r_zz, DB),
            (r_z, K), (r_z, V), (r_zz, DA), (r_z, Q), (r_zz, O), "first",
            (r_end, UA), (r_end, UB), (r_end, DA), (r_end, DB), (r_end, O), (r_end, K), (r_end, V), (r_end, Q), "z",
        ]
    else:
        before = {1: [(r_1, O)]}
        between = {s + 1: [(p_z, s)] for s in range(Z - 1)}
        before[Z - 1] = [(r_2, UA), (r_2, UB), (r_2, DA), (r_2, DB), (r_2, O)]
        late = [(r_z, g) for g in (O, UA, UB, DA, DB)]
        late += ["queries", "sums", "gq", (r_c, Q), (r_c, K), (r_c, V), "core"]
        late += [(r_1, Q), (r_1, K), (r_1, V), "x", (r_2, Q), (r_2, K), (r_2, V), "y", (r_z, Q), (r_z, K), (r_z, V)]
        late += [(r_zz, g) for g in (O, UA, UB, DA, DB)] + ["first", "z"] + [(r_end, g) for g in range(8)]

    def behind(n, carry):
        zz = plane(n)
        run(before, n)
        keys, values, extra = kb[zz], vb[zz], eb[zz]
        dks, dvs = [], []
        for h in range(H):
            cols = slice(h * HD, (h + 1) * HD)
            s = dot_nn(jnp.concatenate([keys[:, cols], extra], axis=1), qt[h])
            dp = dot_nn(jnp.concatenate([values[:, cols], extra], axis=1), dot_[h])
            e = jnp.exp2(s).astype(BF16)
            ds = (e.astype(F32) * dp).astype(BF16)
            dvs.append(dot_nn(e, dos[:, cols]))
            dks.append(dot_nn(ds, qs[:, cols]) * LN2)
            dqt[h] += dot_tn(keys[:, cols], ds)
        dv = jnp.concatenate(dvs, axis=1)
        dkv = jnp.concatenate(dks + [dv], axis=1).astype(BF16)
        run(between, n)
        gp = dot_nt(dkv, w0[:, :, :, :, :, D : 3 * D].reshape(D, 2 * D))
        norm = (tokb[zz].reshape(2 * R, D).astype(F32) - stat[zz, :, 0:1]) * stat[zz, :, 1:2]
        tokb[zz] = gp.astype(BF16).reshape(2, R, D)
        push(tokb.at[zz, oc], crf.at[zz], s_pc.at[zz], r_pc.at[zz], d_core)
        x = (norm * par[0:1, :] + par[1:2, :]).astype(BF16)
        lacc[0] += fold_rows(gp * norm)
        lacc[1] += fold_rows(gp)
        lacc[2] += fold_rows(dv)
        dwkv[...] += dot_tn(x, dkv)
        return carry

    lax.fori_loop(0, Z, behind, 0)

    gs[K] = dwkv[:, 0:D].astype(BF16).reshape(Z, 2, 2, FK, SLAB, D)
    gs[V] = dwkv[:, D : 2 * D].astype(BF16).reshape(Z, 2, 2, FK, SLAB, D)

    def queries():
        dq = jnp.concatenate([(dqt[h] * (HD**-0.5)).T for h in range(H)], axis=1).astype(BF16)
        gs[Q] = dot_tn(xq[...], dq).astype(BF16).reshape(Z, 2, 2, FK, SLAB, D)
        gq = dot_nt(dq, w0[:, :, :, :, :, 0:D].reshape(D, D))
        acc[...] = gq[0:R]
        gqs[...] = gq[R : 2 * R].astype(BF16)
        both = jnp.concatenate([tok_ref[...], tokp[...]], axis=0).astype(F32)
        mean, centered, rstd = moments(both)
        sg[0, 0:1, :] = col_sum(lacc[0]) + col_sum(gq * (centered * rstd))
        sg[0, 1:2, :] = col_sum(lacc[1]) + col_sum(gq)
        sg[0, 2:3, :] = col_sum(dq.astype(F32))
        sg[0, 3:4, :] = col_sum(lacc[2])

    def queries_back():
        push(gqs, gqr, s_y.at[5], r_y.at[5], d_y)

    def sums():
        push(sg.at[0], src, s_sc, r_sc, d_core)

    def sums_core():
        got(src, r_sc)
        sg[1] = sg[0] + src[...]
        for k in range(1, FK):
            ff = fplus(k)
            push(sg.at[1], srx.at[f], s_sx.at[ff], r_sx.at[f], d_f(ff))

    def sums_x():
        t = sg[1]
        for k in range(1, FK):
            got(srx.at[fplus(k)], r_sx.at[fplus(k)])
            t = t + srx[fplus(k)]
        sg[2] = t
        push(sg.at[2], sry, s_sy, r_sy, d_y)

    def sums_y():
        got(sry, r_sy)
        sg[3] = sg[2] + sry[...]
        for k in range(1, Z):
            zz = zplus(k)
            push(sg.at[3], srz.at[z], s_sz.at[zz], r_sz.at[z], d_z(zz))

    def sums_z():
        t = sg[3]
        for k in range(1, Z):
            zz = zplus(k)
            got(srz.at[zz], r_sz.at[zz])
            t = t + srz[zz]
        gsm_ref[...] = t

    def first():
        got(gqr, r_y.at[5])
        t = p_sum(0) + acc[...] + gqr[...].astype(F32)
        mean, centered, rstd = moments(tok_ref[...].astype(F32))
        gtok_ref[...] = (hid[...] + norm_back(t * par[0:1, :], centered * rstd, rstd)).astype(BF16)

    named = {
        "queries": queries, "gq": queries_back, "sums": sums, "core": sums_core, "x": sums_x, "y": sums_y, "z": sums_z, "first": first,
    }
    for step in late:
        if isinstance(step, str):
            named[step]()
        else:
            step[0](step[1])

    for g in range(3):
        for k in range(1, Z):
            sent(wb[g].at[z, y, c, f], s_wz.at[g, zplus(k)])
        for zz in range(Z):
            sent(wb[g].at[zz, y, c, f], s_wy.at[g, zz, f])
            for k in range(1, FK):
                ff = fplus(k)
                sent(wb[g].at[zz, y, c, f], s_wx.at[g, ff, zz, y])
                if g in x_first:
                    sent(wb[g].at[zz, y, c, ff], s_wy.at[g, zz, ff])
                else:
                    sent(wb[g].at[zz, oy, c, f], s_wx.at[g, ff, zz, oy])
        for n in range(w_parts(g)):
            if g in x_first:
                sent(wb[g].at[:, y if n == 0 else oy, c], s_wc.at[g, n])
            else:
                sent(wb[g].at[:, :, c, fplus(n)], s_wc.at[g, n])
    for g in range(8):
        r_sent(g)
    for zz in range(Z):
        sent(tokb.at[zz, oc], s_pc.at[zz])
    for k in range(1, Z):
        sent(tokb.at[zplus(k), c], s_pz.at[zplus(k)])
        sent(sg.at[3], s_sz.at[zplus(k)])
    sent(oh, s_y.at[0])
    sent(ml, s_y.at[1])
    sent(ol, s_y.at[2])
    sent(qt.at[:, HD : HD + SLAB, 0:R], s_y.at[3])
    sent(dot_.at[:, 0 : HD + SLAB, 0:R], s_y.at[4])
    sent(gqs, s_y.at[5])
    sent(sg.at[0], s_sc)
    for k in range(1, FK):
        sent(sg.at[1], s_sx.at[fplus(k)])
    sent(sg.at[2], s_sy)


def layer(Z, FK, R, D, FF, NT, operands):
    vm = lambda shape, dtype: pltpu.VMEM(shape, dtype)
    dma = lambda *shape: pltpu.SemaphoreType.DMA(shape)
    lead = (Z, 2, 2, FK)
    slabs = ((SLAB, 3 * D + 128), (SLAB, D + FF), (4 * SLAB, D))
    gslabs = ((4, SLAB, D), (2, SLAB, FF // 2), (2, 2 * SLAB, D))
    scratch = [
        vm((Z, 2, R, D), BF16),
        vm((R, D), BF16),
        vm((Z, 2 * R, D), BF16),
        vm((Z, 2 * R, D), BF16),
        vm((Z, 2 * R, 128), BF16),
        vm((Z, 2 * R, 128), F32),
        *[vm(lead + s, BF16) for s in slabs],
        *[vm((s[0],) + lead + s[1:], BF16) for s in gslabs],
        *[vm((s[0], Z, 2, FK) + s[1:], BF16) for s in gslabs],
        *[vm((s[0], FK, Z, 2) + s[1:] if FK > 1 else (SLAB, 128), BF16) for s in gslabs],
        *[vm((s[0], Z, FK) + s[1:], BF16) for s in gslabs],
        *[vm((s[0], Z) + s[1:], BF16) for s in gslabs],
        vm((Z, R, D), BF16),
        vm((Z, R, D), BF16),
        vm((SLAB, D), F32),
        vm((1, FF), F32),
        vm((H, 2 * HD, 2 * R), BF16),
        vm((H, 2 * HD, 2 * R), BF16),
        vm((2 * R, D), BF16),
        vm((2 * R, D), BF16),
        vm((H, 2 * HD, 2 * R), F32),
        vm((H, 1, 2 * R), F32),
        vm((H, HD, 2 * R), F32),
        vm((H, HD, R), BF16),
        vm((H, HD, R), BF16),
        vm((2 * H, R), F32),
        vm((H, HD, R), BF16),
        vm((H, HD, R), BF16),
        vm((2 * H, R), F32),
        vm((R, D), BF16),
        vm((R, D), BF16),
        vm((R, D), BF16),
        vm((R, D), F32),
        vm((R, D), F32),
        vm((R, D), F32),
        vm((D, 2 * D), F32),
        vm((3, 8, D), F32),
        vm((1, FF), F32),
        vm((2 * R, D), BF16),
        vm((4, SLAB, D), F32),
        vm((SLAB, D), F32),
        vm((FK, SLAB, D), F32),
        vm((SLAB, D), F32),
        vm((Z, SLAB, D), F32),
        vm((SLAB, 128), F32),
        dma(2, Z), dma(Z), dma(Z, 2), pltpu.SemaphoreType.DMA, pltpu.SemaphoreType.DMA,
        dma(3, Z), dma(3, Z), dma(3, Z, FK), dma(3, Z, FK),
        dma(3, FK, Z, 2), dma(3, FK, Z, 2), dma(3, 2), dma(3, 2),
        dma(8), dma(8), dma(8, FK), dma(8, FK), dma(8), dma(8), dma(8, Z), dma(8, Z),
        dma(Z), dma(Z), dma(Z), dma(Z), dma(6), dma(6),
        pltpu.SemaphoreType.DMA, pltpu.SemaphoreType.DMA,
        dma(FK), dma(FK),
        pltpu.SemaphoreType.DMA, pltpu.SemaphoreType.DMA,
        dma(Z), dma(Z),
    ]
    vmem = pl.BlockSpec(memory_space=pltpu.VMEM)
    smem = pl.BlockSpec(memory_space=pltpu.SMEM)
    shape = jax.ShapeDtypeStruct
    return pl.pallas_call(
        functools.partial(body, Z, FK, R, D, NT),
        out_shape=(
            shape((R, D), BF16),
            shape((R, D), BF16),
            shape((SLAB, 3 * D), F32),
            shape((SLAB, D), F32),
            shape((SLAB, FF), F32),
            shape((4 * SLAB, D), F32),
            shape((SLAB, D), F32),
        ),
        in_specs=[vmem] * 15 + [smem] * 2,
        out_specs=[vmem] * 7,
        scratch_shapes=scratch,
        compiler_params=pltpu.CompilerParams(
            collective_id=0, has_side_effects=True, vmem_limit_bytes=63 * 2**20
        ),
        name="layer",
    )(*operands)


def finish(NSH, FK, *refs):
    big_in, small_in, big_out, small_out = refs[0:6], refs[6], refs[7:13], refs[13:22]
    for a, b in zip(big_in, big_out):
        b[...] = a[...]
    at = lax.axis_index("blk") * FK
    if FK > 1:
        at = at + lax.axis_index("fsdp")
    D = small_in.shape[1]
    piece = D // NSH
    lane = lax.broadcasted_iota(jnp.int32, (128, D), 1)
    take = lax.broadcasted_iota(jnp.int32, (128, D), 0)
    full = small_in[...]
    for r in range(8):
        chosen = jnp.where(lane == at * piece + take, full[r : r + 1, :], 0.0)
        small_out[r][...] = jnp.sum(chosen, axis=1).reshape(1, 128)[:, 0:piece]
    FF = D * 4
    total = jnp.zeros((128,), F32)
    for r in range(4):
        chosen = jnp.where(lane + r * D == at * 4 * piece + take, full[8 + r : 9 + r, :], 0.0)
        total = total + jnp.sum(chosen, axis=1)
    small_out[8][...] = total.reshape(1, 128)[:, 0 : 4 * piece]


def hand_over(NSH, FK, FF, results):
    *big, small = results
    D = small.shape[1]
    vmem = pl.BlockSpec(memory_space=pltpu.VMEM)
    shape = jax.ShapeDtypeStruct
    return pl.pallas_call(
        functools.partial(finish, NSH, FK),
        out_shape=(
            *[shape(v.shape, v.dtype) for v in big],
            *[shape((1, D // NSH), F32) for _ in range(8)],
            shape((1, FF // NSH), F32),
        ),
        in_specs=[vmem] * 7,
        out_specs=[vmem] * 15,
        name="finish",
    )(*results)


def shards(
    blocks, fsdp,
    tokens, ln1_gain, ln1_bias, qkv_weight, query_bias, value_bias, out_weight, out_bias,
    ln2_gain, ln2_bias, up_weight, up_bias, down_weight, down_bias,
    table_lengths, support_lengths, cotangent,
):
    R, D = tokens.shape[1:]
    FF = up_weight.shape[1]
    NT = table_lengths.shape[1]
    smalls = (ln1_gain, ln1_bias, query_bias, value_bias, out_bias, ln2_gain, ln2_bias, down_bias, up_bias)
    weights = (qkv_weight, out_weight, up_weight, down_weight)
    inside = qkv_weight.shape[0] == SLAB
    FK = fsdp if inside else 1
    if not inside:
        whole = lambda v: lax.all_gather(v, "fsdp", axis=0, tiled=True)
        smalls = tuple(whole(v) for v in smalls)
        weights = tuple(whole(v) for v in weights)
    results = layer(
        blocks // 4, FK, R, D, FF, NT,
        (tokens[0], cotangent[0], *weights, *[v[None] for v in smalls], table_lengths, support_lengths),
    )
    block_out, grad_tokens, g_qkv, g_out, g_up, g_down, *small_grads = hand_over(
        blocks * FK, FK, FF, results
    )
    small_grads = [v[0] for v in small_grads]
    weight_grads = [g_qkv, g_out, g_up, g_down]
    if not inside:
        spread = lambda v: lax.psum_scatter(v, "fsdp", scatter_dimension=0, tiled=True)
        small_grads = [spread(v) for v in small_grads]
        weight_grads = [spread(v) for v in weight_grads]
    g_ln1g, g_ln1b, g_qb, g_vb, g_ob, g_ln2g, g_ln2b, g_db, g_ub = small_grads
    g_qkv, g_out, g_up, g_down = weight_grads
    return (
        block_out[None], grad_tokens[None], g_ln1g, g_ln1b, g_qkv, g_qb, g_vb, g_out, g_ob,
        g_ln2g, g_ln2b, g_up, g_ub, g_down, g_db,
    )


def solution(mesh):
    both = ("blk", "fsdp")
    vec, mat, rows = P(both), P(both, None), P("fsdp", "blk", None)
    return jax.shard_map(
        functools.partial(shards, mesh.shape["blk"], mesh.shape["fsdp"]),
        mesh=mesh,
        in_specs=(
            rows, vec, vec, mat, vec, vec, mat, vec, vec, vec, mat, vec, mat, vec,
            P("fsdp", None), P("fsdp", None), rows,
        ),
        out_specs=(rows, rows, vec, vec, mat, vec, vec, mat, vec, vec, vec, mat, vec, mat, vec),
        check_vma=False,
    )
```

time: 135 us -> 129 us (0.956)
  Pallas kernels: 134 us -> 128 us
    pallas_call x1, Pallas kernels: 132 us -> 126 us  [layer(): pl.pallas_call(functools.partial(body, Z, FK, R, D, NT), out_shape=(shape...]
where the time goes in v3:
time: 129 us
  Pallas kernels  128 us (99%)
    pallas_call x1, Pallas kernels, layer(): pl.pallas_call(functools.partial(body, Z, FK, R, D, NT), out_shape=(shape...  126 us

profile of v3, /device:TPU:0, one launch (start us, length us, event | category | flops | bytes accessed | tf_op | source)
XLA Modules:
  0.0 129.1 jit_solution(17477794971585915592)
XLA Ops:
  0.7 126.0 %layer.1 = (bf16[256,512]{1,0:T(8,128)(2,1)}, bf16[256,512]{1,0:T(8,128)(2,1)}, f32[16,1536]{1,0:T(8,128)}, f32[16,512]{1,0:T(8,128)}, f32[16,2048]{1,0:T(8,128)}, /*index=5*/f32[64,512]{1,0:T(8,128)}, f32[16,512]{1,0:T(8,128)}) custom-call(bf16[256,512]{1,0:T(8,128)(2,1)} %bitcast.22, bf16[256,512]{1,0:T(8,128)(2,1)} %bitcast.23, bf16[16,1536]{1,0:T(8,128)(2,1)} %wq_ref.1, ...), custom_call_target="tpu_custom_call" | custom-call | tf_op jit(solution)/shard_map/layer/pallas_call | solution.py:984
  126.7 2.2 %finish.1 = (bf16[256,512]{1,0:T(8,128)(2,1)}, bf16[256,512]{1,0:T(8,128)(2,1)}, f32[16,1536]{1,0:T(8,128)}, f32[16,512]{1,0:T(8,128)}, f32[16,2048]{1,0:T(8,128...) custom-call(bf16[256,512]{1,0:T(8,128)(2,1)} %get-tuple-element.37.r, ...), custom_call_target="tpu_custom_call" | custom-call | tf_op jit(solution)/shard_map/finish/pallas_call | solution.py:1033

commit v4 on v3

--- a/solution.py
+++ b/solution.py
@@ -58,9 +58,79 @@
     return jnp.sum(v.reshape(v.shape[0] // 8, 8, v.shape[1]), axis=0)
 
 
+FOUR = {
+    "masks": [("w_out_z", 0), ("tr",), ("tl",), ("w_own_x", 2), ("tp",), ("w_own_x", 0), ("w_own_y", 2)],
+    "small": [
+        ("gtokp",), ("w_out_z", 1), ("w_own_y", 0), ("w_z", 0), ("w_out_z", 2), ("w_m", 0), ("w_own_x", 1), ("tc",),
+        ("w_z", 1), ("w_l", 0), ("w_c", 0), ("tok_z", 1),
+    ],
+    ("A", 0): [("w_z", 2)],
+    ("A", 2): [("w_m", 1), ("tok_z", 2)],
+    ("A", 3): [("w_own_y", 1), ("w_m", 2), ("tok_z", 3)],
+    ("B", 0): [("o_hi",)],
+    ("B", 1): [("w_l", 1)],
+    ("B", 3): [("w_l", 2), ("o_lo",)],
+    "merge": [("g_o",)],
+    "out": [("qtail",), ("w_c", 1)],
+    "ffn": [("w_c", 2)],
+    "dOc": [("g_ol",)],
+    "dwu": [("dO",)],
+    "dwo": [("r_c", "db")],
+    "sent": [("r_c", "da")],
+    ("e", 1): [("r_1", "db"), ("r_c", "ub"), ("r_1", "da")],
+    "dosT": [("r_c", "ua"), ("g_dO",)],
+    ("t", 0): [("r_2", "da")],
+    ("t", 1): [("r_2", "db"), ("r_z", "db")],
+    ("h", 2): [("r_1", "ua"), ("r_c", "o"), ("p_z", 1)],
+    ("t", 2): [("r_1", "o"), ("r_2", "ua"), ("p_z", 0), ("r_1", "ub")],
+    ("h", 3): [("r_z", "da")],
+    "q": [("r_2", "ub"), ("r_2", "o"), ("r_c", "k"), ("r_z", "ua"), ("r_c", "v")],
+    "end": [
+        ("p_z", 2), ("s", 0), ("r_zz", "db"), ("r_c", "q"), ("r_1", "k"), ("s", 1), ("r_1", "v"), ("r_end", "db"),
+        ("r_1", "q"), ("r_2", "v"), ("r_2", "q"), ("r_zz", "ua"), ("s", 2), ("r_zz", "da"), ("gq",), ("r_end", "ua"),
+        ("r_z", "ub"), ("r_2", "k"), ("r_z", "k"), ("r_z", "v"), ("r_z", "o"), ("r_zz", "k"), ("r_z", "q"), ("s", 3),
+        ("r_zz", "ub"), ("r_end", "da"), ("r_zz", "q"), ("r_zz", "o"), ("r_end", "k"), ("r_zz", "v"), ("first",),
+        ("r_end", "q"), ("r_end", "v"), ("r_end", "ub"), ("s_end",), ("r_end", "o"),
+    ],
+}
+X_FIRST = {0, 1}
+Y_FIRST = {0, 3, 6, 7}
+DIRECT = {0, 1, 2, 3, 4, 5, 6, 7}
+STRAIGHT = {1, 2, 4, 7}
+
+
+def order_of(Z):
+    if Z == 4:
+        return FOUR
+    most = ("ua", "ub", "da", "db", "o")
+    last = ("q", "k", "v")
+    plan = {
+        "masks": [("w_out_z", 0), ("w_own_y", 0), ("w_own_x", 0), ("tr",), ("tl",), ("tp",), ("tc",)],
+        "small": [("w_z", 0), ("w_m", 0), ("w_l", 0), ("gtokp",), ("w_c", 0)],
+        ("A", 0): [(step, g) for g in (1, 2) for step in ("w_out_z", "w_own_y", "w_own_x")],
+        ("B", 0): [("o_hi",), ("w_z", 1), ("w_z", 2), ("w_m", 1), ("w_m", 2)],
+        "merge": [("o_lo",), ("g_o",), ("w_l", 1), ("w_l", 2)],
+        "out": [("qtail",), ("w_c", 1), ("w_c", 2)],
+        "dOc": [("g_ol",)],
+        "dwu": [("dO",)],
+        "sent": [("r_c", g) for g in most],
+        "dosT": [("r_1", g) for g in most] + [("g_dO",)],
+        ("h", Z - 1): [("r_2", g) for g in most],
+        "kv": [("p_z", Z - 2)] + [("r_z", g) for g in most],
+        "end": [("gq",)] + [(step, g) for step in ("r_c", "r_1", "r_2", "r_z") for g in last],
+    }
+    for k in range(1, Z):
+        plan.setdefault(("A", k), []).append(("tok_z", k))
+    for k in range(Z - 2):
+        plan[("t", k + 1)] = [("p_z", k)]
+    plan["end"] += [("r_zz", g) for g in most + last] + [("s", k) for k in range(4)] + [("first",), ("s_end",)]
+    plan["end"] += [("r_end", g) for g in most + last]
+    return plan
+
+
 def body(
     Z, FK, R, D, NT,
-    tok_ref, cot_ref, wq_ref, wo_ref, wu_ref, wd_ref,
+    tok_in, cot_in, wq_in, wo_in, wu_in, wd_in,
     v0, v1, v2, v3, v4, v5, v6, v7, v8, len_ref, sup_ref,
     out_ref, gtok_ref, gqkv_ref, gout_ref, gup_ref, gdown_ref, gsm_ref,
     tokb, tokp, kb, vb, eb, stat, w0, w1, w2, gs, gu, gd,
@@ -68,10 +138,11 @@
     crf, zrf, par, upb, qt, dot_, qs, dos, ot, mrun, dqt,
     oh, ol, ml, ohr, olr, mlr, gqs, gqr,
     nrm2, hid, acc, gsec, dwkv, lacc, upg, xq,
-    sg, src, srx, sry, srz, tile,
+    sg, src, srx, sry, srz, tile, tok_ref, cot_ref, act_all, gpre_all, early,
+    s_in,
     s_tz, s_tc, r_t, s_tp, r_tp,
     s_wz, r_wz, s_wy, r_wy, s_wx, r_wx, s_wc, r_wc,
-    s_gc, r_gc, s_gx, r_gx, s_gy, r_gy, s_gz, r_gz,
+    s_gc, r_gc, s_gx, r_gx, s_gy, r_gy, s_gd, r_gd, s_gz, r_gz,
     s_pc, r_pc, s_pz, r_pz, s_y, r_y,
     s_sc, r_sc, s_sx, r_sx, s_sy, r_sy, s_sz, r_sz,
 ):
@@ -111,6 +182,9 @@
     def d_f(ff):
         return (i, ff)
 
+    def d_diag(ff):
+        return dev(z, oy, c, ff)
+
     def cp(s, d, ss, rs, to):
         return pltpu.make_async_remote_copy(
             src_ref=s, dst_ref=d, send_sem=ss, recv_sem=rs, device_id=to, device_id_type=MESH
@@ -125,10 +199,29 @@
     def sent(s, ss):
         cp(s, s, ss, ss, d_core).wait_send()
 
+    arriving = [
+        pltpu.make_async_copy(a, b, s_in.at[n])
+        for n, (a, b) in enumerate((
+            (wq_in, w0.at[z, y, c, f, :, 0 : 3 * D]),
+            (tok_in, tokb.at[z, c]),
+            (wo_in, w1.at[z, y, c, f, :, 0:D]),
+            (wu_in, w1.at[z, y, c, f, :, D : D + FF]),
+            (wd_in, w2.at[z, y, c, f]),
+            (tok_in, tok_ref),
+            (cot_in, cot_ref),
+        ))
+    ]
+    for t in arriving:
+        t.start()
     bar = pltpu.get_barrier_semaphore()
-    partners = [d_core, d_y] + [d_z(zplus(k)) for k in range(1, Z)] + [d_f(fplus(k)) for k in range(1, FK)]
+    partners = [d_core, d_y] + [d_z(zplus(k)) for k in range(1, Z)]
+    partners += [to(fplus(k)) for k in range(1, FK) for to in (d_f, d_diag)]
     for to in partners:
         pl.semaphore_signal(bar, inc=1, device_id=to, device_id_type=MESH)
+    tile[...] = jnp.zeros((SLAB, 128), F32)
+    for r, v in enumerate((v0, v1, v2, v3, v4, v5, v6, v7, v8)):
+        tile[r : r + 1, 0 : v.shape[1]] = v[...].astype(F32)
+    w0[z, y, c, f, :, 3 * D : 3 * D + 128] = tile[...].astype(BF16)
     pl.semaphore_wait(bar, len(partners))
 
     def tok_push(zz, ss_z, to):
@@ -166,7 +259,7 @@
 
     wb = (w0, w1, w2)
 
-    x_first = {2}
+    x_first = X_FIRST
 
     def w_push_x(g, zz, yy):
         for k in range(1, FK):
@@ -241,28 +334,319 @@
             else:
                 got(wb[g].at[:, :, oc, fplus(n)], r_wc.at[g, n])
 
-    tokb[z, c] = tok_ref[...]
-    w0[z, y, c, f, :, 0 : 3 * D] = wq_ref[...]
-    tile[...] = jnp.zeros((SLAB, 128), F32)
-    for r, v in enumerate((v0, v1, v2, v3, v4, v5, v6, v7, v8)):
-        tile[r : r + 1, 0 : v.shape[1]] = v[...].astype(F32)
-    w0[z, y, c, f, :, 3 * D : 3 * D + 128] = tile[...].astype(BF16)
-    w1[z, y, c, f, :, 0:D] = wo_ref[...]
-    w1[z, y, c, f, :, D : D + FF] = wu_ref[...]
-    w2[z, y, c, f] = wd_ref[...]
-
-    w_out_z(0)
-    w_own_y(0)
-    w_own_x(0)
-    tok_right(z)
-    tok_left(z)
-    w_out_z(1)
-    w_own_y(1)
-    w_own_x(1)
-    w_own_x(2)
-    push(tokb.at[z, c], tokp, s_tp, r_tp, d_y)
-    tok_core(z)
-    w_own_y(2)
+    HF = FF // 2
+    store = (gs, gs, gs, gs, gu, gu, gd, gd)
+    from_core = (cs, cs, cs, cs, cu, cu, cd, cd)
+    from_x = (xs, xs, xs, xs, xu, xu, xd, xd)
+    from_y = (ys, ys, ys, ys, yu, yu, yd, yd)
+    from_z = (zs, zs, zs, zs, zu, zu, zd, zd)
+    lead = (0, 1, 2, 3, 0, 1, 0, 1)
+    Q, K, V, O, UA, UB, DA, DB = range(8)
+    y_first = {(Q, K, V, O, UA, UB, DA, DB)[t] for t in Y_FIRST}
+    direct = {(Q, K, V, O, UA, UB, DA, DB)[t] for t in DIRECT}
+    straight = {(Q, K, V, O, UA, UB, DA, DB)[t] for t in STRAIGHT}
+
+    def r_c(g):
+        n = lead[g]
+        push(store[g].at[n, :, :, oc], from_core[g].at[n], s_gc.at[g], r_gc.at[g], d_core)
+
+    def r_push_x(g, whole):
+        n = lead[g]
+        for k in range(1, FK):
+            ff = fplus(k)
+            if whole:
+                push(store[g].at[n, :, :, c, ff], from_x[g].at[n, f], s_gx.at[g, ff], r_gx.at[g, f], d_f(ff))
+            else:
+                push(store[g].at[n, :, y, c, ff], from_x[g].at[n, f, :, 0], s_gx.at[g, ff], r_gx.at[g, f], d_f(ff))
+
+    def r_push_y(g, whole):
+        n = lead[g]
+        if whole:
+            push(store[g].at[n, :, oy, c], from_y[g].at[n], s_gy.at[g], r_gy.at[g], d_y)
+        else:
+            push(store[g].at[n, :, oy, c, f], from_y[g].at[n, :, 0], s_gy.at[g], r_gy.at[g], d_y)
+
+    def over_z(one):
+        def step(zz, carry):
+            one(zz)
+            return carry
+
+        lax.fori_loop(0, Z, step, 0)
+
+    def r_1(g):
+        n = lead[g]
+        got(from_core[g].at[n], r_gc.at[g])
+
+        def one(zz):
+            t = store[g][n, zz, :, c].astype(F32) + from_core[g][n, zz].astype(F32)
+            store[g][n, zz, :, c] = t.astype(BF16)
+
+        over_z(one)
+        if g in direct:
+            r_push_x(g, False)
+            r_push_y(g, False)
+            for k in range(1, FK):
+                ff = fplus(k)
+                t = store[g].at[n, :, oy, c, ff]
+                push(t, from_x[g].at[n, f, :, 1], s_gd.at[g, ff], r_gd.at[g, f], d_diag(ff))
+        elif g in y_first:
+            r_push_y(g, True)
+        else:
+            r_push_x(g, True)
+
+    def r_2(g):
+        n = lead[g]
+        if g in direct:
+            return
+        if g in y_first:
+            got(from_y[g].at[n], r_gy.at[g])
+
+            def one(zz):
+                t = store[g][n, zz, y, c].astype(F32) + from_y[g][n, zz].astype(F32)
+                store[g][n, zz, y, c] = t.astype(BF16)
+
+            over_z(one)
+            r_push_x(g, False)
+        else:
+            for k in range(1, FK):
+                got(from_x[g].at[n, fplus(k)], r_gx.at[g, fplus(k)])
+
+            def one(zz):
+                t = store[g][n, zz, :, c, f].astype(F32)
+                for k in range(1, FK):
+                    t = t + from_x[g][n, fplus(k), zz].astype(F32)
+                store[g][n, zz, :, c, f] = t.astype(BF16)
+
+            if FK > 1:
+                over_z(one)
+            r_push_y(g, False)
+
+    def r_z(g):
+        n = lead[g]
+        if g in direct:
+            got(from_y[g].at[n, :, 0], r_gy.at[g])
+            for k in range(1, FK):
+                got(from_x[g].at[n, fplus(k), :, 0], r_gx.at[g, fplus(k)])
+                got(from_x[g].at[n, fplus(k), :, 1], r_gd.at[g, fplus(k)])
+
+            def one(zz):
+                t = store[g][n, zz, y, c, f].astype(F32) + from_y[g][n, zz, 0].astype(F32)
+                for k in range(1, FK):
+                    t = t + from_x[g][n, fplus(k), zz, 0].astype(F32) + from_x[g][n, fplus(k), zz, 1].astype(F32)
+                store[g][n, zz, y, c, f] = t.astype(BF16)
+
+            over_z(one)
+        elif g in y_first:
+            for k in range(1, FK):
+                got(from_x[g].at[n, fplus(k), :, 0], r_gx.at[g, fplus(k)])
+
+            def one(zz):
+                t = store[g][n, zz, y, c, f].astype(F32)
+                for k in range(1, FK):
+                    t = t + from_x[g][n, fplus(k), zz, 0].astype(F32)
+                store[g][n, zz, y, c, f] = t.astype(BF16)
+
+            if FK > 1:
+                over_z(one)
+        else:
+            got(from_y[g].at[n, :, 0], r_gy.at[g])
+
+            def one(zz):
+                t = store[g][n, zz, y, c, f].astype(F32) + from_y[g][n, zz, 0].astype(F32)
+                store[g][n, zz, y, c, f] = t.astype(BF16)
+
+            over_z(one)
+        if g in straight:
+            for k in range(1, Z):
+                zz = zplus(k)
+                push(store[g].at[n, zz, y, c, f], from_z[g].at[n, z], s_gz.at[g, zz], r_gz.at[g, z], d_z(zz))
+        else:
+            r_fold(g, 1)
+
+    def r_fold(g, bit):
+        n = lead[g]
+        for m in range(bit, Z, 2 * bit):
+            push(
+                store[g].at[n, zxor(m), y, c, f], from_z[g].at[n, zxor(bit ^ (m - 1))],
+                s_gz.at[g, zxor(m)], r_gz.at[g, zxor(bit ^ (m - 1))], d_z(zxor(bit)),
+            )
+
+    def r_zz(g):
+        n = lead[g]
+        bit = 1
+        while g not in straight and 2 * bit < Z:
+            for m in range(0, Z, 2 * bit):
+                zz, at = zxor(m), zxor(m + bit - 1)
+                got(from_z[g].at[n, at], r_gz.at[g, at])
+                t = store[g][n, zz, y, c, f].astype(F32) + from_z[g][n, at].astype(F32)
+                store[g][n, zz, y, c, f] = t.astype(BF16)
+            bit *= 2
+            r_fold(g, bit)
+
+    def r_end(g):
+        n = lead[g]
+        t = store[g][n, z, y, c, f].astype(F32)
+        if g in straight:
+            for k in range(1, Z):
+                zz = zplus(k)
+                got(from_z[g].at[n, zz], r_gz.at[g, zz])
+                t = t + from_z[g][n, zz].astype(F32)
+        else:
+            at = zxor(Z // 2 - 1)
+            got(from_z[g].at[n, at], r_gz.at[g, at])
+            t = t + from_z[g][n, at].astype(F32)
+        if g <= V:
+            gqkv_ref[:, g * D : (g + 1) * D] = t
+        elif g == O:
+            gout_ref[...] = t
+        elif g <= UB:
+            gup_ref[:, (g - UA) * HF : (g - UA + 1) * HF] = t
+        else:
+            gdown_ref[(g - DA) * 2 * SLAB : (g - DA + 1) * 2 * SLAB, :] = t
+
+    def r_sent(g):
+        n = lead[g]
+        sent(store[g].at[n, :, :, oc], s_gc.at[g])
+        for k in range(1, FK):
+            ff = fplus(k)
+            if g in y_first or g in direct:
+                sent(store[g].at[n, :, y, c, ff], s_gx.at[g, ff])
+            else:
+                sent(store[g].at[n, :, :, c, ff], s_gx.at[g, ff])
+            if g in direct:
+                sent(store[g].at[n, :, oy, c, ff], s_gd.at[g, ff])
+        if g in y_first and g not in direct:
+            sent(store[g].at[n, :, oy, c], s_gy.at[g])
+        else:
+            sent(store[g].at[n, :, oy, c, f], s_gy.at[g])
+        for k in range(1, Z):
+            sent(store[g].at[n, zplus(k), y, c, f], s_gz.at[g, zplus(k)])
+
+    turns = sorted(range(1, Z), key=lambda m: (m & -m, m)) + [0]
+
+    def plane(n):
+        m = jnp.int32(0)
+        for k in range(Z - 1):
+            m = jnp.where(n == k, turns[k], m)
+        return zxor(m)
+
+    def p_sum(m):
+        zz = zxor(m)
+        got(crf.at[zz], r_pc.at[zz])
+        t = tokb[zz, c].astype(F32) + crf[zz].astype(F32)
+        bit = 1
+        while bit < Z and m % (2 * bit) == 0:
+            at = zxor(m + bit - 1)
+            got(zrf.at[at], r_pz.at[at])
+            t = t + zrf[at].astype(F32)
+            bit *= 2
+        return t
+
+    def p_z(s):
+        m = turns[s]
+        bit = m & -m
+        zz, at = zxor(m), zxor(bit ^ (m - 1))
+        tokb[zz, c] = p_sum(m).astype(BF16)
+        push(tokb.at[zz, c], zrf.at[at], s_pz.at[zz], r_pz.at[at], d_z(zxor(bit)))
+
+    def queries_back():
+        push(gqs, gqr, s_y.at[5], r_y.at[5], d_y)
+
+    def sums():
+        push(sg.at[0], src, s_sc, r_sc, d_core)
+
+    def sums_core():
+        got(src, r_sc)
+        sg[1] = sg[0] + src[...]
+        for k in range(1, FK):
+            ff = fplus(k)
+            push(sg.at[1], srx.at[f], s_sx.at[ff], r_sx.at[f], d_f(ff))
+
+    def sums_x():
+        t = sg[1]
+        for k in range(1, FK):
+            got(srx.at[fplus(k)], r_sx.at[fplus(k)])
+            t = t + srx[fplus(k)]
+        sg[2] = t
+        push(sg.at[2], sry, s_sy, r_sy, d_y)
+
+    def sums_y():
+        got(sry, r_sy)
+        sg[3] = sg[2] + sry[...]
+        for k in range(1, Z):
+            zz = zplus(k)
+            push(sg.at[3], srz.at[z], s_sz.at[zz], r_sz.at[z], d_z(zz))
+
+    def sums_z():
+        t = sg[3]
+        for k in range(1, Z):
+            zz = zplus(k)
+            got(srz.at[zz], r_sz.at[zz])
+            t = t + srz[zz]
+        gsm_ref[...] = t
+
+    def first():
+        got(gqr, r_y.at[5])
+        t = p_sum(0) + acc[...] + gqr[...].astype(F32)
+        mean, centered, rstd = moments(tok_ref[...].astype(F32))
+        gtok_ref[...] = (hid[...] + norm_back(t * par[0:1, :], centered * rstd, rstd)).astype(BF16)
+
+
+    qrows = slice(HD, HD + SLAB)
+    grows = slice(0, HD + SLAB)
+    near_half, far_half = slice(0, R), slice(R, 2 * R)
+
+    def far_out():
+        push(oh, ohr, s_y.at[0], r_y.at[0], d_y)
+        push(ml, mlr, s_y.at[1], r_y.at[1], d_y)
+
+    def far_got():
+        got(ohr, r_y.at[0])
+        got(mlr, r_y.at[1])
+
+    def back_got():
+        got(qt.at[:, qrows, far_half], r_y.at[3])
+        got(dot_.at[:, grows, far_half], r_y.at[4])
+
+    events = {
+        "tr": lambda: tok_right(z),
+        "tl": lambda: tok_left(z),
+        "tp": lambda: push(tokb.at[z, c], tokp, s_tp, r_tp, d_y),
+        "tc": lambda: tok_core(z),
+        "tok_z": tok_z,
+        "gtokp": lambda: got(tokp, r_tp),
+        "w_out_z": w_out_z, "w_own_y": w_own_y, "w_own_x": w_own_x, "w_z": w_z, "w_m": w_m, "w_l": w_l, "w_c": w_c,
+        "o_hi": far_out,
+        "o_lo": lambda: push(ol, olr, s_y.at[2], r_y.at[2], d_y),
+        "g_o": far_got,
+        "g_ol": lambda: got(olr, r_y.at[2]),
+        "qtail": lambda: push(qt.at[:, qrows, near_half], qt.at[:, qrows, far_half], s_y.at[3], r_y.at[3], d_y),
+        "dO": lambda: push(dot_.at[:, grows, near_half], dot_.at[:, grows, far_half], s_y.at[4], r_y.at[4], d_y),
+        "g_dO": back_got,
+        "gq": queries_back,
+        "r_c": r_c, "r_1": r_1, "r_2": r_2, "r_z": r_z, "r_zz": r_zz, "r_end": r_end,
+        "p_z": p_z,
+        "first": first,
+        "s": lambda k: (sums, sums_core, sums_x, sums_y)[k](),
+        "s_end": sums_z,
+    }
+    chunks = {"q": Q, "k": K, "v": V, "o": O, "ua": UA, "ub": UB, "da": DA, "db": DB}
+    plan = order_of(Z)
+
+    def do(stage):
+        for name, *which in plan.get(stage, ()):
+            events[name](*[chunks.get(t, t) for t in which])
+
+    def run(stage, n):
+        for at in range(Z):
+            if (stage, at) in plan:
+                @pl.when(n == at)
+                def _():
+                    do((stage, at))
+
+    for t in arriving:
+        t.wait()
+    do("masks")
 
     starts, ends, stops = [], [], []
     total = jnp.int32(0)
@@ -304,13 +688,7 @@
         ot[h] = jnp.zeros((2 * HD, 2 * R), F32)
         mrun[h] = jnp.full((1, 2 * R), MASKED, F32)
 
-    w_z(0)
-    w_m(0)
-    tok_z(1)
-    w_out_z(2)
-    w_l(0)
-    w_z(1)
-    w_c(0)
+    do("small")
 
     piece = D // NSH
     small = w0[:, :, :, :, :, 3 * D : 3 * D + 128].reshape(NSH * SLAB, 128)
@@ -342,7 +720,6 @@
     upb[...] = col_sum(jnp.where(mine, wide, 0.0))
     ln1g, ln1b = par[0:1, :], par[1:2, :]
 
-    got(tokp, r_tp)
     tokens = tok_ref[...].astype(F32)
     mean, centered, rstd = moments(tokens)
     xq[0:R, :] = (centered * rstd * ln1g + ln1b).astype(BF16)
@@ -361,25 +738,6 @@
         rest = jnp.where(z < Z - 1 - z, s, Z - 1 - s)
         return jnp.where(s <= 2 * inner, paired, rest)
 
-    if Z == 4:
-        arrivals = {
-            1: [(tok_z, 2)],
-            2: [(w_m, 1), (w_z, 2)],
-            3: [(tok_z, 3)],
-            4: [(w_m, 2)],
-            6: [(w_l, 1)],
-        }
-    else:
-        arrivals = {n: [(tok_z, n + 1)] for n in range(1, Z - 1)}
-        arrivals[Z] = [(w_m, 1), (w_z, 2), (w_l, 1), (w_m, 2)]
-
-    def run(table, n):
-        for at in sorted(table):
-            @pl.when(n == at)
-            def _():
-                for step, which in table[at]:
-                    step(which)
-
     def attend(h, keys, values, extra, span):
         cols = slice(h * HD, (h + 1) * HD)
         s = dot_nn(jnp.concatenate([keys[:, cols], extra], axis=1), qt[h, :, span])
@@ -392,7 +750,7 @@
 
     def ahead(n, carry):
         zz = near(n)
-        run(arrivals, n)
+        run("A", n)
         got(tokb.at[zz, oc], r_t.at[zz, oc])
         mean, centered, rstd = moments(tokb[zz].reshape(2 * R, D).astype(F32))
         stat[zz] = jnp.where(lax.broadcasted_iota(jnp.int32, (2 * R, 128), 1) == 0, mean, rstd)
@@ -409,6 +767,7 @@
 
     lax.fori_loop(0, Z, ahead, 0)
 
+    do("osplit")
     for h in range(H):
         t = ot[h, 0:HD, R : 2 * R]
         first_part = t.astype(BF16)
@@ -416,23 +775,15 @@
         ol[h] = (t - first_part.astype(F32)).astype(BF16)
         ml[h : h + 1, :] = mrun[h, :, R : 2 * R]
         ml[H + h : H + h + 1, :] = ot[h, HD + NT : HD + NT + 1, R : 2 * R]
-    push(oh, ohr, s_y.at[0], r_y.at[0], d_y)
-    push(ml, mlr, s_y.at[1], r_y.at[1], d_y)
-
     def ahead_own(n, carry):
         zz = near(n)
-        run(arrivals, Z + n)
+        run("B", n)
         for h in range(H):
             attend(h, kb[zz], vb[zz], eb[zz], slice(0, R))
         return carry
 
     lax.fori_loop(0, Z, ahead_own, 0)
-    w_l(2)
-    w_c(1)
-    push(ol, olr, s_y.at[2], r_y.at[2], d_y)
-
-    got(ohr, r_y.at[0])
-    got(mlr, r_y.at[1])
+    do("merge")
     parts = []
     row_tail = lax.broadcasted_iota(jnp.int32, (SLAB, R), 0)
     for h in range(H):
@@ -452,7 +803,7 @@
             jnp.where(row_tail == NT + 1, -m2, jnp.where(row_tail == NT + 2, -m3, onehot[0:SLAB, 0:R])),
         )
         qt[h, HD : HD + SLAB, 0:R] = tail.astype(BF16)
-    push(qt.at[:, HD : HD + SLAB, 0:R], qt.at[:, HD : HD + SLAB, R : 2 * R], s_y.at[3], r_y.at[3], d_y)
+    do("out")
     attn_low = jnp.concatenate(parts, axis=1)
     w_out = w1[:, :, :, :, :, 0:D].reshape(D, D)
     hidden = tokens + (dot_nn(attn_low, w_out) + par[4:5, :])
@@ -462,201 +813,27 @@
     nrm2[...] = (n2 * par[5:6, :] + par[6:7, :]).astype(BF16)
     acc[...] = hidden + par[7:8, :]
     gsec[...] = jnp.zeros((R, D), F32)
-    w_c(2)
-
-    HF = FF // 2
-    store = (gs, gs, gs, gs, gu, gu, gd, gd)
-    from_core = (cs, cs, cs, cs, cu, cu, cd, cd)
-    from_x = (xs, xs, xs, xs, xu, xu, xd, xd)
-    from_y = (ys, ys, ys, ys, yu, yu, yd, yd)
-    from_z = (zs, zs, zs, zs, zu, zu, zd, zd)
-    lead = (0, 1, 2, 3, 0, 1, 0, 1)
-    Q, K, V, O, UA, UB, DA, DB = range(8)
-    y_first = {V, DB}
-    straight = {Q, K, V}
-
-    def r_c(g):
-        n = lead[g]
-        push(store[g].at[n, :, :, oc], from_core[g].at[n], s_gc.at[g], r_gc.at[g], d_core)
-
-    def r_push_x(g, whole):
-        n = lead[g]
-        for k in range(1, FK):
-            ff = fplus(k)
-            if whole:
-                push(store[g].at[n, :, :, c, ff], from_x[g].at[n, f], s_gx.at[g, ff], r_gx.at[g, f], d_f(ff))
-            else:
-                push(store[g].at[n, :, y, c, ff], from_x[g].at[n, f, :, 0], s_gx.at[g, ff], r_gx.at[g, f], d_f(ff))
-
-    def r_push_y(g, whole):
-        n = lead[g]
-        if whole:
-            push(store[g].at[n, :, oy, c], from_y[g].at[n], s_gy.at[g], r_gy.at[g], d_y)
-        else:
-            push(store[g].at[n, :, oy, c, f], from_y[g].at[n, :, 0], s_gy.at[g], r_gy.at[g], d_y)
-
-    def over_z(one):
-        def step(zz, carry):
-            one(zz)
-            return carry
-
-        lax.fori_loop(0, Z, step, 0)
-
-    def r_1(g):
-        n = lead[g]
-        got(from_core[g].at[n], r_gc.at[g])
-
-        def one(zz):
-            t = store[g][n, zz, :, c].astype(F32) + from_core[g][n, zz].astype(F32)
-            store[g][n, zz, :, c] = t.astype(BF16)
-
-        over_z(one)
-        if g in y_first:
-            r_push_y(g, True)
-        else:
-            r_push_x(g, True)
-
-    def r_2(g):
-        n = lead[g]
-        if g in y_first:
-            got(from_y[g].at[n], r_gy.at[g])
-
-            def one(zz):
-                t = store[g][n, zz, y, c].astype(F32) + from_y[g][n, zz].astype(F32)
-                store[g][n, zz, y, c] = t.astype(BF16)
-
-            over_z(one)
-            r_push_x(g, False)
-        else:
-            for k in range(1, FK):
-                got(from_x[g].at[n, fplus(k)], r_gx.at[g, fplus(k)])
-
-            def one(zz):
-                t = store[g][n, zz, :, c, f].astype(F32)
-                for k in range(1, FK):
-                    t = t + from_x[g][n, fplus(k), zz].astype(F32)
-                store[g][n, zz, :, c, f] = t.astype(BF16)
-
-            if FK > 1:
-                over_z(one)
-            r_push_y(g, False)
-
-    def r_z(g):
-        n = lead[g]
-        if g in y_first:
-            for k in range(1, FK):
-                got(from_x[g].at[n, fplus(k), :, 0], r_gx.at[g, fplus(k)])
-
-            def one(zz):
-                t = store[g][n, zz, y, c, f].astype(F32)
-                for k in range(1, FK):
-                    t = t + from_x[g][n, fplus(k), zz, 0].astype(F32)
-                store[g][n, zz, y, c, f] = t.astype(BF16)
-
-            if FK > 1:
-                over_z(one)
-        else:
-            got(from_y[g].at[n, :, 0], r_gy.at[g])
-
-            def one(zz):
-                t = store[g][n, zz, y, c, f].astype(F32) + from_y[g][n, zz, 0].astype(F32)
-                store[g][n, zz, y, c, f] = t.astype(BF16)
-
-            over_z(one)
-        if g in straight:
-            for k in range(1, Z):
-                zz = zplus(k)
-                push(store[g].at[n, zz, y, c, f], from_z[g].at[n, z], s_gz.at[g, zz], r_gz.at[g, z], d_z(zz))
-        else:
-            r_fold(g, 1)
-
-    def r_fold(g, bit):
-        n = lead[g]
-        for m in range(bit, Z, 2 * bit):
-            push(
-                store[g].at[n, zxor(m), y, c, f], from_z[g].at[n, zxor(bit ^ (m - 1))],
-                s_gz.at[g, zxor(m)], r_gz.at[g, zxor(bit ^ (m - 1))], d_z(zxor(bit)),
-            )
-
-    def r_zz(g):
-        n = lead[g]
-        bit = 1
-        while 2 * bit < Z:
-            for m in range(0, Z, 2 * bit):
-                zz, at = zxor(m), zxor(m + bit - 1)
-                got(from_z[g].at[n, at], r_gz.at[g, at])
-                t = store[g][n, zz, y, c, f].astype(F32) + from_z[g][n, at].astype(F32)
-                store[g][n, zz, y, c, f] = t.astype(BF16)
-            bit *= 2
-            r_fold(g, bit)
-
-    def r_end(g):
-        n = lead[g]
-        t = store[g][n, z, y, c, f].astype(F32)
-        if g in straight:
-            for k in range(1, Z):
-                zz = zplus(k)
-                got(from_z[g].at[n, zz], r_gz.at[g, zz])
-                t = t + from_z[g][n, zz].astype(F32)
-        else:
-            at = zxor(Z // 2 - 1)
-            got(from_z[g].at[n, at], r_gz.at[g, at])
-            t = t + from_z[g][n, at].astype(F32)
-        if g <= V:
-            gqkv_ref[:, g * D : (g + 1) * D] = t
-        elif g == O:
-            gout_ref[...] = t
-        elif g <= UB:
-            gup_ref[:, (g - UA) * HF : (g - UA + 1) * HF] = t
-        else:
-            gdown_ref[(g - DA) * 2 * SLAB : (g - DA + 1) * 2 * SLAB, :] = t
-
-    def r_sent(g):
-        n = lead[g]
-        sent(store[g].at[n, :, :, oc], s_gc.at[g])
-        for k in range(1, FK):
-            ff = fplus(k)
-            if g in y_first:
-                sent(store[g].at[n, :, y, c, ff], s_gx.at[g, ff])
-            else:
-                sent(store[g].at[n, :, :, c, ff], s_gx.at[g, ff])
-        if g in y_first:
-            sent(store[g].at[n, :, oy, c], s_gy.at[g])
-        else:
-            sent(store[g].at[n, :, oy, c, f], s_gy.at[g])
-        for k in range(1, Z):
-            sent(store[g].at[n, zplus(k), y, c, f], s_gz.at[g, zplus(k)])
-
-    def half(hh):
-        def chunk(j, carry):
-            cols = pl.ds(pl.multiple_of(D + j * CH, 128), CH)
-            bcols = pl.ds(pl.multiple_of(j * CH, 128), CH)
-            hcols = pl.ds(pl.multiple_of((j - hh * (Z // 2)) * CH, 128), CH)
-            up = w1[:, :, :, :, :, cols].reshape(D, CH)
-            down = w2[j].reshape(CH, D)
-            normed = nrm2[...]
-            cot = cot_ref[...]
-            pre = dot_nn(normed, up) + upb[:, bcols]
-            phi = 0.5 * (1.0 + lax.erf(pre * (0.5**0.5)))
-            act = (pre * phi).astype(BF16)
-            slope = phi + pre * (jnp.exp2(pre * pre * (-0.5 / LN2)) * ((2.0 * math.pi) ** -0.5))
-            acc[...] += dot_nn(act, down)
-            gpre32 = dot_nt(cot, down) * slope
-            gpre = gpre32.astype(BF16)
-            gsec[...] += dot_nt(gpre, up)
-            upg[:, bcols] = col_sum(gpre.astype(F32))
-            gu[hh, :, :, :, :, :, hcols] = dot_tn(normed, gpre).astype(BF16).reshape(Z, 2, 2, FK, SLAB, CH)
-            g_down = dot_tn(act, cot).astype(BF16).reshape(2, 2, FK, 4 * SLAB, D)
-            gd[0, j] = g_down[:, :, :, 0 : 2 * SLAB]
-            gd[1, j] = g_down[:, :, :, 2 * SLAB : 4 * SLAB]
-            return carry
-
-        lax.fori_loop(hh * (Z // 2), (hh + 1) * (Z // 2), chunk, 0)
-
-    half(0)
-    r_c(UA)
-    half(1)
-    r_1(UA)
+
+    def chunk(j, carry):
+        cols = pl.ds(pl.multiple_of(D + j * CH, 128), CH)
+        bcols = pl.ds(pl.multiple_of(j * CH, 128), CH)
+        up = w1[:, :, :, :, :, cols].reshape(D, CH)
+        down = w2[j].reshape(CH, D)
+        pre = dot_nn(nrm2[...], up) + upb[:, bcols]
+        phi = 0.5 * (1.0 + lax.erf(pre * (0.5**0.5)))
+        act = (pre * phi).astype(BF16)
+        slope = phi + pre * (jnp.exp2(pre * pre * (-0.5 / LN2)) * ((2.0 * math.pi) ** -0.5))
+        acc[...] += dot_nn(act, down)
+        gpre = (dot_nt(cot_ref[...], down) * slope).astype(BF16)
+        gsec[...] += dot_nt(gpre, up)
+        upg[:, bcols] = col_sum(gpre.astype(F32))
+        act_all[:, bcols] = act
+        gpre_all[:, bcols] = gpre
+        return carry
+
+    do("ffn")
+    lax.fori_loop(0, Z, chunk, 0)
+    do("ln2")
     out_ref[...] = acc[...].astype(BF16)
 
     g_second = gsec[...]
@@ -666,22 +843,7 @@
     grad_hidden = cot32 + norm_back(g_second * ln2g, n2, rstd2)
     hid[...] = grad_hidden
     g_branch = grad_hidden.astype(BF16)
-    gs[O] = dot_tn(attn_low, g_branch).astype(BF16).reshape(Z, 2, 2, FK, SLAB, D)
-    r_c(UB)
-    r_c(DA)
-    r_c(DB)
-    r_c(O)
-    zero = jnp.zeros((1, D), F32)
-    for r in range(SLAB):
-        sg[0, r : r + 1, :] = zero
-    sg[0, 4:5, :] = col_sum(g_branch.astype(F32))
-    sg[0, 5:6, :] = col_sum(g_second * n2)
-    sg[0, 6:7, :] = col_sum(g_second)
-    sg[0, 7:8, :] = col_sum(cot32)
-    for r in range(FF // D):
-        sg[0, 8 + r : 9 + r, :] = upg[:, r * D : (r + 1) * D]
-
-    got(olr, r_y.at[2])
+    do("dOc")
     for h in range(H):
         rows = slice(h * HD, (h + 1) * HD)
         w_head = w1[:, :, :, :, :, 0:D].reshape(D, D)[rows, :]
@@ -696,7 +858,37 @@
         dot_[h, 0:HD, 0:R] = low
         dot_[h, HD : HD + SLAB, 0:R] = tail.astype(BF16)
         dos[0:R, rows] = low.T
-    push(dot_.at[:, 0 : HD + SLAB, 0:R], dot_.at[:, 0 : HD + SLAB, R : 2 * R], s_y.at[4], r_y.at[4], d_y)
+
+    def g_up(j, carry):
+        bcols = pl.ds(pl.multiple_of(j * CH, 128), CH)
+        t = dot_tn(nrm2[...], gpre_all[:, bcols]).astype(BF16).reshape(Z, 2, 2, FK, SLAB, CH)
+        hh = j // (Z // 2)
+        gu[hh, :, :, :, :, :, pl.ds(pl.multiple_of((j - hh * (Z // 2)) * CH, 128), CH)] = t
+        return carry
+
+    def g_down(j, carry):
+        bcols = pl.ds(pl.multiple_of(j * CH, 128), CH)
+        t = dot_tn(act_all[:, bcols], cot_ref[...]).astype(BF16).reshape(2, 2, FK, 4 * SLAB, D)
+        gd[0, j] = t[:, :, :, 0 : 2 * SLAB]
+        gd[1, j] = t[:, :, :, 2 * SLAB : 4 * SLAB]
+        return carry
+
+    do("dwu")
+    lax.fori_loop(0, Z, g_up, 0)
+    do("dwd")
+    lax.fori_loop(0, Z, g_down, 0)
+    do("dwo")
+    gs[O] = dot_tn(attn_low, g_branch).astype(BF16).reshape(Z, 2, 2, FK, SLAB, D)
+    zero = jnp.zeros((1, D), F32)
+    for r in range(SLAB):
+        sg[0, r : r + 1, :] = zero
+    sg[0, 4:5, :] = col_sum(g_branch.astype(F32))
+    sg[0, 5:6, :] = col_sum(g_second * n2)
+    sg[0, 6:7, :] = col_sum(g_second)
+    sg[0, 7:8, :] = col_sum(cot32)
+    for r in range(FF // D):
+        sg[0, 8 + r : 9 + r, :] = upg[:, r * D : (r + 1) * D]
+
     dqt[...] = jnp.zeros((H, HD, 2 * R), F32)
     dwkv[...] = jnp.zeros((D, 2 * D), F32)
     lacc[...] = jnp.zeros((3, 8, D), F32)
@@ -720,86 +912,23 @@
             sent(tokb.at[zz, c], s_tc.at[zz])
         sent(tokb.at[z, c], s_tp)
 
-    tok_sent()
-    r_1(UB)
-    r_1(DA)
-    r_1(DB)
-
-    got(qt.at[:, HD : HD + SLAB, R : 2 * R], r_y.at[3])
-    got(dot_.at[:, 0 : HD + SLAB, R : 2 * R], r_y.at[4])
-    for h in range(H):
-        dos[R : 2 * R, h * HD : (h + 1) * HD] = dot_[h, 0:HD, R : 2 * R].T
-
-    turns = sorted(range(1, Z), key=lambda m: (m & -m, m)) + [0]
-
-    def plane(n):
-        m = jnp.int32(0)
-        for k in range(Z - 1):
-            m = jnp.where(n == k, turns[k], m)
-        return zxor(m)
-
-    def p_sum(m):
-        zz = zxor(m)
-        got(crf.at[zz], r_pc.at[zz])
-        t = tokb[zz, c].astype(F32) + crf[zz].astype(F32)
-        bit = 1
-        while bit < Z and m % (2 * bit) == 0:
-            at = zxor(m + bit - 1)
-            got(zrf.at[at], r_pz.at[at])
-            t = t + zrf[at].astype(F32)
-            bit *= 2
-        return t
-
-    def p_z(s):
-        m = turns[s]
-        bit = m & -m
-        zz, at = zxor(m), zxor(bit ^ (m - 1))
-        tokb[zz, c] = p_sum(m).astype(BF16)
-        push(tokb.at[zz, c], zrf.at[at], s_pz.at[zz], r_pz.at[at], d_z(zxor(bit)))
-
-    if Z == 4:
-        before = {
-            1: [(r_1, O), (r_2, UA)],
-            2: [(r_2, DB), (r_2, UB)],
-            3: [(r_2, DA), (r_z, UA)],
-        }
-        between = {
-            1: [(p_z, 0)],
-            2: [(p_z, 1)],
-            3: [(p_z, 2), (r_z, UB)],
-        }
-        late = [
-            (r_c, K), (r_c, V), "queries", (r_c, Q), (r_z, DB), "sums", (r_1, V), (r_1, K), "gq", (r_z, DA), (r_2, O),
-            "core", (r_1, Q), (r_zz, UA), "x", (r_2, K), (r_2, V), (r_z, O), (r_zz, UB), (r_2, Q), "y", (r_zz, DB),
-            (r_z, K), (r_z, V), (r_zz, DA), (r_z, Q), (r_zz, O), "first",
-            (r_end, UA), (r_end, UB), (r_end, DA), (r_end, DB), (r_end, O), (r_end, K), (r_end, V), (r_end, Q), "z",
-        ]
-    else:
-        before = {1: [(r_1, O)]}
-        between = {s + 1: [(p_z, s)] for s in range(Z - 1)}
-        before[Z - 1] = [(r_2, UA), (r_2, UB), (r_2, DA), (r_2, DB), (r_2, O)]
-        late = [(r_z, g) for g in (O, UA, UB, DA, DB)]
-        late += ["queries", "sums", "gq", (r_c, Q), (r_c, K), (r_c, V), "core"]
-        late += [(r_1, Q), (r_1, K), (r_1, V), "x", (r_2, Q), (r_2, K), (r_2, V), "y", (r_z, Q), (r_z, K), (r_z, V)]
-        late += [(r_zz, g) for g in (O, UA, UB, DA, DB)] + ["first", "z"] + [(r_end, g) for g in range(8)]
-
-    def behind(n, carry):
-        zz = plane(n)
-        run(before, n)
+    def heads(zz, span):
         keys, values, extra = kb[zz], vb[zz], eb[zz]
         dks, dvs = [], []
         for h in range(H):
             cols = slice(h * HD, (h + 1) * HD)
-            s = dot_nn(jnp.concatenate([keys[:, cols], extra], axis=1), qt[h])
-            dp = dot_nn(jnp.concatenate([values[:, cols], extra], axis=1), dot_[h])
+            s = dot_nn(jnp.concatenate([keys[:, cols], extra], axis=1), qt[h, :, span])
+            dp = dot_nn(jnp.concatenate([values[:, cols], extra], axis=1), dot_[h, :, span])
             e = jnp.exp2(s).astype(BF16)
             ds = (e.astype(F32) * dp).astype(BF16)
-            dvs.append(dot_nn(e, dos[:, cols]))
-            dks.append(dot_nn(ds, qs[:, cols]) * LN2)
-            dqt[h] += dot_tn(keys[:, cols], ds)
-        dv = jnp.concatenate(dvs, axis=1)
-        dkv = jnp.concatenate(dks + [dv], axis=1).astype(BF16)
-        run(between, n)
+            dvs.append(dot_nn(e, dos[span, cols]))
+            dks.append(dot_nn(ds, qs[span, cols]) * LN2)
+            dqt[h, :, span] += dot_tn(keys[:, cols], ds)
+        return jnp.concatenate(dks + dvs, axis=1)
+
+    def rest(n, zz, dkv32):
+        dkv = dkv32.astype(BF16)
+        run("t", n)
         gp = dot_nt(dkv, w0[:, :, :, :, :, D : 3 * D].reshape(D, 2 * D))
         norm = (tokb[zz].reshape(2 * R, D).astype(F32) - stat[zz, :, 0:1]) * stat[zz, :, 1:2]
         tokb[zz] = gp.astype(BF16).reshape(2, R, D)
@@ -807,12 +936,39 @@
         x = (norm * par[0:1, :] + par[1:2, :]).astype(BF16)
         lacc[0] += fold_rows(gp * norm)
         lacc[1] += fold_rows(gp)
-        lacc[2] += fold_rows(dv)
+        lacc[2] += fold_rows(dkv32[:, D : 2 * D])
         dwkv[...] += dot_tn(x, dkv)
+
+    def behind_early(n, carry):
+        run("e", n)
+        early[n] = heads(plane(n), near_half)
         return carry
 
-    lax.fori_loop(0, Z, behind, 0)
-
+    def behind_far(n, carry):
+        run("h", n)
+        zz = plane(n)
+        rest(n, zz, early[n] + heads(zz, far_half))
+        return carry
+
+    def behind(n, carry):
+        run("h", n)
+        zz = plane(n)
+        rest(n, zz, heads(zz, slice(0, 2 * R)))
+        return carry
+
+    do("sent")
+    tok_sent()
+    E = early.shape[0] if Z == 4 else 0
+    if E:
+        lax.fori_loop(0, E, behind_early, 0)
+    do("dosT")
+    for h in range(H):
+        dos[R : 2 * R, h * HD : (h + 1) * HD] = dot_[h, 0:HD, R : 2 * R].T
+    if E:
+        lax.fori_loop(0, E, behind_far, 0)
+    lax.fori_loop(E, Z, behind, 0)
+
+    do("kv")
     gs[K] = dwkv[:, 0:D].astype(BF16).reshape(Z, 2, 2, FK, SLAB, D)
     gs[V] = dwkv[:, D : 2 * D].astype(BF16).reshape(Z, 2, 2, FK, SLAB, D)
 
@@ -829,56 +985,9 @@
         sg[0, 2:3, :] = col_sum(dq.astype(F32))
         sg[0, 3:4, :] = col_sum(lacc[2])
 
-    def queries_back():
-        push(gqs, gqr, s_y.at[5], r_y.at[5], d_y)
-
-    def sums():
-        push(sg.at[0], src, s_sc, r_sc, d_core)
-
-    def sums_core():
-        got(src, r_sc)
-        sg[1] = sg[0] + src[...]
-        for k in range(1, FK):
-            ff = fplus(k)
-            push(sg.at[1], srx.at[f], s_sx.at[ff], r_sx.at[f], d_f(ff))
-
-    def sums_x():
-        t = sg[1]
-        for k in range(1, FK):
-            got(srx.at[fplus(k)], r_sx.at[fplus(k)])
-            t = t + srx[fplus(k)]
-        sg[2] = t
-        push(sg.at[2], sry, s_sy, r_sy, d_y)
-
-    def sums_y():
-        got(sry, r_sy)
-        sg[3] = sg[2] + sry[...]
-        for k in range(1, Z):
-            zz = zplus(k)
-            push(sg.at[3], srz.at[z], s_sz.at[zz], r_sz.at[z], d_z(zz))
-
-    def sums_z():
-        t = sg[3]
-        for k in range(1, Z):
-            zz = zplus(k)
-            got(srz.at[zz], r_sz.at[zz])
-            t = t + srz[zz]
-        gsm_ref[...] = t
-
-    def first():
-        got(gqr, r_y.at[5])
-        t = p_sum(0) + acc[...] + gqr[...].astype(F32)
-        mean, centered, rstd = moments(tok_ref[...].astype(F32))
-        gtok_ref[...] = (hid[...] + norm_back(t * par[0:1, :], centered * rstd, rstd)).astype(BF16)
-
-    named = {
-        "queries": queries, "gq": queries_back, "sums": sums, "core": sums_core, "x": sums_x, "y": sums_y, "z": sums_z, "first": first,
-    }
-    for step in late:
-        if isinstance(step, str):
-            named[step]()
-        else:
-            step[0](step[1])
+    do("q")
+    queries()
+    do("end")
 
     for g in range(3):
         for k in range(1, Z):
@@ -968,10 +1077,16 @@
         vm((SLAB, D), F32),
         vm((Z, SLAB, D), F32),
         vm((SLAB, 128), F32),
+        vm((R, D), BF16),
+        vm((R, D), BF16),
+        vm((R, FF), BF16),
+        vm((R, FF), BF16),
+        vm((2, 2 * R, 2 * D) if Z == 4 else (1, 8, 128), F32),
+        dma(7),
         dma(2, Z), dma(Z), dma(Z, 2), pltpu.SemaphoreType.DMA, pltpu.SemaphoreType.DMA,
         dma(3, Z), dma(3, Z), dma(3, Z, FK), dma(3, Z, FK),
         dma(3, FK, Z, 2), dma(3, FK, Z, 2), dma(3, 2), dma(3, 2),
-        dma(8), dma(8), dma(8, FK), dma(8, FK), dma(8), dma(8), dma(8, Z), dma(8, Z),
+        dma(8), dma(8), dma(8, FK), dma(8, FK), dma(8), dma(8), dma(8, FK), dma(8, FK), dma(8, Z), dma(8, Z),
         dma(Z), dma(Z), dma(Z), dma(Z), dma(6), dma(6),
         pltpu.SemaphoreType.DMA, pltpu.SemaphoreType.DMA,
         dma(FK), dma(FK),
@@ -992,7 +1107,7 @@
             shape((4 * SLAB, D), F32),
             shape((SLAB, D), F32),
         ),
-        in_specs=[vmem] * 15 + [smem] * 2,
+        in_specs=[pl.BlockSpec(memory_space=pl.ANY)] * 6 + [vmem] * 9 + [smem] * 2,
         out_specs=[vmem] * 7,
         scratch_shapes=scratch,
         compiler_params=pltpu.CompilerParams(

time: 129 us -> 118 us (0.915)
  Pallas kernels: 128 us -> 117 us
    pallas_call x1, Pallas kernels: 126 us -> 115 us  [layer(): pl.pallas_call(functools.partial(body, Z, FK, R, D, NT), out_shape=(shape...]
where the time goes in v4:
time: 118 us
  Pallas kernels  117 us (99%)
    pallas_call x1, Pallas kernels, layer(): pl.pallas_call(functools.partial(body, Z, FK, R, D, NT), out_shape=(shape...  115 us

profile of v4, /device:TPU:0, one launch (start us, length us, event | category | flops | bytes accessed | tf_op | source)
XLA Modules:
  0.0 117.6 jit_solution(4855578701730587960)
XLA Ops:
  0.7 114.6 %layer.1 = (bf16[256,512]{1,0:T(8,128)(2,1)}, bf16[256,512]{1,0:T(8,128)(2,1)}, f32[16,1536]{1,0:T(8,128)}, f32[16,512]{1,0:T(8,128)}, f32[16,2048]{1,0:T(8,128)}, /*index=5*/f32[64,512]{1,0:T(8,128)}, f32[16,512]{1,0:T(8,128)}) custom-call(bf16[256,512]{1,0:T(8,128)(2,1)} %bitcast.22, bf16[256,512]{1,0:T(8,128)(2,1)} %bitcast.23, bf16[16,1536]{1,0:T(8,128)(2,1)} %wq_in.1, ...), custom_call_target="tpu_custom_call" | custom-call | tf_op jit(solution)/shard_map/layer/pallas_call | solution.py:1099
  115.3 2.2 %finish.1 = (bf16[256,512]{1,0:T(8,128)(2,1)}, bf16[256,512]{1,0:T(8,128)(2,1)}, f32[16,1536]{1,0:T(8,128)}, f32[16,512]{1,0:T(8,128)}, f32[16,2048]{1,0:T(8,128...) custom-call(bf16[256,512]{1,0:T(8,128)(2,1)} %get-tuple-element.37.r, ...), custom_call_target="tpu_custom_call" | custom-call | tf_op jit(solution)/shard_map/finish/pallas_call | solution.py:1148

commit v5 on v4

--- a/solution.py
+++ b/solution.py
@@ -59,44 +59,46 @@
 
 
 FOUR = {
-    "masks": [("w_out_z", 0), ("tr",), ("tl",), ("w_own_x", 2), ("tp",), ("w_own_x", 0), ("w_own_y", 2)],
+    "masks": [("w_out_z", 0), ("tc",), ("w_own_y", 0), ("tp",), ("w_own_x", 2), ("w_own_x", 1), ("tl",), ("tr",)],
     "small": [
-        ("gtokp",), ("w_out_z", 1), ("w_own_y", 0), ("w_z", 0), ("w_out_z", 2), ("w_m", 0), ("w_own_x", 1), ("tc",),
-        ("w_z", 1), ("w_l", 0), ("w_c", 0), ("tok_z", 1),
+        ("w_z", 0), ("w_own_x", 4), ("w_out_z", 1), ("tok_z", 1), ("w_m", 0), ("gtokp",), ("w_own_x", 0), ("w_z", 1),
+        ("w_own_y", 1), ("w_own_y", 4), ("w_out_z", 2), ("w_own_y", 2), ("w_l", 0), ("w_m", 1), ("tok_z", 2),
+        ("w_own_y", 3), ("w_c", 0),
     ],
-    ("A", 0): [("w_z", 2)],
-    ("A", 2): [("w_m", 1), ("tok_z", 2)],
-    ("A", 3): [("w_own_y", 1), ("w_m", 2), ("tok_z", 3)],
+    ("A", 0): [("w_out_z", 4), ("w_z", 2), ("w_out_z", 3), ("w_own_x", 3)],
+    ("A", 2): [("w_l", 1), ("w_m", 2)],
+    ("A", 3): [("tok_z", 3), ("w_z", 4)],
+    "osplit": [("w_z", 3), ("w_m", 4), ("w_l", 2)],
     ("B", 0): [("o_hi",)],
-    ("B", 1): [("w_l", 1)],
-    ("B", 3): [("w_l", 2), ("o_lo",)],
-    "merge": [("g_o",)],
-    "out": [("qtail",), ("w_c", 1)],
+    ("B", 1): [("w_m", 3)],
+    ("B", 3): [("w_c", 1), ("w_l", 4)],
+    "merge": [("w_l", 3), ("o_lo",), ("g_o",), ("w_c", 4)],
     "ffn": [("w_c", 2)],
-    "dOc": [("g_ol",)],
+    "ffd": [("w_c", 3)],
+    "dOc": [("qtail",), ("g_ol",)],
     "dwu": [("dO",)],
-    "dwo": [("r_c", "db")],
-    "sent": [("r_c", "da")],
-    ("e", 1): [("r_1", "db"), ("r_c", "ub"), ("r_1", "da")],
-    "dosT": [("r_c", "ua"), ("g_dO",)],
-    ("t", 0): [("r_2", "da")],
-    ("t", 1): [("r_2", "db"), ("r_z", "db")],
-    ("h", 2): [("r_1", "ua"), ("r_c", "o"), ("p_z", 1)],
-    ("t", 2): [("r_1", "o"), ("r_2", "ua"), ("p_z", 0), ("r_1", "ub")],
-    ("h", 3): [("r_z", "da")],
-    "q": [("r_2", "ub"), ("r_2", "o"), ("r_c", "k"), ("r_z", "ua"), ("r_c", "v")],
+    "sent": [("r_c", "ub")],
+    ("e", 2): [("r_1", "ub"), ("r_2", "ub")],
+    "dosT": [("r_c", "o"), ("g_dO",)],
+    ("h", 0): [("r_c", "db")],
+    ("h", 1): [("r_1", "o"), ("r_2", "o"), ("p_z", 0), ("r_c", "da")],
+    ("t", 1): [("r_1", "db")],
+    ("h", 2): [("r_z", "ub"), ("r_1", "da"), ("r_c", "ua")],
+    ("t", 2): [("r_2", "db"), ("p_z", 1), ("r_1", "ua")],
+    ("h", 3): [("r_z", "o"), ("r_z", "db")],
+    "kv": [("r_2", "da")],
+    "q": [("r_c", "v"), ("p_z", 2), ("r_1", "v"), ("r_zz", "ub"), ("r_c", "k"), ("r_2", "ua")],
     "end": [
-        ("p_z", 2), ("s", 0), ("r_zz", "db"), ("r_c", "q"), ("r_1", "k"), ("s", 1), ("r_1", "v"), ("r_end", "db"),
-        ("r_1", "q"), ("r_2", "v"), ("r_2", "q"), ("r_zz", "ua"), ("s", 2), ("r_zz", "da"), ("gq",), ("r_end", "ua"),
-        ("r_z", "ub"), ("r_2", "k"), ("r_z", "k"), ("r_z", "v"), ("r_z", "o"), ("r_zz", "k"), ("r_z", "q"), ("s", 3),
-        ("r_zz", "ub"), ("r_end", "da"), ("r_zz", "q"), ("r_zz", "o"), ("r_end", "k"), ("r_zz", "v"), ("first",),
-        ("r_end", "q"), ("r_end", "v"), ("r_end", "ub"), ("s_end",), ("r_end", "o"),
+        ("r_zz", "db"), ("s", 0), ("r_1", "k"), ("s", 1), ("r_c", "q"), ("r_z", "da"), ("r_2", "k"), ("r_z", "ua"),
+        ("r_2", "v"), ("r_end", "ub"), ("r_1", "q"), ("r_zz", "o"), ("r_zz", "da"), ("r_end", "db"), ("s", 2),
+        ("r_z", "k"), ("r_2", "q"), ("gq",), ("r_z", "v"), ("r_zz", "ua"), ("r_z", "q"), ("r_zz", "k"), ("s", 3),
+        ("r_zz", "v"), ("r_end", "ua"), ("r_end", "o"), ("r_zz", "q"), ("r_end", "da"), ("r_end", "k"), ("first",),
+        ("s_end",), ("r_end", "v"), ("r_end", "q"),
     ],
 }
-X_FIRST = {0, 1}
-Y_FIRST = {0, 3, 6, 7}
+Y_FIRST = {0, 1, 2, 3, 6}
 DIRECT = {0, 1, 2, 3, 4, 5, 6, 7}
-STRAIGHT = {1, 2, 4, 7}
+STRAIGHT = {3, 5, 7}
 
 
 def order_of(Z):
@@ -107,10 +109,10 @@
     plan = {
         "masks": [("w_out_z", 0), ("w_own_y", 0), ("w_own_x", 0), ("tr",), ("tl",), ("tp",), ("tc",)],
         "small": [("w_z", 0), ("w_m", 0), ("w_l", 0), ("gtokp",), ("w_c", 0)],
-        ("A", 0): [(step, g) for g in (1, 2) for step in ("w_out_z", "w_own_y", "w_own_x")],
-        ("B", 0): [("o_hi",), ("w_z", 1), ("w_z", 2), ("w_m", 1), ("w_m", 2)],
-        "merge": [("o_lo",), ("g_o",), ("w_l", 1), ("w_l", 2)],
-        "out": [("qtail",), ("w_c", 1), ("w_c", 2)],
+        ("A", 0): [(step, g) for g in range(1, 5) for step in ("w_out_z", "w_own_y", "w_own_x")],
+        ("B", 0): [("o_hi",)] + [(step, g) for step in ("w_z", "w_m") for g in range(1, 5)],
+        "merge": [("o_lo",), ("g_o",)] + [("w_l", g) for g in range(1, 5)],
+        "out": [("qtail",)] + [("w_c", g) for g in range(1, 5)],
         "dOc": [("g_ol",)],
         "dwu": [("dO",)],
         "sent": [("r_c", g) for g in most],
@@ -137,8 +139,8 @@
     cs, cu, cd, xs, xu, xd, ys, yu, yd, zs, zu, zd,
     crf, zrf, par, upb, qt, dot_, qs, dos, ot, mrun, dqt,
     oh, ol, ml, ohr, olr, mlr, gqs, gqr,
-    nrm2, hid, acc, gsec, dwkv, lacc, upg, xq,
-    sg, src, srx, sry, srz, tile, tok_ref, cot_ref, act_all, gpre_all, early,
+    nrm2, hid, acc, gsec, lacc, upg, xq,
+    sg, src, srx, sry, srz, tile, tok_ref, cot_ref, act_all, gpre_all, big,
     s_in,
     s_tz, s_tc, r_t, s_tp, r_tp,
     s_wz, r_wz, s_wy, r_wy, s_wx, r_wx, s_wc, r_wc,
@@ -181,6 +183,9 @@
 
     def d_f(ff):
         return (i, ff)
+
+    def fminus(k):
+        return lax.rem(f + FK - k, FK)
 
     def d_diag(ff):
         return dev(z, oy, c, ff)
@@ -230,7 +235,7 @@
 
     def tok_core(zz):
         t = tokb.at[zz, c]
-        push(t, t, s_tc.at[zz], r_t.at[zz, c], d_core)
+        push(t, t, s_tc, r_t.at[zz, c], d_core)
 
     def tok_right(zz):
         @pl.when(z < Z - 1)
@@ -257,28 +262,36 @@
             tok_left(zz)
             tok_core(zz)
 
-    wb = (w0, w1, w2)
-
-    x_first = X_FIRST
+    HF = FF // 2
+    everything = slice(None)
+    groups = (
+        (w0, everything, everything),
+        (w1, everything, slice(0, D + HF)),
+        (w1, everything, slice(D + HF, D + FF)),
+        (w2, slice(0, 2 * SLAB), everything),
+        (w2, slice(2 * SLAB, 4 * SLAB), everything),
+    )
+
+    def w_at(g, zz, yy, cc, ff):
+        where, rows, cols = groups[g]
+        return where.at[zz, yy, cc, ff, rows, cols]
 
     def w_push_x(g, zz, yy):
+        t = w_at(g, zz, yy, c, f)
         for k in range(1, FK):
-            ff = fplus(k)
-            t = wb[g].at[zz, yy, c, f]
-            push(t, t, s_wx.at[g, ff, zz, yy], r_wx.at[g, f, zz, yy], d_f(ff))
-
-    def w_push_y(g, zz, ff):
-        t = wb[g].at[zz, y, c, ff]
-        push(t, t, s_wy.at[g, zz, ff], r_wy.at[g, zz, ff], d_y)
+            push(t, t, s_wx.at[g, k - 1], r_wx.at[g, k - 1], d_f(fplus(k)))
+
+    def w_push_y(g, zz):
+        t = w_at(g, zz, y, c, f)
+        push(t, t, s_wy.at[g], r_wy.at[g, zz], d_y)
 
     def w_out_z(g):
-        t = wb[g].at[z, y, c, f]
+        t = w_at(g, z, y, c, f)
         for k in range(1, Z):
-            zz = zplus(k)
-            push(t, t, s_wz.at[g, zz], r_wz.at[g, z], d_z(zz))
+            push(t, t, s_wz.at[g], r_wz.at[g, z], d_z(zplus(k)))
 
     def w_own_y(g):
-        w_push_y(g, z, f)
+        w_push_y(g, z)
 
     def w_own_x(g):
         w_push_x(g, z, y)
@@ -286,55 +299,35 @@
     def w_z(g):
         for k in range(1, Z):
             zz = zplus(k)
-            got(wb[g].at[zz, y, c, f], r_wz.at[g, zz])
+            got(w_at(g, zz, y, c, f), r_wz.at[g, zz])
             w_push_x(g, zz, y)
-            w_push_y(g, zz, f)
-
-    def w_to_core(g, n):
-        if g in x_first:
-            t = wb[g].at[:, y if n == 0 else oy, c]
-        else:
-            t = wb[g].at[:, :, c, fplus(n)]
-        push(t, t, s_wc.at[g, n], r_wc.at[g, n], d_core)
+            w_push_y(g, zz)
+
+    def w_to_core(g, ff):
+        t = w_at(g, everything, everything, c, ff)
+        push(t, t, s_wc.at[g], r_wc.at[g], d_core)
 
     def w_m(g):
-        if g in x_first:
-            for zz in range(Z):
-                for k in range(1, FK):
-                    ff = fplus(k)
-                    got(wb[g].at[zz, y, c, ff], r_wx.at[g, ff, zz, y])
-                    w_push_y(g, zz, ff)
-        else:
-            for zz in range(Z):
-                got(wb[g].at[zz, oy, c, f], r_wy.at[g, zz, f])
-                w_push_x(g, zz, oy)
-        w_to_core(g, 0)
+        for zz in range(Z):
+            got(w_at(g, zz, oy, c, f), r_wy.at[g, zz])
+            w_push_x(g, zz, oy)
+        w_to_core(g, f)
 
     def w_l(g):
-        if g in x_first:
-            for zz in range(Z):
-                for ff in range(FK):
-                    got(wb[g].at[zz, oy, c, ff], r_wy.at[g, zz, ff])
-            w_to_core(g, 1)
-        else:
-            for k in range(1, FK):
-                ff = fplus(k)
-                for zz in range(Z):
-                    for yy in range(2):
-                        got(wb[g].at[zz, yy, c, ff], r_wx.at[g, ff, zz, yy])
-                w_to_core(g, k)
-
-    def w_parts(g):
-        return 2 if g in x_first else FK
+        for k in range(1, FK):
+            got(w_at(g, everything, everything, c, fminus(k)), r_wx.at[g, k - 1])
+            w_to_core(g, fminus(k))
 
     def w_c(g):
-        for n in range(w_parts(g)):
-            if g in x_first:
-                got(wb[g].at[:, y if n == 0 else oy, oc], r_wc.at[g, n])
-            else:
-                got(wb[g].at[:, :, oc, fplus(n)], r_wc.at[g, n])
-
-    HF = FF // 2
+        got(w_at(g, everything, everything, oc, everything), r_wc.at[g])
+
+    def w_sent(g):
+        sent(w_at(g, slice(0, Z - 1), y, c, f), s_wz.at[g])
+        sent(w_at(g, everything, y, c, f), s_wy.at[g])
+        for k in range(1, FK):
+            sent(w_at(g, everything, everything, c, f), s_wx.at[g, k - 1])
+        sent(w_at(g, everything, everything, c, everything), s_wc.at[g])
+
     store = (gs, gs, gs, gs, gu, gu, gd, gd)
     from_core = (cs, cs, cs, cs, cu, cu, cd, cd)
     from_x = (xs, xs, xs, xs, xu, xu, xd, xd)
@@ -344,20 +337,22 @@
     Q, K, V, O, UA, UB, DA, DB = range(8)
     y_first = {(Q, K, V, O, UA, UB, DA, DB)[t] for t in Y_FIRST}
     direct = {(Q, K, V, O, UA, UB, DA, DB)[t] for t in DIRECT}
+    slot = {g: n for n, g in enumerate(sorted(direct))}
     straight = {(Q, K, V, O, UA, UB, DA, DB)[t] for t in STRAIGHT}
 
     def r_c(g):
         n = lead[g]
-        push(store[g].at[n, :, :, oc], from_core[g].at[n], s_gc.at[g], r_gc.at[g], d_core)
+        push(store[g].at[n, :, :, oc], from_core[g].at[n], s_gc.at[(g > O) + (g > UB)], r_gc.at[g], d_core)
 
     def r_push_x(g, whole):
         n = lead[g]
         for k in range(1, FK):
             ff = fplus(k)
             if whole:
-                push(store[g].at[n, :, :, c, ff], from_x[g].at[n, f], s_gx.at[g, ff], r_gx.at[g, f], d_f(ff))
+                push(store[g].at[n, :, :, c, ff], from_x[g].at[n, f], s_gx.at[g, k - 1], r_gx.at[g, k - 1], d_f(ff))
             else:
-                push(store[g].at[n, :, y, c, ff], from_x[g].at[n, f, :, 0], s_gx.at[g, ff], r_gx.at[g, f], d_f(ff))
+                t = store[g].at[n, :, y, c, ff]
+                push(t, from_x[g].at[n, f, :, 0], s_gx.at[g, k - 1], r_gx.at[g, k - 1], d_f(ff))
 
     def r_push_y(g, whole):
         n = lead[g]
@@ -388,7 +383,7 @@
             for k in range(1, FK):
                 ff = fplus(k)
                 t = store[g].at[n, :, oy, c, ff]
-                push(t, from_x[g].at[n, f, :, 1], s_gd.at[g, ff], r_gd.at[g, f], d_diag(ff))
+                push(t, from_x[g].at[n, f, :, 1], s_gd.at[slot[g], k - 1], r_gd.at[slot[g], k - 1], d_diag(ff))
         elif g in y_first:
             r_push_y(g, True)
         else:
@@ -409,7 +404,7 @@
             r_push_x(g, False)
         else:
             for k in range(1, FK):
-                got(from_x[g].at[n, fplus(k)], r_gx.at[g, fplus(k)])
+                got(from_x[g].at[n, fminus(k)], r_gx.at[g, k - 1])
 
             def one(zz):
                 t = store[g][n, zz, :, c, f].astype(F32)
@@ -426,8 +421,8 @@
         if g in direct:
             got(from_y[g].at[n, :, 0], r_gy.at[g])
             for k in range(1, FK):
-                got(from_x[g].at[n, fplus(k), :, 0], r_gx.at[g, fplus(k)])
-                got(from_x[g].at[n, fplus(k), :, 1], r_gd.at[g, fplus(k)])
+                got(from_x[g].at[n, fminus(k), :, 0], r_gx.at[g, k - 1])
+                got(from_x[g].at[n, fminus(k), :, 1], r_gd.at[slot[g], k - 1])
 
             def one(zz):
                 t = store[g][n, zz, y, c, f].astype(F32) + from_y[g][n, zz, 0].astype(F32)
@@ -438,7 +433,7 @@
             over_z(one)
         elif g in y_first:
             for k in range(1, FK):
-                got(from_x[g].at[n, fplus(k), :, 0], r_gx.at[g, fplus(k)])
+                got(from_x[g].at[n, fminus(k), :, 0], r_gx.at[g, k - 1])
 
             def one(zz):
                 t = store[g][n, zz, y, c, f].astype(F32)
@@ -459,7 +454,7 @@
         if g in straight:
             for k in range(1, Z):
                 zz = zplus(k)
-                push(store[g].at[n, zz, y, c, f], from_z[g].at[n, z], s_gz.at[g, zz], r_gz.at[g, z], d_z(zz))
+                push(store[g].at[n, zz, y, c, f], from_z[g].at[n, z], s_gz.at[g], r_gz.at[g, 0], d_z(zz))
         else:
             r_fold(g, 1)
 
@@ -468,16 +463,16 @@
         for m in range(bit, Z, 2 * bit):
             push(
                 store[g].at[n, zxor(m), y, c, f], from_z[g].at[n, zxor(bit ^ (m - 1))],
-                s_gz.at[g, zxor(m)], r_gz.at[g, zxor(bit ^ (m - 1))], d_z(zxor(bit)),
+                s_gz.at[g], r_gz.at[g, bit.bit_length() - 1], d_z(zxor(bit)),
             )
 
     def r_zz(g):
         n = lead[g]
         bit = 1
         while g not in straight and 2 * bit < Z:
+            got(from_z[g].at[n, 0 : Z // (2 * bit)], r_gz.at[g, bit.bit_length() - 1])
             for m in range(0, Z, 2 * bit):
                 zz, at = zxor(m), zxor(m + bit - 1)
-                got(from_z[g].at[n, at], r_gz.at[g, at])
                 t = store[g][n, zz, y, c, f].astype(F32) + from_z[g][n, at].astype(F32)
                 store[g][n, zz, y, c, f] = t.astype(BF16)
             bit *= 2
@@ -487,13 +482,12 @@
         n = lead[g]
         t = store[g][n, z, y, c, f].astype(F32)
         if g in straight:
+            got(from_z[g].at[n, 0 : Z - 1], r_gz.at[g, 0])
             for k in range(1, Z):
-                zz = zplus(k)
-                got(from_z[g].at[n, zz], r_gz.at[g, zz])
-                t = t + from_z[g][n, zz].astype(F32)
+                t = t + from_z[g][n, zplus(k)].astype(F32)
         else:
             at = zxor(Z // 2 - 1)
-            got(from_z[g].at[n, at], r_gz.at[g, at])
+            got(from_z[g].at[n, at], r_gz.at[g, (Z // 2).bit_length() - 1])
             t = t + from_z[g][n, at].astype(F32)
         if g <= V:
             gqkv_ref[:, g * D : (g + 1) * D] = t
@@ -503,24 +497,23 @@
             gup_ref[:, (g - UA) * HF : (g - UA + 1) * HF] = t
         else:
             gdown_ref[(g - DA) * 2 * SLAB : (g - DA + 1) * 2 * SLAB, :] = t
+        r_sent(g)
 
     def r_sent(g):
         n = lead[g]
-        sent(store[g].at[n, :, :, oc], s_gc.at[g])
         for k in range(1, FK):
             ff = fplus(k)
             if g in y_first or g in direct:
-                sent(store[g].at[n, :, y, c, ff], s_gx.at[g, ff])
+                sent(store[g].at[n, :, y, c, ff], s_gx.at[g, k - 1])
             else:
-                sent(store[g].at[n, :, :, c, ff], s_gx.at[g, ff])
+                sent(store[g].at[n, :, :, c, ff], s_gx.at[g, k - 1])
             if g in direct:
-                sent(store[g].at[n, :, oy, c, ff], s_gd.at[g, ff])
+                sent(store[g].at[n, :, oy, c, ff], s_gd.at[slot[g], k - 1])
         if g in y_first and g not in direct:
             sent(store[g].at[n, :, oy, c], s_gy.at[g])
         else:
             sent(store[g].at[n, :, oy, c, f], s_gy.at[g])
-        for k in range(1, Z):
-            sent(store[g].at[n, zplus(k), y, c, f], s_gz.at[g, zplus(k)])
+        sent(store[g].at[n, 0 : Z - 1, y, c, f], s_gz.at[g])
 
     turns = sorted(range(1, Z), key=lambda m: (m & -m, m)) + [0]
 
@@ -547,7 +540,7 @@
         bit = m & -m
         zz, at = zxor(m), zxor(bit ^ (m - 1))
         tokb[zz, c] = p_sum(m).astype(BF16)
-        push(tokb.at[zz, c], zrf.at[at], s_pz.at[zz], r_pz.at[at], d_z(zxor(bit)))
+        push(tokb.at[zz, c], zrf.at[at], s_pz, r_pz.at[at], d_z(zxor(bit)))
 
     def queries_back():
         push(gqs, gqr, s_y.at[5], r_y.at[5], d_y)
@@ -559,14 +552,13 @@
         got(src, r_sc)
         sg[1] = sg[0] + src[...]
         for k in range(1, FK):
-            ff = fplus(k)
-            push(sg.at[1], srx.at[f], s_sx.at[ff], r_sx.at[f], d_f(ff))
+            push(sg.at[1], srx.at[f], s_sx.at[k - 1], r_sx.at[k - 1], d_f(fplus(k)))
 
     def sums_x():
         t = sg[1]
         for k in range(1, FK):
-            got(srx.at[fplus(k)], r_sx.at[fplus(k)])
-            t = t + srx[fplus(k)]
+            got(srx.at[fminus(k)], r_sx.at[k - 1])
+            t = t + srx[fminus(k)]
         sg[2] = t
         push(sg.at[2], sry, s_sy, r_sy, d_y)
 
@@ -575,17 +567,27 @@
         sg[3] = sg[2] + sry[...]
         for k in range(1, Z):
             zz = zplus(k)
-            push(sg.at[3], srz.at[z], s_sz.at[zz], r_sz.at[z], d_z(zz))
+            push(sg.at[3], srz.at[z], s_sz, r_sz, d_z(zz))
 
     def sums_z():
+        sent(sg.at[0], s_sc)
+        for k in range(1, FK):
+            sent(sg.at[1], s_sx.at[k - 1])
+        sent(sg.at[2], s_sy)
+        sent(srz.at[0 : Z - 1], s_sz)
         t = sg[3]
+        got(srz.at[0 : Z - 1], r_sz)
         for k in range(1, Z):
-            zz = zplus(k)
-            got(srz.at[zz], r_sz.at[zz])
-            t = t + srz[zz]
+            t = t + srz[zplus(k)]
         gsm_ref[...] = t
 
     def first():
+        for n, t in enumerate((gs, gu, gd)):
+            sent(t.at[:, :, :, oc], s_gc.at[n])
+        sent(tokb.at[:, oc], s_pc)
+        sent(tokb.at[0 : Z - 1, c], s_pz)
+        sent(dot_.at[:, grows, near_half], s_y.at[4])
+        sent(gqs, s_y.at[5])
         got(gqr, r_y.at[5])
         t = p_sum(0) + acc[...] + gqr[...].astype(F32)
         mean, centered, rstd = moments(tok_ref[...].astype(F32))
@@ -814,27 +816,33 @@
     acc[...] = hidden + par[7:8, :]
     gsec[...] = jnp.zeros((R, D), F32)
 
-    def chunk(j, carry):
+    def slope_at(j):
+        hh = j // (Z // 2)
+        return pl.ds(pl.multiple_of(hh * R, R), R), pl.ds(pl.multiple_of((j - hh * (Z // 2)) * CH, 128), CH)
+
+    def forward(j, carry):
         cols = pl.ds(pl.multiple_of(D + j * CH, 128), CH)
         bcols = pl.ds(pl.multiple_of(j * CH, 128), CH)
-        up = w1[:, :, :, :, :, cols].reshape(D, CH)
-        down = w2[j].reshape(CH, D)
-        pre = dot_nn(nrm2[...], up) + upb[:, bcols]
+        pre = dot_nn(nrm2[...], w1[:, :, :, :, :, cols].reshape(D, CH)) + upb[:, bcols]
         phi = 0.5 * (1.0 + lax.erf(pre * (0.5**0.5)))
-        act = (pre * phi).astype(BF16)
+        act_all[:, bcols] = (pre * phi).astype(BF16)
         slope = phi + pre * (jnp.exp2(pre * pre * (-0.5 / LN2)) * ((2.0 * math.pi) ** -0.5))
-        acc[...] += dot_nn(act, down)
-        gpre = (dot_nt(cot_ref[...], down) * slope).astype(BF16)
-        gsec[...] += dot_nt(gpre, up)
-        upg[:, bcols] = col_sum(gpre.astype(F32))
-        act_all[:, bcols] = act
+        big[1, *slope_at(j)] = slope
+        return carry
+
+    def backward(j, carry):
+        cols = pl.ds(pl.multiple_of(D + j * CH, 128), CH)
+        bcols = pl.ds(pl.multiple_of(j * CH, 128), CH)
+        gpre = (dot_nt(cot_ref[...], w2[j].reshape(CH, D)) * big[1, *slope_at(j)]).astype(BF16)
+        gsec[...] += dot_nt(gpre, w1[:, :, :, :, :, cols].reshape(D, CH))
         gpre_all[:, bcols] = gpre
         return carry
 
     do("ffn")
-    lax.fori_loop(0, Z, chunk, 0)
+    lax.fori_loop(0, Z, forward, 0)
+    do("ffd")
+    lax.fori_loop(0, Z, backward, 0)
     do("ln2")
-    out_ref[...] = acc[...].astype(BF16)
 
     g_second = gsec[...]
     n2 = (hid[...] - mean2) * rstd2
@@ -863,11 +871,13 @@
         bcols = pl.ds(pl.multiple_of(j * CH, 128), CH)
         t = dot_tn(nrm2[...], gpre_all[:, bcols]).astype(BF16).reshape(Z, 2, 2, FK, SLAB, CH)
         hh = j // (Z // 2)
+        upg[:, bcols] = col_sum(gpre_all[:, bcols].astype(F32))
         gu[hh, :, :, :, :, :, pl.ds(pl.multiple_of((j - hh * (Z // 2)) * CH, 128), CH)] = t
         return carry
 
     def g_down(j, carry):
         bcols = pl.ds(pl.multiple_of(j * CH, 128), CH)
+        acc[...] += dot_nn(act_all[:, bcols], w2[j].reshape(CH, D))
         t = dot_tn(act_all[:, bcols], cot_ref[...]).astype(BF16).reshape(2, 2, FK, 4 * SLAB, D)
         gd[0, j] = t[:, :, :, 0 : 2 * SLAB]
         gd[1, j] = t[:, :, :, 2 * SLAB : 4 * SLAB]
@@ -877,6 +887,7 @@
     lax.fori_loop(0, Z, g_up, 0)
     do("dwd")
     lax.fori_loop(0, Z, g_down, 0)
+    out_ref[...] = acc[...].astype(BF16)
     do("dwo")
     gs[O] = dot_tn(attn_low, g_branch).astype(BF16).reshape(Z, 2, 2, FK, SLAB, D)
     zero = jnp.zeros((1, D), F32)
@@ -890,7 +901,6 @@
         sg[0, 8 + r : 9 + r, :] = upg[:, r * D : (r + 1) * D]
 
     dqt[...] = jnp.zeros((H, HD, 2 * R), F32)
-    dwkv[...] = jnp.zeros((D, 2 * D), F32)
     lacc[...] = jnp.zeros((3, 8, D), F32)
 
     def tok_sent():
@@ -908,8 +918,7 @@
                 def _():
                     sent(tokb.at[z + k, c], s_tz.at[1, z + k])
 
-        for zz in range(Z):
-            sent(tokb.at[zz, c], s_tc.at[zz])
+        sent(tokb.at[:, c], s_tc)
         sent(tokb.at[z, c], s_tp)
 
     def heads(zz, span):
@@ -932,22 +941,22 @@
         gp = dot_nt(dkv, w0[:, :, :, :, :, D : 3 * D].reshape(D, 2 * D))
         norm = (tokb[zz].reshape(2 * R, D).astype(F32) - stat[zz, :, 0:1]) * stat[zz, :, 1:2]
         tokb[zz] = gp.astype(BF16).reshape(2, R, D)
-        push(tokb.at[zz, oc], crf.at[zz], s_pc.at[zz], r_pc.at[zz], d_core)
+        push(tokb.at[zz, oc], crf.at[zz], s_pc, r_pc.at[zz], d_core)
         x = (norm * par[0:1, :] + par[1:2, :]).astype(BF16)
         lacc[0] += fold_rows(gp * norm)
         lacc[1] += fold_rows(gp)
         lacc[2] += fold_rows(dkv32[:, D : 2 * D])
-        dwkv[...] += dot_tn(x, dkv)
+        big[0] = jnp.where(n == 0, 0.0, big[0]) + dot_tn(x, dkv)
 
     def behind_early(n, carry):
         run("e", n)
-        early[n] = heads(plane(n), near_half)
+        big[n] = heads(plane(n), near_half)
         return carry
 
     def behind_far(n, carry):
         run("h", n)
         zz = plane(n)
-        rest(n, zz, early[n] + heads(zz, far_half))
+        rest(n, zz, big[n] + heads(zz, far_half))
         return carry
 
     def behind(n, carry):
@@ -958,7 +967,13 @@
 
     do("sent")
     tok_sent()
-    E = early.shape[0] if Z == 4 else 0
+    for g in range(len(groups)):
+        w_sent(g)
+    sent(oh, s_y.at[0])
+    sent(ml, s_y.at[1])
+    sent(ol, s_y.at[2])
+    sent(qt.at[:, qrows, near_half], s_y.at[3])
+    E = big.shape[0] if Z == 4 else 0
     if E:
         lax.fori_loop(0, E, behind_early, 0)
     do("dosT")
@@ -969,8 +984,8 @@
     lax.fori_loop(E, Z, behind, 0)
 
     do("kv")
-    gs[K] = dwkv[:, 0:D].astype(BF16).reshape(Z, 2, 2, FK, SLAB, D)
-    gs[V] = dwkv[:, D : 2 * D].astype(BF16).reshape(Z, 2, 2, FK, SLAB, D)
+    gs[K] = big[0, :, 0:D].astype(BF16).reshape(Z, 2, 2, FK, SLAB, D)
+    gs[V] = big[0, :, D : 2 * D].astype(BF16).reshape(Z, 2, 2, FK, SLAB, D)
 
     def queries():
         dq = jnp.concatenate([(dqt[h] * (HD**-0.5)).T for h in range(H)], axis=1).astype(BF16)
@@ -989,45 +1004,12 @@
     queries()
     do("end")
 
-    for g in range(3):
-        for k in range(1, Z):
-            sent(wb[g].at[z, y, c, f], s_wz.at[g, zplus(k)])
-        for zz in range(Z):
-            sent(wb[g].at[zz, y, c, f], s_wy.at[g, zz, f])
-            for k in range(1, FK):
-                ff = fplus(k)
-                sent(wb[g].at[zz, y, c, f], s_wx.at[g, ff, zz, y])
-                if g in x_first:
-                    sent(wb[g].at[zz, y, c, ff], s_wy.at[g, zz, ff])
-                else:
-                    sent(wb[g].at[zz, oy, c, f], s_wx.at[g, ff, zz, oy])
-        for n in range(w_parts(g)):
-            if g in x_first:
-                sent(wb[g].at[:, y if n == 0 else oy, c], s_wc.at[g, n])
-            else:
-                sent(wb[g].at[:, :, c, fplus(n)], s_wc.at[g, n])
-    for g in range(8):
-        r_sent(g)
-    for zz in range(Z):
-        sent(tokb.at[zz, oc], s_pc.at[zz])
-    for k in range(1, Z):
-        sent(tokb.at[zplus(k), c], s_pz.at[zplus(k)])
-        sent(sg.at[3], s_sz.at[zplus(k)])
-    sent(oh, s_y.at[0])
-    sent(ml, s_y.at[1])
-    sent(ol, s_y.at[2])
-    sent(qt.at[:, HD : HD + SLAB, 0:R], s_y.at[3])
-    sent(dot_.at[:, 0 : HD + SLAB, 0:R], s_y.at[4])
-    sent(gqs, s_y.at[5])
-    sent(sg.at[0], s_sc)
-    for k in range(1, FK):
-        sent(sg.at[1], s_sx.at[fplus(k)])
-    sent(sg.at[2], s_sy)
-
 
 def layer(Z, FK, R, D, FF, NT, operands):
     vm = lambda shape, dtype: pltpu.VMEM(shape, dtype)
     dma = lambda *shape: pltpu.SemaphoreType.DMA(shape)
+    one = pltpu.SemaphoreType.DMA
+    others = max(FK - 1, 1)
     lead = (Z, 2, 2, FK)
     slabs = ((SLAB, 3 * D + 128), (SLAB, D + FF), (4 * SLAB, D))
     gslabs = ((4, SLAB, D), (2, SLAB, FF // 2), (2, 2 * SLAB, D))
@@ -1067,7 +1049,6 @@
         vm((R, D), F32),
         vm((R, D), F32),
         vm((R, D), F32),
-        vm((D, 2 * D), F32),
         vm((3, 8, D), F32),
         vm((1, FF), F32),
         vm((2 * R, D), BF16),
@@ -1081,17 +1062,14 @@
         vm((R, D), BF16),
         vm((R, FF), BF16),
         vm((R, FF), BF16),
-        vm((2, 2 * R, 2 * D) if Z == 4 else (1, 8, 128), F32),
+        vm((3 if Z == 4 else 2, 2 * R, 2 * D), F32),
         dma(7),
-        dma(2, Z), dma(Z), dma(Z, 2), pltpu.SemaphoreType.DMA, pltpu.SemaphoreType.DMA,
-        dma(3, Z), dma(3, Z), dma(3, Z, FK), dma(3, Z, FK),
-        dma(3, FK, Z, 2), dma(3, FK, Z, 2), dma(3, 2), dma(3, 2),
-        dma(8), dma(8), dma(8, FK), dma(8, FK), dma(8), dma(8), dma(8, FK), dma(8, FK), dma(8, Z), dma(8, Z),
-        dma(Z), dma(Z), dma(Z), dma(Z), dma(6), dma(6),
-        pltpu.SemaphoreType.DMA, pltpu.SemaphoreType.DMA,
-        dma(FK), dma(FK),
-        pltpu.SemaphoreType.DMA, pltpu.SemaphoreType.DMA,
-        dma(Z), dma(Z),
+        dma(2, Z), one, dma(Z, 2), one, one,
+        dma(5), dma(5, Z), dma(5), dma(5, Z), dma(5, others), dma(5, others), dma(5), dma(5),
+        dma(3), dma(8), dma(8, others), dma(8, others), dma(8), dma(8),
+        dma(max(len(DIRECT), 1), others), dma(max(len(DIRECT), 1), others), dma(8), dma(8, Z.bit_length() - 1),
+        one, dma(Z), one, dma(Z), dma(6), dma(6),
+        one, one, dma(others), dma(others), one, one, one, one,
     ]
     vmem = pl.BlockSpec(memory_space=pltpu.VMEM)
     smem = pl.BlockSpec(memory_space=pltpu.SMEM)

time: 118 us -> 117 us (level)
    pallas_call x1, Pallas kernels: 115 us -> 113 us  [layer(): pl.pallas_call(functools.partial(body, Z, FK, R, D, NT), out_shape=(shape...]
where the time goes in v5:
time: 117 us; the launch traced here: 116 us
  Pallas kernels  116 us (99%)
    pallas_call x1, Pallas kernels, layer(): pl.pallas_call(functools.partial(body, Z, FK, R, D, NT), out_shape=(shape...  113 us

profile of v5, /device:TPU:0, one launch (start us, length us, event | category | flops | bytes accessed | tf_op | source)
XLA Modules:
  0.0 116.4 jit_solution(14480315455642556775)
XLA Ops:
  0.7 113.4 %layer.1 = (bf16[256,512]{1,0:T(8,128)(2,1)}, bf16[256,512]{1,0:T(8,128)(2,1)}, f32[16,1536]{1,0:T(8,128)}, f32[16,512]{1,0:T(8,128)}, f32[16,2048]{1,0:T(8,128)}, /*index=5*/f32[64,512]{1,0:T(8,128)}, f32[16,512]{1,0:T(8,128)}) custom-call(bf16[256,512]{1,0:T(8,128)(2,1)} %bitcast.22, bf16[256,512]{1,0:T(8,128)(2,1)} %bitcast.23, bf16[16,1536]{1,0:T(8,128)(2,1)} %wq_in.1, ...), custom_call_target="tpu_custom_call" | custom-call | tf_op jit(solution)/shard_map/layer/pallas_call | solution.py:1077
  114.0 2.2 %finish.1 = (bf16[256,512]{1,0:T(8,128)(2,1)}, bf16[256,512]{1,0:T(8,128)(2,1)}, f32[16,1536]{1,0:T(8,128)}, f32[16,512]{1,0:T(8,128)}, f32[16,2048]{1,0:T(8,128...) custom-call(bf16[256,512]{1,0:T(8,128)(2,1)} %get-tuple-element.37.r, ...), custom_call_target="tpu_custom_call" | custom-call | tf_op jit(solution)/shard_map/finish/pallas_call | solution.py:1126

commit v6 on v5

--- a/solution.py
+++ b/solution.py
@@ -1077,13 +1077,13 @@
     return pl.pallas_call(
         functools.partial(body, Z, FK, R, D, NT),
         out_shape=(
-            shape((R, D), BF16),
-            shape((R, D), BF16),
-            shape((SLAB, 3 * D), F32),
-            shape((SLAB, D), F32),
-            shape((SLAB, FF), F32),
-            shape((4 * SLAB, D), F32),
-            shape((SLAB, D), F32),
+            pltpu.VMEM((R, D), BF16),
+            pltpu.VMEM((R, D), BF16),
+            pltpu.VMEM((SLAB, 3 * D), F32),
+            pltpu.VMEM((SLAB, D), F32),
+            pltpu.VMEM((SLAB, FF), F32),
+            pltpu.VMEM((4 * SLAB, D), F32),
+            pltpu.VMEM((SLAB, D), F32),
         ),
         in_specs=[pl.BlockSpec(memory_space=pl.ANY)] * 6 + [vmem] * 9 + [smem] * 2,
         out_specs=[vmem] * 7,
@@ -1133,7 +1133,7 @@
         in_specs=[vmem] * 7,
         out_specs=[vmem] * 15,
         name="finish",
-    )(*results)
+    )(*[pltpu.with_memory_space_constraint(v, pltpu.VMEM) for v in results])
 
 
 def shards(

time: 117 us -> 114 us (0.974)
  Pallas kernels: 116 us -> 113 us
    pallas_call x1, Pallas kernels: 2.22 us -> 1.03 us  [hand_over(): pl.pallas_call(functools.partial(finish, NSH, FK), out_shape=(*[shape(v.s...]
where the time goes in v6:
time: 114 us
  Pallas kernels  113 us (99%)
    pallas_call x1, Pallas kernels, layer(): pl.pallas_call(functools.partial(body, Z, FK, R, D, NT), out_shape=(pltpu...  112 us

profile of v6, /device:TPU:0, one launch (start us, length us, event | category | flops | bytes accessed | tf_op | source)
XLA Modules:
  0.0 114.2 jit_solution(2515392317098569199)
XLA Ops:
  0.7 112.4 %layer.1 = (bf16[256,512]{1,0:T(8,128)(2,1)S(1)}, bf16[256,512]{1,0:T(8,128)(2,1)S(1)}, f32[16,1536]{1,0:T(8,128)S(1)}, f32[16,512]{1,0:T(8,128)S(1)}, f32[16,20...) custom-call(bf16[256,512]{1,0:T(8,128)(2,1)} %bitcast.22, bf16[256,512]{1,0:T(8,128)(2,1)} %bitcast.23, ...), custom_call_target="tpu_custom_call" | custom-call | tf_op jit(solution)/shard_map/layer/pallas_call | solution.py:1077
  113.0 1.0 finish.1

commit v7 on v6

--- a/solution.py
+++ b/solution.py
@@ -59,46 +59,46 @@
 
 
 FOUR = {
-    "masks": [("w_out_z", 0), ("tc",), ("w_own_y", 0), ("tp",), ("w_own_x", 2), ("w_own_x", 1), ("tl",), ("tr",)],
+    "masks": [
+        ("w_out_z", 0), ("w_own_x", 2), ("w_own_y", 0), ("tr",), ("w_out_z", 1), ("tl",), ("tp",), ("w_out_z", 2),
+    ],
     "small": [
-        ("w_z", 0), ("w_own_x", 4), ("w_out_z", 1), ("tok_z", 1), ("w_m", 0), ("gtokp",), ("w_own_x", 0), ("w_z", 1),
-        ("w_own_y", 1), ("w_own_y", 4), ("w_out_z", 2), ("w_own_y", 2), ("w_l", 0), ("w_m", 1), ("tok_z", 2),
-        ("w_own_y", 3), ("w_c", 0),
+        ("w_z", 0), ("tc",), ("w_own_x", 0), ("w_m", 0), ("w_own_y", 1), ("w_own_y", 4), ("gtokp",), ("w_z", 1),
+        ("tok_z", 1), ("w_l", 0), ("w_m", 1), ("w_z", 2), ("w_own_y", 3), ("w_own_y", 2), ("w_c", 0), ("w_own_x", 3),
+        ("w_out_z", 4),
     ],
-    ("A", 0): [("w_out_z", 4), ("w_z", 2), ("w_out_z", 3), ("w_own_x", 3)],
-    ("A", 2): [("w_l", 1), ("w_m", 2)],
-    ("A", 3): [("tok_z", 3), ("w_z", 4)],
-    "osplit": [("w_z", 3), ("w_m", 4), ("w_l", 2)],
+    ("A", 0): [("w_own_x", 1), ("w_own_x", 4), ("tok_z", 2)],
+    ("A", 1): [("w_z", 4), ("w_m", 2), ("w_out_z", 3)],
+    ("A", 3): [("tok_z", 3), ("w_l", 1), ("w_m", 4), ("w_z", 3)],
     ("B", 0): [("o_hi",)],
-    ("B", 1): [("w_m", 3)],
-    ("B", 3): [("w_c", 1), ("w_l", 4)],
-    "merge": [("w_l", 3), ("o_lo",), ("g_o",), ("w_c", 4)],
-    "ffn": [("w_c", 2)],
-    "ffd": [("w_c", 3)],
-    "dOc": [("qtail",), ("g_ol",)],
+    ("B", 1): [("o_lo",)],
+    ("B", 2): [("w_m", 3), ("w_l", 4), ("w_l", 2)],
+    "merge": [("w_c", 2), ("w_c", 1), ("w_l", 3), ("w_c", 4), ("g_o",)],
+    "out": [("qtail",)],
+    "ffn": [("w_c", 3)],
+    "dOc": [("g_ol",)],
     "dwu": [("dO",)],
-    "sent": [("r_c", "ub")],
-    ("e", 2): [("r_1", "ub"), ("r_2", "ub")],
-    "dosT": [("r_c", "o"), ("g_dO",)],
-    ("h", 0): [("r_c", "db")],
-    ("h", 1): [("r_1", "o"), ("r_2", "o"), ("p_z", 0), ("r_c", "da")],
-    ("t", 1): [("r_1", "db")],
-    ("h", 2): [("r_z", "ub"), ("r_1", "da"), ("r_c", "ua")],
-    ("t", 2): [("r_2", "db"), ("p_z", 1), ("r_1", "ua")],
-    ("h", 3): [("r_z", "o"), ("r_z", "db")],
-    "kv": [("r_2", "da")],
-    "q": [("r_c", "v"), ("p_z", 2), ("r_1", "v"), ("r_zz", "ub"), ("r_c", "k"), ("r_2", "ua")],
+    "dwd": [("r_c", "ub")],
+    "sent": [("r_1", "ub"), ("r_c", "db")],
+    "dosT": [("r_1", "db"), ("g_dO",), ("r_2", "ub")],
+    ("h", 1): [("r_c", "ua")],
+    ("t", 1): [("r_2", "db"), ("r_c", "o"), ("r_z", "ub")],
+    ("h", 2): [("r_zz", "ub"), ("r_1", "ua"), ("p_z", 1)],
+    ("t", 2): [("r_c", "da"), ("r_z", "db"), ("p_z", 0)],
+    ("h", 3): [("r_1", "da"), ("r_1", "o"), ("r_zz", "db")],
+    "kv": [("r_2", "ua"), ("p_z", 2)],
+    "q": [("r_2", "da"), ("r_c", "v"), ("r_c", "k")],
     "end": [
-        ("r_zz", "db"), ("s", 0), ("r_1", "k"), ("s", 1), ("r_c", "q"), ("r_z", "da"), ("r_2", "k"), ("r_z", "ua"),
-        ("r_2", "v"), ("r_end", "ub"), ("r_1", "q"), ("r_zz", "o"), ("r_zz", "da"), ("r_end", "db"), ("s", 2),
-        ("r_z", "k"), ("r_2", "q"), ("gq",), ("r_z", "v"), ("r_zz", "ua"), ("r_z", "q"), ("r_zz", "k"), ("s", 3),
-        ("r_zz", "v"), ("r_end", "ua"), ("r_end", "o"), ("r_zz", "q"), ("r_end", "da"), ("r_end", "k"), ("first",),
-        ("s_end",), ("r_end", "v"), ("r_end", "q"),
+        ("r_1", "v"), ("r_1", "k"), ("r_2", "o"), ("r_c", "q"), ("r_z", "ua"), ("r_1", "q"), ("s", 0), ("r_z", "da"),
+        ("r_end", "db"), ("s", 1), ("r_2", "v"), ("r_z", "o"), ("r_zz", "o"), ("r_2", "k"), ("r_zz", "da"), ("s", 2),
+        ("r_2", "q"), ("r_end", "ub"), ("r_z", "k"), ("gq",), ("r_zz", "ua"), ("r_z", "v"), ("r_z", "q"), ("s", 3),
+        ("r_zz", "v"), ("r_end", "ua"), ("r_zz", "k"), ("r_zz", "q"), ("r_end", "da"), ("r_end", "o"), ("first",),
+        ("r_end", "v"), ("r_end", "k"), ("s_end",), ("r_end", "q"),
     ],
 }
-Y_FIRST = {0, 1, 2, 3, 6}
-DIRECT = {0, 1, 2, 3, 4, 5, 6, 7}
-STRAIGHT = {3, 5, 7}
+Y_FIRST = {0, 2, 5, 6, 7}
+DIRECT = {0, 1, 3, 4, 5, 6, 7}
+STRAIGHT = {3, 5, 6, 7}
 
 
 def order_of(Z):

time: 114 us -> 111 us (0.974)
  Pallas kernels: 113 us -> 111 us
    pallas_call x1, Pallas kernels: 112 us -> 109 us  [layer(): pl.pallas_call(functools.partial(body, Z, FK, R, D, NT), out_shape=(pltpu...]
where the time goes in v7:
time: 111 us
  Pallas kernels  111 us (100%)
    pallas_call x1, Pallas kernels, layer(): pl.pallas_call(functools.partial(body, Z, FK, R, D, NT), out_shape=(pltpu...  109 us

profile of v7, /device:TPU:0, one launch (start us, length us, event | category | flops | bytes accessed | tf_op | source)
XLA Modules:
  0.0 111.3 jit_solution(11444079179425066892)
XLA Ops:
  0.7 109.5 %layer.1 = (bf16[256,512]{1,0:T(8,128)(2,1)S(1)}, bf16[256,512]{1,0:T(8,128)(2,1)S(1)}, f32[16,1536]{1,0:T(8,128)S(1)}, f32[16,512]{1,0:T(8,128)S(1)}, f32[16,20...) custom-call(bf16[256,512]{1,0:T(8,128)(2,1)} %bitcast.22, bf16[256,512]{1,0:T(8,128)(2,1)} %bitcast.23, ...), custom_call_target="tpu_custom_call" | custom-call | tf_op jit(solution)/shard_map/layer/pallas_call | solution.py:1077
  110.1 1.0 finish.1

commit v8 on v7

--- a/solution.py
+++ b/solution.py
@@ -14,6 +14,7 @@
 EPSILON = 1e-05
 MASKED = -1e30
 LN2 = math.log(2.0)
+BINARY = HD ** (-0.5) / LN2
 MESH = pl.DeviceIdType.MESH
 F32 = jnp.float32
 BF16 = jnp.bfloat16
@@ -728,8 +729,7 @@
     mean, centered, rstd = moments(tokp[...].astype(F32))
     xq[R : 2 * R, :] = (centered * rstd * ln1g + ln1b).astype(BF16)
     wq = w0[:, :, :, :, :, 0:D].reshape(D, D)
-    qscale = HD ** (-0.5) / LN2
-    qs[...] = ((dot_nn(xq[...], wq) + par[2:3, :]) * qscale).astype(BF16)
+    qs[...] = (dot_nn(xq[...], wq) + par[2:3, :]).astype(BF16)
     for h in range(H):
         qt[h, 0:HD, :] = qs[:, h * HD : (h + 1) * HD].T
 
@@ -742,7 +742,7 @@
 
     def attend(h, keys, values, extra, span):
         cols = slice(h * HD, (h + 1) * HD)
-        s = dot_nn(jnp.concatenate([keys[:, cols], extra], axis=1), qt[h, :, span])
+        s = dot_nn(jnp.concatenate([keys[:, cols], extra], axis=1), qt[h, :, span]) * BINARY
         top0 = mrun[h, :, span]
         top = jnp.maximum(top0, jnp.ceil(jnp.max(s, axis=0, keepdims=True)))
         e = jnp.exp2(s - top).astype(BF16)
@@ -801,8 +801,8 @@
         parts.append(attended.T.astype(BF16))
         m1, m2, m3 = three_terms(top)
         tail = jnp.where(
-            row_tail == NT, -m1,
-            jnp.where(row_tail == NT + 1, -m2, jnp.where(row_tail == NT + 2, -m3, onehot[0:SLAB, 0:R])),
+            row_tail == NT + 3, m1,
+            jnp.where(row_tail == NT + 4, m2, jnp.where(row_tail == NT + 5, m3, onehot[0:SLAB, 0:R])),
         )
         qt[h, HD : HD + SLAB, 0:R] = tail.astype(BF16)
     do("out")
@@ -926,12 +926,15 @@
         dks, dvs = [], []
         for h in range(H):
             cols = slice(h * HD, (h + 1) * HD)
-            s = dot_nn(jnp.concatenate([keys[:, cols], extra], axis=1), qt[h, :, span])
+            s = dot_nn(jnp.concatenate([keys[:, cols], extra], axis=1), qt[h, :, span]) * BINARY
+            tail = qt[h, HD : HD + SLAB, span].astype(F32)
+            at = lax.broadcasted_iota(jnp.int32, tail.shape, 0)
+            top = col_sum(jnp.where((at >= NT + 3) & (at < NT + 6), tail, 0.0))
             dp = dot_nn(jnp.concatenate([values[:, cols], extra], axis=1), dot_[h, :, span])
-            e = jnp.exp2(s).astype(BF16)
+            e = jnp.exp2(s - top).astype(BF16)
             ds = (e.astype(F32) * dp).astype(BF16)
             dvs.append(dot_nn(e, dos[span, cols]))
-            dks.append(dot_nn(ds, qs[span, cols]) * LN2)
+            dks.append(dot_nn(ds, qs[span, cols]) * HD ** (-0.5))
             dqt[h, :, span] += dot_tn(keys[:, cols], ds)
         return jnp.concatenate(dks + dvs, axis=1)
 

time: 111 us -> 112 us (level)
  no operation moved by 1% of the time
where the time goes in v8:
time: 112 us; the launch traced here: 111 us
  Pallas kernels  111 us (99%)
    pallas_call x1, Pallas kernels, layer(): pl.pallas_call(functools.partial(body, Z, FK, R, D, NT), out_shape=(pltpu...  110 us

profile of v8, /device:TPU:0, one launch (start us, length us, event | category | flops | bytes accessed | tf_op | source)
XLA Modules:
  0.0 111.4 jit_solution(476365358571088146)
XLA Ops:
  0.7 109.5 %layer.1 = (bf16[256,512]{1,0:T(8,128)(2,1)S(1)}, bf16[256,512]{1,0:T(8,128)(2,1)S(1)}, f32[16,1536]{1,0:T(8,128)S(1)}, f32[16,512]{1,0:T(8,128)S(1)}, f32[16,20...) custom-call(bf16[256,512]{1,0:T(8,128)(2,1)} %bitcast.22, bf16[256,512]{1,0:T(8,128)(2,1)} %bitcast.23, ...), custom_call_target="tpu_custom_call" | custom-call | tf_op jit(solution)/shard_map/layer/pallas_call | solution.py:1080
  110.2 1.0 finish.1

commit v9 on v8

--- a/solution.py
+++ b/solution.py
@@ -588,6 +588,7 @@
         sent(tokb.at[:, oc], s_pc)
         sent(tokb.at[0 : Z - 1, c], s_pz)
         sent(dot_.at[:, grows, near_half], s_y.at[4])
+        sent(dot_.at[:, qrows, near_half], s_y.at[6])
         sent(gqs, s_y.at[5])
         got(gqr, r_y.at[5])
         t = p_sum(0) + acc[...] + gqr[...].astype(F32)
@@ -596,7 +597,7 @@
 
 
     qrows = slice(HD, HD + SLAB)
-    grows = slice(0, HD + SLAB)
+    grows = slice(0, HD)
     near_half, far_half = slice(0, R), slice(R, 2 * R)
 
     def far_out():
@@ -610,6 +611,7 @@
     def back_got():
         got(qt.at[:, qrows, far_half], r_y.at[3])
         got(dot_.at[:, grows, far_half], r_y.at[4])
+        got(dot_.at[:, qrows, far_half], r_y.at[6])
 
     events = {
         "tr": lambda: tok_right(z),
@@ -622,9 +624,9 @@
         "o_hi": far_out,
         "o_lo": lambda: push(ol, olr, s_y.at[2], r_y.at[2], d_y),
         "g_o": far_got,
-        "g_ol": lambda: got(olr, r_y.at[2]),
+        "g_ol": lambda: None,
         "qtail": lambda: push(qt.at[:, qrows, near_half], qt.at[:, qrows, far_half], s_y.at[3], r_y.at[3], d_y),
-        "dO": lambda: push(dot_.at[:, grows, near_half], dot_.at[:, grows, far_half], s_y.at[4], r_y.at[4], d_y),
+        "dO": lambda: push(dot_.at[:, qrows, near_half], dot_.at[:, qrows, far_half], s_y.at[6], r_y.at[6], d_y),
         "g_dO": back_got,
         "gq": queries_back,
         "r_c": r_c, "r_1": r_1, "r_2": r_2, "r_z": r_z, "r_zz": r_zz, "r_end": r_end,
@@ -856,14 +858,18 @@
         rows = slice(h * HD, (h + 1) * HD)
         w_head = w1[:, :, :, :, :, 0:D].reshape(D, D)[rows, :]
         ga = dot_nt(w_head, g_branch).astype(BF16).astype(F32)
-        low = (ga * ot[h, HD : HD + 1, 0:R]).astype(BF16)
+        dot_[h, 0:HD, 0:R] = (ga * ot[h, HD : HD + 1, 0:R]).astype(BF16)
+    push(dot_.at[:, grows, near_half], dot_.at[:, grows, far_half], s_y.at[4], r_y.at[4], d_y)
+    got(olr, r_y.at[2])
+    for h in range(H):
+        rows = slice(h * HD, (h + 1) * HD)
+        low = dot_[h, 0:HD, 0:R]
         exact = ot[h, 0:HD, 0:R] + olr[h].astype(F32) * ot[h, HD + 1 : HD + 2, 0:R]
         delta = col_sum(low.astype(F32) * exact)
         d1, d2, d3 = three_terms(delta)
         tail = jnp.where(
             row_tail == NT, -d1, jnp.where(row_tail == NT + 1, -d2, jnp.where(row_tail == NT + 2, -d3, 0.0))
         )
-        dot_[h, 0:HD, 0:R] = low
         dot_[h, HD : HD + SLAB, 0:R] = tail.astype(BF16)
         dos[0:R, rows] = low.T
 
@@ -1071,7 +1077,7 @@
         dma(5), dma(5, Z), dma(5), dma(5, Z), dma(5, others), dma(5, others), dma(5), dma(5),
         dma(3), dma(8), dma(8, others), dma(8, others), dma(8), dma(8),
         dma(max(len(DIRECT), 1), others), dma(max(len(DIRECT), 1), others), dma(8), dma(8, Z.bit_length() - 1),
-        one, dma(Z), one, dma(Z), dma(6), dma(6),
+        one, dma(Z), one, dma(Z), dma(7), dma(7),
         one, one, dma(others), dma(others), one, one, one, one,
     ]
     vmem = pl.BlockSpec(memory_space=pltpu.VMEM)

time: 112 us -> 111 us (level)
  no operation moved by 1% of the time
where the time goes in v9:
time: 111 us
  Pallas kernels  110 us (99%)
    pallas_call x1, Pallas kernels, layer(): pl.pallas_call(functools.partial(body, Z, FK, R, D, NT), out_shape=(pltpu...  109 us

profile of v9, /device:TPU:0, one launch (start us, length us, event | category | flops | bytes accessed | tf_op | source)
XLA Modules:
  0.0 111.0 jit_solution(11520034556634073817)
XLA Ops:
  0.7 109.2 %layer.1 = (bf16[256,512]{1,0:T(8,128)(2,1)S(1)}, bf16[256,512]{1,0:T(8,128)(2,1)S(1)}, f32[16,1536]{1,0:T(8,128)S(1)}, f32[16,512]{1,0:T(8,128)S(1)}, f32[16,20...) custom-call(bf16[256,512]{1,0:T(8,128)(2,1)} %bitcast.22, bf16[256,512]{1,0:T(8,128)(2,1)} %bitcast.23, ...), custom_call_target="tpu_custom_call" | custom-call | tf_op jit(solution)/shard_map/layer/pallas_call | solution.py:1086
  109.8 1.0 finish.1
